TPU v7x, 512 devices: a whole 4x8x8 slice. The times are simulated.
512 devices in a mesh: cuts: 64 (over x, z_lo, y), circ: 8 (over z_hi, core).
Axes of the slice: x: 4, y: 8, z: 8 (z_hi: 4, z_lo: 2; z = z_hi * 2 + z_lo), core: 2. Of those that a mesh axis runs over, the one named last changes fastest.
Arguments:
- sources: bfloat16 [64, 8, 8, 16, 1024], P('cuts', None, 'circ'), may hold values from -6 to 6
- block_inverse: bfloat16 [8, 1024, 1024], P('circ'), may hold values from -0.0115625 to 0.92
- memory_factor: float32 [64, 8, 1024], P('cuts', 'circ'), may hold values from 0.5 to 1
- coupling_target: int32 [8, 4], P('circ'), may hold values from 0 to 7, as said below
- coupling_weight: bfloat16 [8, 4, 128, 1024], P('circ'), may hold values from -0.09375 to 0.09375
- coarse_decay: float32 [64, 8, 1024], P('cuts', 'circ'), may hold values from 0.2 to 0.995
- initial_state: float32 [8, 16, 1024], P('circ'), may hold values from -6 to 6
Outputs:
- slice_starts: float32 [64, 8, 16, 1024], P('cuts', 'circ')
- waveform: bfloat16 [64, 8, 8, 16, 1024], P('cuts', None, 'circ')
Inputs may be any that keep to these rules, and one draw needn't show every extreme that they name: `coupling_target`: row j names 4 subcircuits, j itself among them possibly; a row may name one subcircuit twice.
All inputs are finite; a program needn't handle non-finite values.
Results may differ from a plain program's by a relative error of at most 0.007.
Values sent between devices are 32-bit elements; how exact they have to be, the bound alone decides.
No kernel may reach another device: no remote copies, remote signals or barrier semaphores. Data moves between devices by JAX's collectives and lax.ppermute only.
A program may use at most 64 MiB of HBM per device.

v0:
```python
import jax
import jax.numpy as jnp
from jax import lax
from jax.sharding import Mesh
from jax.sharding import PartitionSpec as P

SWEEPS = 3
ITERS = 2
CUTS = ("cuts_0", "cuts_1", "cuts_2")


def neutral_like(shard, identity):
    return jax.tree.map(
        lambda part, zero: jnp.zeros_like(part) + jnp.asarray(zero, part.dtype), shard, identity
    )


def gathered_once(shard, axis):
    leaves = jax.tree.leaves(shard)
    turns = sorted(range(len(leaves)), key=lambda k: -leaves[k].size)
    width = (1, *leaves[turns[0]].shape)[-1]
    lines = [
        jnp.pad(leaves[k].reshape(-1), (0, -leaves[k].size % width)).reshape(-1, width)
        for k in turns
    ]
    both, at, found = (lax.all_gather(jnp.concatenate(lines), axis), 0, {})
    for k, line in zip(turns, lines):
        section = both[:, at : at + len(line)].reshape(len(both), -1)
        found[k] = section[:, : leaves[k].size].reshape(-1, *leaves[k].shape)
        at += len(line)
    numbers = iter(range(len(leaves)))
    return jax.tree.map(lambda _: found[next(numbers)], shard)


def once_a_type(shard, axis):
    leaves, found = (jax.tree.leaves(shard), {})
    for initial, a in enumerate(leaves):
        if initial not in found:
            alike = [k for k, b in enumerate(leaves) if b.dtype == a.dtype]
            got = (
                gathered_once([leaves[k] for k in alike], axis)
                if len(alike) > 1
                else [lax.all_gather(a, axis)]
            )
            for k, b in zip(alike, got):
                found[k] = b
    numbers = iter(range(len(leaves)))
    return jax.tree.map(lambda _: found[next(numbers)], shard)


def carried_in(shard, axes, combine, identity):
    before = start = neutral_like(shard, identity)
    total = shard
    for axis in reversed(axes):
        peers, index = (lax.axis_size(axis), lax.axis_index(axis))
        pieces = once_a_type(total, axis)
        inside, total = (start, start)
        for k in range(peers):
            passed = k < index
            total = combine(total, jax.tree.map(lambda part: part[k], pieces))
            inside = jax.tree.map(lambda new, old: jnp.where(passed, new, old), total, inside)
        before = combine(inside, before)
    return before


def in_blocks(shard, dim, peers):
    before, after = (shard.shape[:dim], shard.shape[dim + 1 :])
    return jnp.moveaxis(shard.reshape(*before, peers, -1, *after), dim, 0)


def sum_at_owner(shard, axis, dim):
    peers = lax.axis_size(axis)
    blocks = lax.all_to_all(in_blocks(shard, dim, peers), axis, 0, 0, tiled=True)
    return jnp.sum(blocks, axis=0)


def run_chain(decay_rate, coarse_terms, initial):

    def compose(earlier, latter):
        return (earlier[0] * latter[0], latter[0] * earlier[1] + latter[1])

    identity = (jnp.ones_like(decay_rate), jnp.zeros_like(coarse_terms))
    total_decay, total_terms = carried_in((decay_rate, coarse_terms), CUTS, compose, identity)
    return total_decay * initial + total_terms


def shards(
    sources,
    block_inverse,
    memory_factor,
    coupling_target,
    coupling_weight,
    coarse_decay,
    initial_state,
):
    own_sources = sources[0]
    factor = memory_factor[0][:, None, :]
    decay_rate = coarse_decay[0][:, None, :]
    local_subs = block_inverse.shape[0]
    every_sub = local_subs * lax.axis_size("circ")
    port_count = coupling_weight.shape[2]
    steps_count = own_sources.shape[0]
    owners = (
        coupling_target[:, :, None] == jnp.arange(every_sub, dtype=jnp.int32)[None, None, :]
    ).astype(jnp.float32)
    coarse_load = jnp.mean(own_sources.astype(jnp.float32), axis=0)
    begin_state = run_chain(decay_rate, coarse_load, initial_state)
    wave_now = None
    for iteration in range(ITERS):
        wave_now = jnp.broadcast_to(begin_state, (steps_count,) + begin_state.shape)
        for sweep_index in range(SWEEPS):
            sweep_wave_low = wave_now.astype(jnp.bfloat16)
            inflow = sum_at_owner(
                jnp.einsum(
                    "skg,sktqp->gtqp",
                    owners,
                    jnp.einsum(
                        "skpn,tsqn->sktqp",
                        coupling_weight,
                        sweep_wave_low,
                        preferred_element_type=jnp.float32,
                    ),
                ),
                "circ",
                0,
            )
            previous = begin_state
            columns = []
            for step_index in range(steps_count):
                drive_term = factor * previous + own_sources[step_index].astype(jnp.float32)
                drive_term = drive_term.at[:, :, :port_count].add(inflow[:, step_index])
                previous = jnp.einsum(
                    "smn,sqn->sqm",
                    block_inverse,
                    drive_term.astype(jnp.bfloat16),
                    preferred_element_type=jnp.float32,
                )
                columns.append(previous)
            wave_now = jnp.stack(columns)
        correction = wave_now[-1] - decay_rate * begin_state
        begin_state = run_chain(decay_rate, correction, initial_state)
    return (begin_state[None], wave_now.astype(jnp.bfloat16)[None])


def solution(mesh):
    finer = Mesh(
        mesh.devices.reshape(4, 2, 8, mesh.shape["circ"]), ("cuts_0", "cuts_1", "cuts_2", "circ")
    )
    in_specs = (
        P(CUTS, None, "circ", None, None),
        P("circ", None, None),
        P(CUTS, "circ", None),
        P("circ", None),
        P("circ", None, None, None),
        P(CUTS, "circ", None),
        P("circ", None, None),
    )
    out_specs = (P(CUTS, "circ", None, None), P(CUTS, None, "circ", None, None))
    return jax.shard_map(
        shards, mesh=finer, in_specs=in_specs, out_specs=out_specs, check_vma=False
    )
```

profile of v0, /device:TPU:2, one launch (start us, length us, event | category | flops | bytes accessed | tf_op | source)
XLA Modules:
  0.0 455.4 jit_solution(6986316868407700193)
XLA Ops:
  2.5 27.9 %all-gather.9 = f32[8,17,1024]{2,1,0:T(8,128)S(1)} all-gather(f32[1,17,1024]{2,1,0:T(8,128)S(1)} %fusion.203), channel_id=2, replica_groups=mesh['cuts_0'=4,'cuts_1'=2,'cuts_2'=8,'circ'=8] {'cuts_2'}, dimensions={0}, use_global_device_ids=true | all-gather | bytes 626688 | tf_op jit(solution)/shard_map/all_gather | solution.py:26
  30.5 5.6 %all-gather.10 = f32[2,17,1024]{2,1,0:T(8,128)S(1)} all-gather(f32[1,17,1024]{2,1,0:T(8,128)S(1)} %maximum_bitcast_fusion), channel_id=3, replica_groups=mesh['cuts_0'=4,'cuts_1'=2,'cuts_2'=8,'circ'=8] {'cuts_1'}, dimensions={0}, use_global_device_ids=true | all-gather | bytes 208896 | tf_op jit(solution)/shard_map/all_gather | solution.py:26
  36.2 13.4 %all-gather.11 = f32[4,17,1024]{2,1,0:T(8,128)S(1)} all-gather(f32[1,17,1024]{2,1,0:T(8,128)S(1)} %maximum_bitcast_fusion.1), channel_id=4, replica_groups=mesh['cuts_0'=4,'cuts_1'=2,'cuts_2'=8,'circ'=8] {'cuts_0'}, dimensions={0}, use_global_device_ids=true | all-gather | bytes 348160 | tf_op jit(solution)/shard_map/all_gather | solution.py:26
  51.5 9.2 %all-to-all-start = ((f32[8,1,8,16,128]{4,3,2,1,0:T(8,128)}), f32[8,1,8,16,128]{4,3,2,1,0:T(8,128)}, u32[]{:S(2)}, u32[]{:S(2)}) async-start(f32[8,1,8,16,128]{4,3,2,1,0:T(8,128)} %copy.16), calls=%async_computation | async-start | bytes 1048576 | tf_op jit(solution)/shard_map/all_to_all | solution.py:73
  61.6 17.7 %all-to-all-done = f32[8,1,8,16,128]{4,3,2,1,0:T(8,128)} async-done(((f32[8,1,8,16,128]{4,3,2,1,0:T(8,128)}), f32[8,1,8,16,128]{4,3,2,1,0:T(8,128)}, u32[]{:S(2)}, u32[]{:S(2)}) %all-to-all-start) | async-done | bytes 524320 | tf_op jit(solution)/shard_map/all_to_all | solution.py:73
  83.7 1.5 constant_dynamic-update-slice_fusion.5
  87.9 1.5 constant_dynamic-update-slice_fusion.4
  96.3 1.5 constant_dynamic-update-slice_fusion.2
  100.5 1.5 constant_dynamic-update-slice_fusion.1
  111.3 20.8 %all_to_all.30 = f32[8,1,8,16,128]{4,3,2,1,0:T(8,128)} all-to-all(f32[8,1,8,16,128]{4,3,2,1,0:T(8,128)S(1)} %copy.18), channel_id=1, replica_groups=mesh['cuts_0'=4,'cuts_1'=2,'cuts_2'=8,'circ'=8] {'circ'}, dimensions={0} | all-to-all | bytes 1048576 | tf_op jit(solution)/shard_map/all_to_all | solution.py:73
  140.8 1.5 constant_dynamic-update-slice_fusion.11
  145.0 1.5 constant_dynamic-update-slice_fusion.10
  153.4 1.5 constant_dynamic-update-slice_fusion.8
  157.6 1.5 constant_dynamic-update-slice_fusion.7
  164.2 21.4 %all_to_all.31 = f32[8,1,8,16,128]{4,3,2,1,0:T(8,128)} all-to-all(f32[8,1,8,16,128]{4,3,2,1,0:T(8,128)S(1)} %copy.20), channel_id=1, replica_groups=mesh['cuts_0'=4,'cuts_1'=2,'cuts_2'=8,'circ'=8] {'circ'}, dimensions={0} | all-to-all | bytes 1048576 | tf_op jit(solution)/shard_map/all_to_all | solution.py:73
  187.3 1.5 fusion.99
  190.8 1.5 fusion.105
  194.2 1.5 fusion.111
  197.6 1.5 fusion.117
  201.1 1.5 fusion.123
  204.5 1.5 fusion.129
  207.9 1.5 fusion.135
  211.4 1.5 fusion.144
  212.9 26.1 %all-gather.12 = f32[8,17,1024]{2,1,0:T(8,128)S(1)} all-gather(f32[1,17,1024]{2,1,0:T(8,128)S(1)} %fusion.204), channel_id=5, replica_groups=mesh['cuts_0'=4,'cuts_1'=2,'cuts_2'=8,'circ'=8] {'cuts_2'}, dimensions={0}, use_global_device_ids=true | all-gather | bytes 626688 | tf_op jit(solution)/shard_map/all_gather | solution.py:26
  239.1 5.3 %all-gather.13 = f32[2,17,1024]{2,1,0:T(8,128)S(1)} all-gather(f32[1,17,1024]{2,1,0:T(8,128)S(1)} %maximum_bitcast_fusion.2), channel_id=6, replica_groups=mesh['cuts_0'=4,'cuts_1'=2,'cuts_2'=8,'circ'=8] {'cuts_1'}, dimensions={0}, use_global_device_ids=true | all-gather | bytes 208896 | tf_op jit(solution)/shard_map/all_gather | solution.py:26
  244.4 12.5 %all-gather.14 = f32[4,17,1024]{2,1,0:T(8,128)S(1)} all-gather(f32[1,17,1024]{2,1,0:T(8,128)S(1)} %maximum_bitcast_fusion.3), channel_id=7, replica_groups=mesh['cuts_0'=4,'cuts_1'=2,'cuts_2'=8,'circ'=8] {'cuts_0'}, dimensions={0}, use_global_device_ids=true | all-gather | bytes 348160 | tf_op jit(solution)/shard_map/all_gather | solution.py:26
  258.9 4.1 all-to-all-start.3
  263.8 16.2 %all-to-all-done.3 = f32[8,1,8,16,128]{4,3,2,1,0:T(8,128)} async-done(((f32[8,1,8,16,128]{4,3,2,1,0:T(8,128)}), f32[8,1,8,16,128]{4,3,2,1,0:T(8,128)}, u32[]{:S(2)}, u32[]{:S(2)}) %all-to-all-start.3) | async-done | bytes 524320 | tf_op jit(solution)/shard_map/all_to_all | solution.py:73
  284.5 1.5 constant_dynamic-update-slice_fusion.19
  288.7 1.5 constant_dynamic-update-slice_fusion.18
  301.3 1.5 constant_dynamic-update-slice_fusion.15
  312.1 18.1 %all_to_all.32 = f32[8,1,8,16,128]{4,3,2,1,0:T(8,128)} all-to-all(f32[8,1,8,16,128]{4,3,2,1,0:T(8,128)S(1)} %copy.24), channel_id=1, replica_groups=mesh['cuts_0'=4,'cuts_1'=2,'cuts_2'=8,'circ'=8] {'circ'}, dimensions={0} | all-to-all | bytes 1048576 | tf_op jit(solution)/shard_map/all_to_all | solution.py:73
  338.9 1.5 constant_dynamic-update-slice_fusion.25
  343.1 1.5 constant_dynamic-update-slice_fusion.24
  351.5 1.5 constant_dynamic-update-slice_fusion.22
  355.7 1.5 constant_dynamic-update-slice_fusion.21
  362.3 19.9 %all_to_all.33 = f32[8,1,8,16,128]{4,3,2,1,0:T(8,128)S(1)} all-to-all(f32[8,1,8,16,128]{4,3,2,1,0:T(8,128)S(1)} %copy.26), channel_id=1, replica_groups=mesh['cuts_0'=4,'cuts_1'=2,'cuts_2'=8,'circ'=8] {'circ'}, dimensions={0} | all-to-all | bytes 1048576 | tf_op jit(solution)/shard_map/all_to_all | solution.py:73
  382.9 1.5 convert_add_fusion.30
  386.4 1.5 convert_add_fusion.25
  389.8 1.5 convert_add_fusion.20
  393.2 1.5 convert_add_fusion.15
  396.7 1.5 convert_add_fusion.10
  400.1 1.5 convert_add_fusion.5
  403.5 1.5 convert_add_fusion
  407.0 1.5 constant_dynamic-update-slice_fusion.28
  408.6 26.3 %all-gather.15 = f32[8,17,1024]{2,1,0:T(8,128)S(1)} all-gather(f32[1,17,1024]{2,1,0:T(8,128)S(1)} %fusion.205), channel_id=8, replica_groups=mesh['cuts_0'=4,'cuts_1'=2,'cuts_2'=8,'circ'=8] {'cuts_2'}, dimensions={0}, use_global_device_ids=true | all-gather | bytes 626688 | tf_op jit(solution)/shard_map/all_gather | solution.py:26
  435.0 6.9 %all-gather.16 = f32[2,17,1024]{2,1,0:T(8,128)S(1)} all-gather(f32[1,17,1024]{2,1,0:T(8,128)S(1)} %maximum_bitcast_fusion.4), channel_id=9, replica_groups=mesh['cuts_0'=4,'cuts_1'=2,'cuts_2'=8,'circ'=8] {'cuts_1'}, dimensions={0}, use_global_device_ids=true | all-gather | bytes 208896 | tf_op jit(solution)/shard_map/all_gather | solution.py:26
  442.0 12.5 %all-gather.17 = f32[4,17,1024]{2,1,0:T(8,128)S(1)} all-gather(f32[1,17,1024]{2,1,0:T(8,128)S(1)} %maximum_bitcast_fusion.5), channel_id=10, replica_groups=mesh['cuts_0'=4,'cuts_1'=2,'cuts_2'=8,'circ'=8] {'cuts_0'}, dimensions={0}, use_global_device_ids=true | all-gather | bytes 348160 | tf_op jit(solution)/shard_map/all_gather | solution.py:26
  (235 shorter events, 144.1 us)
Async XLA Ops:
  0.6 79.7 %copy-start = (bf16[1,1024,1024]{2,1,0:T(8,128)(2,1)S(1)}, bf16[1,1024,1024]{2,1,0:T(8,128)(2,1)}, u32[]{:S(2)}) copy-start(bf16[1,1024,1024]{2,1,0:T(8,128)(2,1)} %param.104) | copy-start | bytes 6291460
  0.6 49.0 %copy-start.3 = (f32[1,16,1024]{2,1,0:T(8,128)S(1)}, f32[1,16,1024]{2,1,0:T(8,128)}, u32[]{:S(2)}) copy-start(f32[1,16,1024]{2,1,0:T(8,128)} %param.109) | copy-start | bytes 196612
  2.5 47.3 %copy-start.1 = (bf16[1,4,128,1024]{3,2,1,0:T(8,128)(2,1)S(1)}, bf16[1,4,128,1024]{3,2,1,0:T(8,128)(2,1)}, u32[]{:S(2)}) copy-start(bf16[1,4,128,1024]{3,2,1,0:T(8,128)(2,1)} %param.107) | copy-start | bytes 3145732
  30.5 19.8 %copy-start.13 = (s32[1,4]{1,0:T(1,128)S(1)}, s32[1,4]{1,0:T(1,128)}, u32[]{:S(2)}) copy-start(s32[1,4]{1,0:T(1,128)} %param.106) | copy-start | bytes 52
  49.8 11.0 %copy-start.2 = (f32[1,1,1024]{2,1,0:T(1,128)S(1)}, f32[1,1,1024]{2,1,0:T(1,128)}, u32[]{:S(2)}) copy-start(f32[1,1,1024]{2,1,0:T(1,128)} %param.105) | copy-start | bytes 12292
  51.5 27.7 %all-to-all-start = ((f32[8,1,8,16,128]{4,3,2,1,0:T(8,128)}), f32[8,1,8,16,128]{4,3,2,1,0:T(8,128)}, u32[]{:S(2)}, u32[]{:S(2)}) async-start(f32[8,1,8,16,128]{4,3,2,1,0:T(8,128)} %copy.16), calls=%async_computation | async-start | bytes 1048576 | tf_op jit(solution)/shard_map/all_to_all | solution.py:73
  80.3 2.1 copy-start.6
  133.2 2.1 copy-start.7
  186.7 2.8 copy-start.11
  186.7 0.6 copy-start.5
  204.5 6.9 %copy-start.12 = (f32[1,1,1024]{2,1,0:T(1,128)S(1)}, f32[1,1,1024]{2,1,0:T(1,128)}, u32[]{:S(2)}) copy-start(f32[1,1,1024]{2,1,0:T(1,128)} %param.108) | copy-start | bytes 12292
  258.9 21.1 %all-to-all-start.3 = ((f32[8,1,8,16,128]{4,3,2,1,0:T(8,128)}), f32[8,1,8,16,128]{4,3,2,1,0:T(8,128)}, u32[]{:S(2)}, u32[]{:S(2)}) async-start(f32[8,1,8,16,128]{4,3,2,1,0:T(8,128)} %copy.22), calls=%async_computation.3 | async-start | bytes 1048576 | tf_op jit(solution)/shard_map/all_to_all | solution.py:73
  281.1 2.1 copy-start.8
  331.3 2.1 copy-start.9
  382.3 2.8 copy-start.10
  382.3 0.6 copy-start.4
  408.5 46.9 %copy-start.14 = (bf16[1,8,1,16,1024]{4,3,2,1,0:T(8,128)(2,1)}, bf16[1,8,1,16,1024]{4,3,2,1,0:T(8,128)(2,1)S(1)}, u32[]{:S(2)}) copy-start(bf16[1,8,1,16,1024]{4,3,2,1,0:T(8,128)(2,1)S(1)} %get-tuple-element.715) | copy-start | bytes 786436
where the time goes:
time: 462 us; the launch traced here: 455 us
  blocking collectives  217 us (47%)
  other arithmetic  87 us (19%)
  matrix products  72.8 us (16%)
  waiting for transfers between devices  33.9 us (7%)
  local copies, waits for them, and re-layouts  30.4 us (7%)
  starting transfers between devices  13.3 us (3%)
    all_gather x9, blocking collectives, gathered_once(): both, at, found = (lax.all_gather(jnp.concatenate(lines), axis), 0, {})  137 us
    all_to_all x4, blocking collectives, sum_at_owner(): lax.all_to_all(in_blocks(shard, dim, peers), axis, 0, 0, tiled=True)  80.2 us
    dot_general x48, matrix products, shards(): jnp.einsum('smn,sqn->sqm', block_inverse, drive_term.astype(jnp.bfloat16)...  67.9 us
    scatter-add x48, other arithmetic, shards(): drive_term = drive_term.at[:, :, :port_count].add(inflow[:, step_index])  54.5 us
    all_to_all x2, waiting for transfers between devices, sum_at_owner(): lax.all_to_all(in_blocks(shard, dim, peers), axis, 0, 0, tiled=True)  33.9 us
    unnamed x83, local copies, waits for them, and re-layouts  28.1 us
    add x30, other arithmetic, shards(): drive_term = factor * previous + own_sources[step_index].astype(jnp.float32)  23.5 us
    all_to_all x2, starting transfers between devices, sum_at_owner(): lax.all_to_all(in_blocks(shard, dim, peers), axis, 0, 0, tiled=True)  13.3 us
  transfers between devices with their start and end apart: 2, of which 2 were waited for; matrix products, arithmetic and copies ran while one was open for 0% of the time, Pallas kernels for 0%

commit v1 on v0

v1 whole, which is shorter than its diff:
```python
import jax
import jax.numpy as jnp
from jax import lax
from jax.experimental import pallas as pl
from jax.experimental.pallas import tpu as pltpu
from jax.sharding import Mesh
from jax.sharding import PartitionSpec as P

ITERS = 2
STEPS = 8
SCEN = 16
PORTS = 128
KC = 4
SUBS = 8
LANES = 128
CUTS = ("cuts_0", "cuts_1", "cuts_2")
CIRC = ("circ_0", "circ_1")
F32 = jnp.float32
BF16 = jnp.bfloat16
VMEM = pl.BlockSpec(memory_space=pltpu.VMEM)
SMEM = pl.BlockSpec(memory_space=pltpu.SMEM)


def shape(dims, dtype=F32):
    return jax.ShapeDtypeStruct(dims, dtype)


def call(body, outs, args, name, flops=0, scratch=()):
    specs = [SMEM if a.dtype == jnp.int32 else VMEM for a in args]
    size = sum(a.size * a.dtype.itemsize for a in (*args, *outs))
    return pl.pallas_call(
        body,
        out_shape=outs,
        in_specs=specs,
        out_specs=[VMEM] * len(outs),
        scratch_shapes=list(scratch),
        compiler_params=pltpu.CompilerParams(vmem_limit_bytes=32 << 20),
        cost_estimate=pl.CostEstimate(flops=flops, bytes_accessed=size, transcendentals=0),
        name=name,
    )(*args)


def dot(a, b):
    return jnp.dot(a, b, preferred_element_type=F32)


def pack(state, out_ref):
    for b in range(64):
        block, pair = divmod(b, 8)
        out_ref[b, 0:2, :] = state[2 * pair : 2 * pair + 2, block * LANES : (block + 1) * LANES]


def load_body(sources_ref, decay_ref, out_ref):
    total = sources_ref[0].astype(F32)
    for t in range(1, STEPS):
        total = total + sources_ref[t].astype(F32)
    pack(total * (1.0 / STEPS), out_ref)
    for b in range(64):
        block = b // 8
        row = decay_ref[:, block * LANES : (block + 1) * LANES]
        out_ref[b, 2:4, :] = jnp.concatenate([row, row], axis=0)


def setup_body(b_ref, c_ref, m_ref, bt_ref, ct_ref, h_ref, ch_ref):
    bt_ref[...] = b_ref[...].T
    ct_ref[...] = c_ref[...].T
    response = bt_ref[0:PORTS, :]
    h_ref[0:PORTS, :] = response
    response = response.astype(F32)
    for k in range(1, STEPS):
        response = dot((m_ref[...] * response).astype(BF16), bt_ref[...])
        h_ref[k * PORTS : (k + 1) * PORTS, :] = response.astype(BF16)
    ch_ref[...] = dot(h_ref[...], ct_ref[...]).astype(BF16)


def first_chain_body(mine_ref, terms_ref, initial_ref, start_ref):
    start = initial_ref[mine_ref[0]]
    for n in range(64):
        start_ref[n] = start
        start = terms_ref[n, 2:4, :] * start + terms_ref[n, 0:2, :]


def chain_body(mine_ref, last_ref, terms_ref, old_ref, initial_ref, start_ref):
    start = initial_ref[mine_ref[0]]
    for n in range(64):
        start_ref[n] = start
        decay = terms_ref[n, 2:4, :]
        start = decay * start + (last_ref[n] - decay * old_ref[n])


def group(target_ref, blocks, out_ref):
    for g in range(SUBS):
        total = None
        for k in range(KC):
            feeds = jnp.where(target_ref[k] == g, F32(1.0), F32(0.0))
            term = feeds * blocks[:, k * PORTS : (k + 1) * PORTS]
            total = term if total is None else total + term
        out_ref[g] = total


def start_body(target_ref, pieces_ref, ct_ref, start_ref, out_ref):
    for b in range(64):
        block, pair = divmod(b, 8)
        start_ref[2 * pair : 2 * pair + 2, block * LANES : (block + 1) * LANES] = pieces_ref[b]
    group(target_ref, dot(start_ref[...].astype(BF16), ct_ref[...]), out_ref)


def free_body(start_ref, sources_ref, m_ref, bt_ref, ct_ref, z_ref, cz_ref, low_ref):
    previous = start_ref[...]
    for t in range(STEPS):
        drive = m_ref[...] * previous + sources_ref[t].astype(F32)
        previous = dot(drive.astype(BF16), bt_ref[...])
        z_ref[t * SCEN : (t + 1) * SCEN, :] = previous
        low_ref[t * SCEN : (t + 1) * SCEN, :] = previous.astype(BF16)
    cz_ref[...] = dot(low_ref[...], ct_ref[...])


def delays(inflow, x_ref):
    for k in range(STEPS):
        columns = slice(k * PORTS, (k + 1) * PORTS)
        if k:
            x_ref[0 : k * SCEN, columns] = jnp.zeros((k * SCEN, PORTS), BF16)
        x_ref[k * SCEN :, columns] = inflow[: (STEPS - k) * SCEN]


def couple_first_body(target_ref, f_ref, cz_ref, ch_ref, out_ref, x_ref):
    inflow = jnp.sum(f_ref[...], axis=0).astype(BF16)
    delays(jnp.concatenate([inflow] * STEPS, axis=0), x_ref)
    group(target_ref, cz_ref[...] + dot(x_ref[...], ch_ref[...]), out_ref)


def couple_body(target_ref, f_ref, cz_ref, ch_ref, out_ref, x_ref):
    delays(jnp.sum(f_ref[...], axis=0).astype(BF16), x_ref)
    group(target_ref, cz_ref[...] + dot(x_ref[...], ch_ref[...]), out_ref)


def last_step_body(f_ref, z_ref, h_ref, out_ref, x_ref):
    inflow = jnp.sum(f_ref[...], axis=0).astype(BF16)
    for k in range(STEPS):
        t = STEPS - 1 - k
        x_ref[:, k * PORTS : (k + 1) * PORTS] = inflow[t * SCEN : (t + 1) * SCEN]
    pack(z_ref[(STEPS - 1) * SCEN :, :] + dot(x_ref[...], h_ref[...]), out_ref)


def wave_body(f_ref, z_ref, h_ref, out_ref, wave_ref, x_ref):
    delays(jnp.sum(f_ref[...], axis=0).astype(BF16), x_ref)
    wave = z_ref[...] + dot(x_ref[...], h_ref[...])
    wave_ref[...] = wave.astype(BF16)
    pack(wave[(STEPS - 1) * SCEN :, :], out_ref)


def over_cuts(pieces):
    return lax.all_to_all(pieces, CUTS, 0, 0, tiled=True)


def over_circ(blocks):
    return lax.all_to_all(blocks, CIRC, 0, 0, tiled=True)


def shards(
    sources,
    block_inverse,
    memory_factor,
    coupling_target,
    coupling_weight,
    coarse_decay,
    initial_state,
):
    nodes = block_inverse.shape[-1]
    rows = STEPS * SCEN
    src = sources.reshape(STEPS, SCEN, nodes)
    inverse = block_inverse.reshape(nodes, nodes)
    weight = coupling_weight.reshape(KC * PORTS, nodes)
    factor = memory_factor.reshape(1, nodes)
    decay = coarse_decay.reshape(1, nodes)
    target = coupling_target.reshape(KC)
    mine = lax.axis_index(CUTS).reshape(1).astype(jnp.int32)
    initial = initial_state.reshape(SCEN, 8, LANES).transpose(1, 0, 2).reshape(64, 2, LANES)

    (loads,) = call(load_body, [shape((64, 4, LANES))], (src, decay), "load")
    terms = over_cuts(loads)
    bt, ct, h, ch = call(
        setup_body,
        [
            shape((nodes, nodes), BF16),
            shape((nodes, KC * PORTS), BF16),
            shape((STEPS * PORTS, nodes), BF16),
            shape((STEPS * PORTS, KC * PORTS), BF16),
        ],
        (inverse, weight, factor),
        "setup",
        flops=2 * nodes * nodes * (7 * PORTS + KC * PORTS),
    )
    (starts,) = call(first_chain_body, [shape((64, 2, LANES))], (mine, terms, initial), "chain")
    wave = None
    for iteration in range(ITERS):
        pieces = over_cuts(starts)
        start, sent = call(
            start_body,
            [shape((SCEN, nodes)), shape((SUBS, SCEN, PORTS))],
            (target, pieces, ct),
            "start",
            flops=2 * SCEN * nodes * KC * PORTS,
        )
        inflow = over_circ(sent)
        z, cz = call(
            free_body,
            [shape((rows, nodes)), shape((rows, KC * PORTS))],
            (start, src, factor, bt, ct),
            "free",
            flops=2 * rows * nodes * (nodes + KC * PORTS),
            scratch=[pltpu.VMEM((rows, nodes), BF16)],
        )
        delayed = [pltpu.VMEM((rows, STEPS * PORTS), BF16)]
        for body in (couple_first_body, couple_body):
            (sent,) = call(
                body,
                [shape((SUBS, rows, PORTS))],
                (target, inflow, cz, ch),
                "couple",
                flops=2 * rows * nodes * KC * PORTS,
                scratch=delayed,
            )
            inflow = over_circ(sent)
        if iteration < ITERS - 1:
            (last,) = call(
                last_step_body,
                [shape((64, 2, LANES))],
                (inflow, z, h),
                "last",
                flops=2 * SCEN * nodes * nodes,
                scratch=[pltpu.VMEM((SCEN, STEPS * PORTS), BF16)],
            )
        else:
            last, wave = call(
                wave_body,
                [shape((64, 2, LANES)), shape((rows, nodes), BF16)],
                (inflow, z, h),
                "wave",
                flops=2 * rows * nodes * nodes,
                scratch=delayed,
            )
        (starts,) = call(
            chain_body,
            [shape((64, 2, LANES))],
            (mine, over_cuts(last), terms, starts, initial),
            "chain",
        )
    pieces = over_cuts(starts)
    start = pieces.reshape(8, SCEN, LANES).transpose(1, 0, 2).reshape(1, 1, SCEN, nodes)
    return start, wave.reshape(1, STEPS, 1, SCEN, nodes)


def solution(mesh):
    finer = Mesh(mesh.devices.reshape(4, 2, 8, 4, 2), CUTS + CIRC)
    in_specs = (
        P(CUTS, None, CIRC, None, None),
        P(CIRC, None, None),
        P(CUTS, CIRC, None),
        P(CIRC, None),
        P(CIRC, None, None, None),
        P(CUTS, CIRC, None),
        P(CIRC, None, None),
    )
    out_specs = (P(CUTS, CIRC, None, None), P(CUTS, None, CIRC, None, None))
    return jax.shard_map(
        shards, mesh=finer, in_specs=in_specs, out_specs=out_specs, check_vma=False
    )
```

time: 462 us -> 229 us (0.50)
  the two profiles are of different devices: /device:TPU:2 before, /device:TPU:8 now
where the time goes in v1:
time: 229 us; the launch traced here: 228 us
  blocking collectives  147 us (64%)
  starting transfers between devices  30.6 us (13%)
  Pallas kernels  19.9 us (9%)
  waiting for transfers between devices  17.7 us (8%)
  local copies, waits for them, and re-layouts  12.5 us (5%)
    all_to_all x4, blocking collectives, over_circ(): return lax.all_to_all(blocks, CIRC, 0, 0, tiled=True)  82.2 us
    all_to_all x4, blocking collectives, over_cuts(): return lax.all_to_all(pieces, CUTS, 0, 0, tiled=True)  64.6 us
    pallas_call x15, Pallas kernels, call(): pl.pallas_call(body, out_shape=outs, in_specs=specs, out_specs=[VMEM] * l...  19.9 us
    all_to_all x2, starting transfers between devices, over_cuts(): return lax.all_to_all(pieces, CUTS, 0, 0, tiled=True)  17.6 us
    all_to_all x2, starting transfers between devices, over_circ(): return lax.all_to_all(blocks, CIRC, 0, 0, tiled=True)  12.9 us
    unnamed x29, local copies, waits for them, and re-layouts  11.8 us
    all_to_all x2, waiting for transfers between devices, over_cuts(): return lax.all_to_all(pieces, CUTS, 0, 0, tiled=True)  9.51 us
    all_to_all x2, waiting for transfers between devices, over_circ(): return lax.all_to_all(blocks, CIRC, 0, 0, tiled=True)  8.2 us
  transfers between devices with their start and end apart: 4, of which 3 were waited for; matrix products, arithmetic and copies ran while one was open for 0% of the time, Pallas kernels for 4%

profile of v1, /device:TPU:8, one launch (start us, length us, event | category | flops | bytes accessed | tf_op | source)
XLA Modules:
  0.0 228.3 jit_solution(4742348511313878144)
XLA Ops:
  0.6 0.0 copy-start.6
  0.6 0.9 copy-done.6
  1.6 0.7 copy-done.11
  2.3 0.7 load.1
  3.0 12.4 %all-to-all-start = ((f32[64,4,128]{2,1,0:T(4,128)}), f32[64,4,128]{2,1,0:T(4,128)S(1)}, u32[]{:S(2)}, u32[]{:S(2)}) async-start(f32[64,4,128]{2,1,0:T(4,128)} %load.1), calls=%async_computation | async-start | bytes 262144 | tf_op jit(solution)/shard_map/all_to_all | solution.py:153
  15.4 0.9 copy.12
  16.3 9.5 %all-to-all-done.terms_ref = f32[64,4,128]{2,1,0:T(4,128)S(1)} async-done(((f32[64,4,128]{2,1,0:T(4,128)}), f32[64,4,128]{2,1,0:T(4,128)S(1)}, u32[]{:S(2)}, u32[]{:S(2)}) %all-to-all-start) | async-done | bytes 131104 | tf_op jit(solution)/shard_map/all_to_all | solution.py:153
  25.8 0.8 chain.3.old_ref
  26.5 5.3 %all-to-all-start.1 = ((f32[64,2,128]{2,1,0:T(2,128)}), f32[64,2,128]{2,1,0:T(2,128)S(1)}, u32[]{:S(2)}, u32[]{:S(2)}) async-start(f32[64,2,128]{2,1,0:T(2,128)} %chain.3.old_ref), calls=%async_computation.1 | async-start | bytes 131072 | tf_op jit(solution)/shard_map/all_to_all | solution.py:153
  31.8 0.0 copy-start.9
  31.8 0.7 copy-done.9
  32.5 1.6 copy-done.12
  34.1 1.2 copy-done.13
  35.3 3.8 %setup.1 = (bf16[1024,1024]{1,0:T(8,128)(2,1)S(1)}, bf16[1024,512]{1,0:T(8,128)(2,1)S(1)}, bf16[1024,1024]{1,0:T(8,128)(2,1)S(1)}, bf16[1024,512]{1,0:T(8,128)(2,1)S(1)}) custom-call(bf16[1024,1024]{1,0:T(8,128)(2,1)S(1)} %bitcast.35, bf16[512,1024]{1,0:T(8,128)(2,1)S(1)} %bitcast.36, f32[1,1024]{1,0:T(1,128)S(1)} %bitcast.31), custom_call_target="tpu_custom_call" | custom-call | flops 2952790016 | bytes 9441280 | tf_op jit(solution)/shard_map/setup/pallas_call | solution.py:31
  39.1 1.3 copy-done
  40.4 1.3 copy-done.3
  41.7 0.0 all-to-all-done.1.pieces_ref
  41.7 1.4 start.2
  43.2 9.4 %all-to-all-start.2 = ((f32[8,16,128]{2,1,0:T(8,128)}), f32[8,16,128]{2,1,0:T(8,128)S(1)}, u32[]{:S(2)}, u32[]{:S(2)}) async-start(f32[8,16,128]{2,1,0:T(8,128)} %get-tuple-element.17), calls=%async_computation.2 | async-start | bytes 131072 | tf_op jit(solution)/shard_map/all_to_all | solution.py:157
  52.6 0.0 copy-done.10
  52.6 0.0 copy-start.4
  52.6 1.6 copy-done.4
  54.2 2.6 %free.2 = (f32[128,1024]{1,0:T(8,128)S(1)}, f32[128,512]{1,0:T(8,128)S(1)}) custom-call(f32[16,1024]{1,0:T(8,128)S(1)} %get-tuple-element.18.start_ref, bf16[8,16,1024]{2,1,0:T(8,128)(2,1)S(1)} %bitcast.20, f32[1,1024]{1,0:T(1,128)S(1)} %bitcast.32, bf16[1024,1024]{1,0:T(8,128)(2,1)S(1)} %copy-done.4, bf16[1024,512]{1,0:T(8,128)(2,1)S(1)} %get-tuple-element.16.ct_ref), custom_call_target="tpu_custom_call" | custom-call | flops 402653184 | bytes 4263936 | tf_op jit(solution)/shard_map/free/pallas_call | solution.py:31
  56.8 4.4 %all-to-all-done.2.f_ref = f32[8,16,128]{2,1,0:T(8,128)S(1)} async-done(((f32[8,16,128]{2,1,0:T(8,128)}), f32[8,16,128]{2,1,0:T(8,128)S(1)}, u32[]{:S(2)}, u32[]{:S(2)}) %all-to-all-start.2) | async-done | bytes 65568 | tf_op jit(solution)/shard_map/all_to_all | solution.py:157
  61.2 1.0 couple.4
  62.2 0.0 copy-start.1
  62.2 21.2 %all_to_all.60.f_ref = f32[8,128,128]{2,1,0:T(8,128)S(1)} all-to-all(f32[8,128,128]{2,1,0:T(8,128)S(1)} %couple.4), channel_id=1, replica_groups=mesh['cuts_0'=4,'cuts_1'=2,'cuts_2'=8,'circ_0'=4,'circ_1'=2] {'circ_0','..., dimensions={0} | all-to-all | bytes 1048576 | tf_op jit(solution)/shard_map/all_to_all | solution.py:157
  83.3 1.0 couple.5
  84.3 20.1 %all_to_all.61.f_ref = f32[8,128,128]{2,1,0:T(8,128)S(1)} all-to-all(f32[8,128,128]{2,1,0:T(8,128)S(1)} %couple.5), channel_id=1, replica_groups=mesh['cuts_0'=4,'cuts_1'=2,'cuts_2'=8,'circ_0'=4,'circ_1'=2] {'circ_0','..., dimensions={0} | all-to-all | bytes 1048576 | tf_op jit(solution)/shard_map/all_to_all | solution.py:157
  104.5 0.4 last.1
  104.8 20.7 %all_to_all.62.last_ref = f32[64,2,128]{2,1,0:T(2,128)S(1)} all-to-all(f32[64,2,128]{2,1,0:T(2,128)S(1)} %last.1), channel_id=1, replica_groups=mesh['cuts_0'=4,'cuts_1'=2,'cuts_2'=8,'circ_0'=4,'circ_1'=2] {'cuts_0','..., dimensions={0} | all-to-all | bytes 131072 | tf_op jit(solution)/shard_map/all_to_all | solution.py:153
  125.6 1.0 chain.4.old_ref
  126.5 14.5 %all_to_all.63.pieces_ref = f32[64,2,128]{2,1,0:T(2,128)S(1)} all-to-all(f32[64,2,128]{2,1,0:T(2,128)S(1)} %chain.4.old_ref), channel_id=1, replica_groups=mesh['cuts_0'=4,'cuts_1'=2,'cuts_2'=8,'circ_0'=4,'circ_1'=2] {'cuts_0','..., dimensions={0} | all-to-all | bytes 131072 | tf_op jit(solution)/shard_map/all_to_all | solution.py:153
  141.0 1.4 start.3
  142.4 3.5 %all-to-all-start.7 = ((f32[8,16,128]{2,1,0:T(8,128)}), f32[8,16,128]{2,1,0:T(8,128)S(1)}, u32[]{:S(2)}, u32[]{:S(2)}) async-start(f32[8,16,128]{2,1,0:T(8,128)} %get-tuple-element.24), calls=%async_computation.7 | async-start | bytes 131072 | tf_op jit(solution)/shard_map/all_to_all | solution.py:157
  146.0 0.0 copy-start.5
  146.0 1.6 copy-done.5
  147.6 2.6 %free.3 = (f32[128,1024]{1,0:T(8,128)S(1)}, f32[128,512]{1,0:T(8,128)S(1)}) custom-call(f32[16,1024]{1,0:T(8,128)S(1)} %get-tuple-element.25.start_ref, bf16[8,16,1024]{2,1,0:T(8,128)(2,1)S(1)} %bitcast.21, f32[1,1024]{1,0:T(1,128)S(1)} %bitcast.33, bf16[1024,1024]{1,0:T(8,128)(2,1)S(1)} %copy-done.5, bf16[1024,512]{1,0:T(8,128)(2,1)S(1)} %get-tuple-element.16.ct_ref), custom_call_target="tpu_custom_call" | custom-call | flops 402653184 | bytes 4263936 | tf_op jit(solution)/shard_map/free/pallas_call | solution.py:31
  150.2 3.8 %all-to-all-done.7.f_ref = f32[8,16,128]{2,1,0:T(8,128)S(1)} async-done(((f32[8,16,128]{2,1,0:T(8,128)}), f32[8,16,128]{2,1,0:T(8,128)S(1)}, u32[]{:S(2)}, u32[]{:S(2)}) %all-to-all-start.7) | async-done | bytes 65568 | tf_op jit(solution)/shard_map/all_to_all | solution.py:157
  154.0 1.0 couple.6
  155.0 20.9 %all_to_all.64.f_ref = f32[8,128,128]{2,1,0:T(8,128)S(1)} all-to-all(f32[8,128,128]{2,1,0:T(8,128)S(1)} %couple.6), channel_id=1, replica_groups=mesh['cuts_0'=4,'cuts_1'=2,'cuts_2'=8,'circ_0'=4,'circ_1'=2] {'circ_0','..., dimensions={0} | all-to-all | bytes 1048576 | tf_op jit(solution)/shard_map/all_to_all | solution.py:157
  175.8 1.0 couple.7
  176.8 20.1 %all_to_all.65.f_ref = f32[8,128,128]{2,1,0:T(8,128)S(1)} all-to-all(f32[8,128,128]{2,1,0:T(8,128)S(1)} %couple.7), channel_id=1, replica_groups=mesh['cuts_0'=4,'cuts_1'=2,'cuts_2'=8,'circ_0'=4,'circ_1'=2] {'circ_0','..., dimensions={0} | all-to-all | bytes 1048576 | tf_op jit(solution)/shard_map/all_to_all | solution.py:157
  196.9 1.2 wave.1
  198.0 15.0 %all_to_all.66.last_ref = f32[64,2,128]{2,1,0:T(2,128)S(1)} all-to-all(f32[64,2,128]{2,1,0:T(2,128)S(1)} %get-tuple-element.28), channel_id=1, replica_groups=mesh['cuts_0'=4,'cuts_1'=2,'cuts_2'=8,'circ_0'=4,'circ_1'=2] {'cuts_0','..., dimensions={0} | all-to-all | bytes 131072 | tf_op jit(solution)/shard_map/all_to_all | solution.py:153
  213.1 0.1 chain.5
  213.2 14.4 %all_to_all.67 = f32[64,2,128]{2,1,0:T(2,128)S(1)} all-to-all(f32[64,2,128]{2,1,0:T(2,128)S(1)} %chain.5), channel_id=1, replica_groups=mesh['cuts_0'=4,'cuts_1'=2,'cuts_2'=8,'circ_0'=4,'circ_1'=2] {'cuts_0','..., dimensions={0} | all-to-all | bytes 131072 | tf_op jit(solution)/shard_map/all_to_all | solution.py:153
  227.7 0.6 reshape.50
  (15 shorter events, 0.1 us)
Async XLA Ops:
  0.6 1.0 copy-start.6
  1.6 0.7 copy-start.11
  3.0 22.8 %all-to-all-start = ((f32[64,4,128]{2,1,0:T(4,128)}), f32[64,4,128]{2,1,0:T(4,128)S(1)}, u32[]{:S(2)}, u32[]{:S(2)}) async-start(f32[64,4,128]{2,1,0:T(4,128)} %load.1), calls=%async_computation | async-start | bytes 262144 | tf_op jit(solution)/shard_map/all_to_all | solution.py:153
  26.5 15.2 %all-to-all-start.1 = ((f32[64,2,128]{2,1,0:T(2,128)}), f32[64,2,128]{2,1,0:T(2,128)S(1)}, u32[]{:S(2)}, u32[]{:S(2)}) async-start(f32[64,2,128]{2,1,0:T(2,128)} %chain.3.old_ref), calls=%async_computation.1 | async-start | bytes 131072 | tf_op jit(solution)/shard_map/all_to_all | solution.py:153
  31.8 0.7 copy-start.9
  32.5 1.6 copy-start.12
  34.1 1.2 copy-start.13
  35.3 6.4 %copy-start.8 = (s32[1,4]{1,0:T(1,128)S(1)}, s32[1,4]{1,0:T(1,128)}, u32[]{:S(2)}) copy-start(s32[1,4]{1,0:T(1,128)} %param.10) | copy-start | bytes 52
  35.3 17.3 %copy-start.7 = (bf16[1,8,1,16,1024]{4,3,2,1,0:T(8,128)(2,1)S(1)}, bf16[1,8,1,16,1024]{4,3,2,1,0:T(8,128)(2,1)}, u32[]{:S(2)}) copy-start(bf16[1,8,1,16,1024]{4,3,2,1,0:T(8,128)(2,1)} %param.7) | copy-start | bytes 786436
  35.3 17.3 %copy-start.10 = (f32[1,1,1024]{2,1,0:T(1,128)S(1)}, f32[1,1,1024]{2,1,0:T(1,128)}, u32[]{:S(2)}) copy-start(f32[1,1,1024]{2,1,0:T(1,128)} %param.9) | copy-start | bytes 12292
  39.1 1.3 copy-start
  40.4 1.3 copy-start.3
  43.2 18.0 %all-to-all-start.2 = ((f32[8,16,128]{2,1,0:T(8,128)}), f32[8,16,128]{2,1,0:T(8,128)S(1)}, u32[]{:S(2)}, u32[]{:S(2)}) async-start(f32[8,16,128]{2,1,0:T(8,128)} %get-tuple-element.17), calls=%async_computation.2 | async-start | bytes 131072 | tf_op jit(solution)/shard_map/all_to_all | solution.py:157
  52.6 1.6 copy-start.4
  62.2 42.3 %copy-start.1 = (bf16[1024,1024]{1,0:T(8,128)(2,1)S(1)}, bf16[1024,1024]{1,0:T(8,128)(2,1)}, u32[]{:S(2)}) copy-start(bf16[1024,1024]{1,0:T(8,128)(2,1)} %copy-done) | copy-start | bytes 6291460
  142.4 11.6 %all-to-all-start.7 = ((f32[8,16,128]{2,1,0:T(8,128)}), f32[8,16,128]{2,1,0:T(8,128)S(1)}, u32[]{:S(2)}, u32[]{:S(2)}) async-start(f32[8,16,128]{2,1,0:T(8,128)} %get-tuple-element.24), calls=%async_computation.7 | async-start | bytes 131072 | tf_op jit(solution)/shard_map/all_to_all | solution.py:157
  146.0 1.6 copy-start.5
  155.0 41.9 %copy-start.2 = (bf16[1024,1024]{1,0:T(8,128)(2,1)S(1)}, bf16[1024,1024]{1,0:T(8,128)(2,1)}, u32[]{:S(2)}) copy-start(bf16[1024,1024]{1,0:T(8,128)(2,1)} %copy-done) | copy-start | bytes 6291460

commit v2 on v1

--- a/solution.py
+++ b/solution.py
@@ -12,29 +12,29 @@
 PORTS = 128
 KC = 4
 SUBS = 8
+CHIPS = 4
 LANES = 128
 CUTS = ("cuts_0", "cuts_1", "cuts_2")
 CIRC = ("circ_0", "circ_1")
 F32 = jnp.float32
 BF16 = jnp.bfloat16
 VMEM = pl.BlockSpec(memory_space=pltpu.VMEM)
-SMEM = pl.BlockSpec(memory_space=pltpu.SMEM)
+HBM = pl.BlockSpec(memory_space=pl.ANY)
 
 
 def shape(dims, dtype=F32):
     return jax.ShapeDtypeStruct(dims, dtype)
 
 
-def call(body, outs, args, name, flops=0, scratch=()):
-    specs = [SMEM if a.dtype == jnp.int32 else VMEM for a in args]
+def call(body, outs, args, name, flops=0, scratch=(), place=VMEM, grant=16):
     size = sum(a.size * a.dtype.itemsize for a in (*args, *outs))
     return pl.pallas_call(
         body,
         out_shape=outs,
-        in_specs=specs,
+        in_specs=[place] * len(args),
         out_specs=[VMEM] * len(outs),
         scratch_shapes=list(scratch),
-        compiler_params=pltpu.CompilerParams(vmem_limit_bytes=32 << 20),
+        compiler_params=pltpu.CompilerParams(vmem_limit_bytes=grant << 20),
         cost_estimate=pl.CostEstimate(flops=flops, bytes_accessed=size, transcendentals=0),
         name=name,
     )(*args)
@@ -50,14 +50,24 @@
         out_ref[b, 0:2, :] = state[2 * pair : 2 * pair + 2, block * LANES : (block + 1) * LANES]
 
 
-def load_body(sources_ref, decay_ref, out_ref):
-    total = sources_ref[0].astype(F32)
-    for t in range(1, STEPS):
-        total = total + sources_ref[t].astype(F32)
+def load_body(sources_ref, decay_ref, out_ref, held_ref, rate_ref, sems):
+    rate = pltpu.make_async_copy(decay_ref, rate_ref, sems.at[STEPS])
+    steps = [
+        pltpu.make_async_copy(sources_ref.at[t], held_ref.at[t], sems.at[t]) for t in range(STEPS)
+    ]
+    for step in steps:
+        step.start()
+    rate.start()
+    total = None
+    for t, step in enumerate(steps):
+        step.wait()
+        now = held_ref[t].astype(F32)
+        total = now if total is None else total + now
     pack(total * (1.0 / STEPS), out_ref)
+    rate.wait()
     for b in range(64):
         block = b // 8
-        row = decay_ref[:, block * LANES : (block + 1) * LANES]
+        row = rate_ref[:, block * LANES : (block + 1) * LANES]
         out_ref[b, 2:4, :] = jnp.concatenate([row, row], axis=0)
 
 
@@ -73,36 +83,37 @@
     ch_ref[...] = dot(h_ref[...], ct_ref[...]).astype(BF16)
 
 
-def first_chain_body(mine_ref, terms_ref, initial_ref, start_ref):
-    start = initial_ref[mine_ref[0]]
+def first_chain_body(terms_ref, initial_ref, start_ref):
+    start = initial_ref[...]
     for n in range(64):
         start_ref[n] = start
         start = terms_ref[n, 2:4, :] * start + terms_ref[n, 0:2, :]
 
 
-def chain_body(mine_ref, last_ref, terms_ref, old_ref, initial_ref, start_ref):
-    start = initial_ref[mine_ref[0]]
+def chain_body(last_ref, terms_ref, old_ref, initial_ref, start_ref):
+    start = initial_ref[...]
     for n in range(64):
         start_ref[n] = start
         decay = terms_ref[n, 2:4, :]
         start = decay * start + (last_ref[n] - decay * old_ref[n])
 
 
-def group(target_ref, blocks, out_ref):
-    for g in range(SUBS):
-        total = None
-        for k in range(KC):
-            feeds = jnp.where(target_ref[k] == g, F32(1.0), F32(0.0))
-            term = feeds * blocks[:, k * PORTS : (k + 1) * PORTS]
-            total = term if total is None else total + term
-        out_ref[g] = total
-
-
-def start_body(target_ref, pieces_ref, ct_ref, start_ref, out_ref):
+def group(feeds_ref, first, blocks):
+    total = None
+    for k in range(KC):
+        at = first * KC + k
+        term = feeds_ref[at : at + 1, :] * blocks[:, k * PORTS : (k + 1) * PORTS]
+        total = term if total is None else total + term
+    return total
+
+
+def start_body(feeds_ref, pieces_ref, ct_ref, start_ref, out_ref):
     for b in range(64):
         block, pair = divmod(b, 8)
         start_ref[2 * pair : 2 * pair + 2, block * LANES : (block + 1) * LANES] = pieces_ref[b]
-    group(target_ref, dot(start_ref[...].astype(BF16), ct_ref[...]), out_ref)
+    blocks = dot(start_ref[...].astype(BF16), ct_ref[...])
+    for g in range(SUBS):
+        out_ref[g] = group(feeds_ref, g, blocks)
 
 
 def free_body(start_ref, sources_ref, m_ref, bt_ref, ct_ref, z_ref, cz_ref, low_ref):
@@ -123,15 +134,24 @@
         x_ref[k * SCEN :, columns] = inflow[: (STEPS - k) * SCEN]
 
 
-def couple_first_body(target_ref, f_ref, cz_ref, ch_ref, out_ref, x_ref):
+def couple_first_body(feeds_ref, f_ref, cz_ref, ch_ref, blocks_ref, out_ref, x_ref):
     inflow = jnp.sum(f_ref[...], axis=0).astype(BF16)
     delays(jnp.concatenate([inflow] * STEPS, axis=0), x_ref)
-    group(target_ref, cz_ref[...] + dot(x_ref[...], ch_ref[...]), out_ref)
-
-
-def couple_body(target_ref, f_ref, cz_ref, ch_ref, out_ref, x_ref):
+    blocks_ref[...] = cz_ref[...] + dot(x_ref[...], ch_ref[...])
+    for g in range(CHIPS):
+        out_ref[g] = group(feeds_ref, g, blocks_ref[...])
+
+
+def couple_body(feeds_ref, f_ref, cz_ref, ch_ref, blocks_ref, out_ref, x_ref):
     delays(jnp.sum(f_ref[...], axis=0).astype(BF16), x_ref)
-    group(target_ref, cz_ref[...] + dot(x_ref[...], ch_ref[...]), out_ref)
+    blocks_ref[...] = cz_ref[...] + dot(x_ref[...], ch_ref[...])
+    for g in range(CHIPS):
+        out_ref[g] = group(feeds_ref, g, blocks_ref[...])
+
+
+def gather_body(feeds_ref, blocks_ref, got_ref, out_ref):
+    for g in range(CHIPS):
+        out_ref[g] = got_ref[g] + group(feeds_ref, g, blocks_ref[...])
 
 
 def last_step_body(f_ref, z_ref, h_ref, out_ref, x_ref):
@@ -155,6 +175,19 @@
 
 def over_circ(blocks):
     return lax.all_to_all(blocks, CIRC, 0, 0, tiled=True)
+
+
+def over_chips(blocks):
+    return lax.all_to_all(blocks, CIRC[0], 0, 0, tiled=True)
+
+
+def other_core(blocks):
+    return lax.ppermute(blocks, CIRC[1], [(0, 1), (1, 0)])
+
+
+def feeds_of(target, owners):
+    feeds = (target[None, :] == owners[:, None]).astype(F32)
+    return jnp.broadcast_to(feeds.reshape(-1, 1), (feeds.size, LANES))
 
 
 def shards(
@@ -174,10 +207,27 @@
     factor = memory_factor.reshape(1, nodes)
     decay = coarse_decay.reshape(1, nodes)
     target = coupling_target.reshape(KC)
-    mine = lax.axis_index(CUTS).reshape(1).astype(jnp.int32)
-    initial = initial_state.reshape(SCEN, 8, LANES).transpose(1, 0, 2).reshape(64, 2, LANES)
-
-    (loads,) = call(load_body, [shape((64, 4, LANES))], (src, decay), "load")
+    core = lax.axis_index(CIRC[1]).astype(jnp.int32)
+    chips = 2 * jnp.arange(CHIPS, dtype=jnp.int32)
+    feeds_all = feeds_of(target, jnp.arange(SUBS, dtype=jnp.int32))
+    feeds_own = feeds_of(target, chips + core)
+    feeds_other = feeds_of(target, chips + 1 - core)
+    pairs = initial_state.reshape(SCEN, 8, LANES).transpose(1, 0, 2).reshape(64, 2, LANES)
+    initial = lax.dynamic_index_in_dim(pairs, lax.axis_index(CUTS), 0, keepdims=False)
+
+    (loads,) = call(
+        load_body,
+        [shape((64, 4, LANES))],
+        (src, decay),
+        "load",
+        scratch=[
+            pltpu.VMEM((STEPS, SCEN, nodes), BF16),
+            pltpu.VMEM((1, nodes), F32),
+            pltpu.SemaphoreType.DMA((STEPS + 1,)),
+        ],
+        place=HBM,
+        grant=60,
+    )
     terms = over_cuts(loads)
     bt, ct, h, ch = call(
         setup_body,
@@ -191,14 +241,15 @@
         "setup",
         flops=2 * nodes * nodes * (7 * PORTS + KC * PORTS),
     )
-    (starts,) = call(first_chain_body, [shape((64, 2, LANES))], (mine, terms, initial), "chain")
+    terms, bt, ct, h, ch = lax.optimization_barrier((terms, bt, ct, h, ch))
+    (starts,) = call(first_chain_body, [shape((64, 2, LANES))], (terms, initial), "chain")
     wave = None
     for iteration in range(ITERS):
         pieces = over_cuts(starts)
         start, sent = call(
             start_body,
             [shape((SCEN, nodes)), shape((SUBS, SCEN, PORTS))],
-            (target, pieces, ct),
+            (feeds_all, pieces, ct),
             "start",
             flops=2 * SCEN * nodes * KC * PORTS,
         )
@@ -213,15 +264,21 @@
         )
         delayed = [pltpu.VMEM((rows, STEPS * PORTS), BF16)]
         for body in (couple_first_body, couple_body):
-            (sent,) = call(
+            blocks, sent = call(
                 body,
-                [shape((SUBS, rows, PORTS))],
-                (target, inflow, cz, ch),
+                [shape((rows, KC * PORTS)), shape((CHIPS, rows, PORTS))],
+                (feeds_other, inflow, cz, ch),
                 "couple",
                 flops=2 * rows * nodes * KC * PORTS,
                 scratch=delayed,
             )
-            inflow = over_circ(sent)
+            (sent,) = call(
+                gather_body,
+                [shape((CHIPS, rows, PORTS))],
+                (feeds_own, blocks, other_core(sent)),
+                "gather",
+            )
+            inflow = over_chips(sent)
         if iteration < ITERS - 1:
             (last,) = call(
                 last_step_body,
@@ -243,7 +300,7 @@
         (starts,) = call(
             chain_body,
             [shape((64, 2, LANES))],
-            (mine, over_cuts(last), terms, starts, initial),
+            (over_cuts(last), terms, starts, initial),
             "chain",
         )
     pieces = over_cuts(starts)

time: 229 us -> 218 us (0.952)
  blocking collectives: 147 us -> 115 us
  starting transfers between devices: 30.6 us -> 44.2 us
  waiting for transfers between devices: 17.7 us -> 23.1 us
    all_to_all x4, blocking collectives: 82.2 us -> 56.2 us  [over_chips(): return lax.all_to_all(blocks, CIRC[0], 0, 0, tiled=True)]
    ppermute x0 -> x4, starting transfers between devices: none -> 7.67 us  [other_core(): return lax.ppermute(blocks, CIRC[1], [(0, 1), (1, 0)])]
    all_to_all x4, blocking collectives: 64.6 us -> 58.5 us  [over_cuts(): return lax.all_to_all(pieces, CUTS, 0, 0, tiled=True)]
    all_to_all x2, starting transfers between devices: 17.6 us -> 23.6 us  [over_cuts(): return lax.all_to_all(pieces, CUTS, 0, 0, tiled=True)]
    ppermute x0 -> x4, waiting for transfers between devices: none -> 5.68 us  [other_core(): return lax.ppermute(blocks, CIRC[1], [(0, 1), (1, 0)])]
    pallas_call x15 -> x19, Pallas kernels: 19.9 us -> 19.4 us  [call(): pl.pallas_call(body, out_shape=outs, in_specs=[place] * len(args), out_sp...]
    unnamed x29 -> x39, local copies, waits for them, and re-layouts: 11.8 us -> 11.7 us
  transfers between devices with their start and end apart: 4 -> 8, of which waited for: 3 -> 7; matrix products, arithmetic and copies ran while one was open for 0% -> 1% of each run, Pallas kernels for 4% -> 4%
where the time goes in v2:
time: 218 us; the launch traced here: 216 us
  blocking collectives  115 us (53%)
  starting transfers between devices  44.2 us (20%)
  waiting for transfers between devices  23.1 us (11%)
  Pallas kernels  19.4 us (9%)
  local copies, waits for them, and re-layouts  14.1 us (6%)
    all_to_all x4, blocking collectives, over_cuts(): return lax.all_to_all(pieces, CUTS, 0, 0, tiled=True)  58.5 us
    all_to_all x4, blocking collectives, over_chips(): return lax.all_to_all(blocks, CIRC[0], 0, 0, tiled=True)  56.2 us
    all_to_all x2, starting transfers between devices, over_cuts(): return lax.all_to_all(pieces, CUTS, 0, 0, tiled=True)  23.6 us
    pallas_call x19, Pallas kernels, call(): pl.pallas_call(body, out_shape=outs, in_specs=[place] * len(args), out_sp...  19.4 us
    all_to_all x2, starting transfers between devices, over_circ(): return lax.all_to_all(blocks, CIRC, 0, 0, tiled=True)  12.9 us
    unnamed x39, local copies, waits for them, and re-layouts  11.7 us
    all_to_all x2, waiting for transfers between devices, over_cuts(): return lax.all_to_all(pieces, CUTS, 0, 0, tiled=True)  9.69 us
    all_to_all x2, waiting for transfers between devices, over_circ(): return lax.all_to_all(blocks, CIRC, 0, 0, tiled=True)  7.68 us
  transfers between devices with their start and end apart: 8, of which 7 were waited for; matrix products, arithmetic and copies ran while one was open for 1% of the time, Pallas kernels for 4%

profile of v2, /device:TPU:8, one launch (start us, length us, event | category | flops | bytes accessed | tf_op | source)
XLA Modules:
  0.0 216.5 jit_solution(11889832063341066904)
XLA Ops:
  0.6 1.6 load.1
  2.3 12.4 %all-to-all-start = ((f32[64,4,128]{2,1,0:T(4,128)}), f32[64,4,128]{2,1,0:T(4,128)S(1)}, u32[]{:S(2)}, u32[]{:S(2)}) async-start(f32[64,4,128]{2,1,0:T(4,128)} %load.1), calls=%async_computation | async-start | bytes 262144 | tf_op jit(solution)/shard_map/all_to_all | solution.py:173
  14.7 0.9 copy.15
  15.6 0.7 copy-done.11
  16.3 1.6 copy-done.16
  17.9 1.2 copy-done.17
  19.1 3.8 %setup.1 = (bf16[1024,1024]{1,0:T(8,128)(2,1)S(1)}, bf16[1024,512]{1,0:T(8,128)(2,1)S(1)}, bf16[1024,1024]{1,0:T(8,128)(2,1)S(1)}, bf16[1024,512]{1,0:T(8,128)(2,1)S(1)}) custom-call(bf16[1024,1024]{1,0:T(8,128)(2,1)S(1)} %bitcast.26, bf16[512,1024]{1,0:T(8,128)(2,1)S(1)} %bitcast.27, f32[1,1024]{1,0:T(1,128)S(1)} %bitcast.23), custom_call_target="tpu_custom_call" | custom-call | flops 2952790016 | bytes 9441280 | tf_op jit(solution)/shard_map/setup/pallas_call | solution.py:31
  22.9 1.4 copy-done
  24.3 1.3 copy-done.3
  25.6 0.8 chain.3.old_ref
  26.4 11.2 %all-to-all-start.1 = ((f32[64,2,128]{2,1,0:T(2,128)}), f32[64,2,128]{2,1,0:T(2,128)S(1)}, u32[]{:S(2)}, u32[]{:S(2)}) async-start(f32[64,2,128]{2,1,0:T(2,128)} %chain.3.old_ref), calls=%async_computation.1 | async-start | bytes 131072 | tf_op jit(solution)/shard_map/all_to_all | solution.py:173
  37.7 9.7 %all-to-all-done.1.pieces_ref = f32[64,2,128]{2,1,0:T(2,128)S(1)} async-done(((f32[64,2,128]{2,1,0:T(2,128)}), f32[64,2,128]{2,1,0:T(2,128)S(1)}, u32[]{:S(2)}, u32[]{:S(2)}) %all-to-all-start.1) | async-done | bytes 65568 | tf_op jit(solution)/shard_map/all_to_all | solution.py:173
  47.5 0.9 start.2
  48.4 9.4 %all-to-all-start.2 = ((f32[8,16,128]{2,1,0:T(8,128)}), f32[8,16,128]{2,1,0:T(8,128)S(1)}, u32[]{:S(2)}, u32[]{:S(2)}) async-start(f32[8,16,128]{2,1,0:T(8,128)} %get-tuple-element.35), calls=%async_computation.2 | async-start | bytes 131072 | tf_op jit(solution)/shard_map/all_to_all | solution.py:177
  58.0 1.6 copy-done.4
  59.6 2.6 %free.2 = (f32[128,1024]{1,0:T(8,128)S(1)}, f32[128,512]{1,0:T(8,128)S(1)}) custom-call(f32[16,1024]{1,0:T(8,128)S(1)} %get-tuple-element.36.start_ref, bf16[8,16,1024]{2,1,0:T(8,128)(2,1)S(1)} %bitcast.21, f32[1,1024]{1,0:T(1,128)S(1)} %bitcast.24, bf16[1024,1024]{1,0:T(8,128)(2,1)S(1)} %copy-done.4, bf16[1024,512]{1,0:T(8,128)(2,1)S(1)} %get-tuple-element.34.ct_ref), custom_call_target="tpu_custom_call" | custom-call | flops 402653184 | bytes 4263936 | tf_op jit(solution)/shard_map/free/pallas_call | solution.py:31
  62.2 3.9 %all-to-all-done.2.f_ref = f32[8,16,128]{2,1,0:T(8,128)S(1)} async-done(((f32[8,16,128]{2,1,0:T(8,128)}), f32[8,16,128]{2,1,0:T(8,128)S(1)}, u32[]{:S(2)}, u32[]{:S(2)}) %all-to-all-start.2) | async-done | bytes 65568 | tf_op jit(solution)/shard_map/all_to_all | solution.py:177
  66.0 0.6 copy-done.7
  66.7 0.8 copy-done.8
  67.6 1.1 couple.4
  68.6 1.9 collective-permute-start
  70.6 0.7 reshape.107
  71.2 1.2 collective-permute-done.got_ref
  72.4 0.7 broadcast_in_dim.6.feeds_ref
  73.1 1.2 gather.4
  74.3 14.3 %all_to_all.60.f_ref = f32[4,128,128]{2,1,0:T(8,128)S(1)} all-to-all(f32[4,128,128]{2,1,0:T(8,128)S(1)} %gather.4), channel_id=1, replica_groups=mesh['cuts_0'=4,'cuts_1'=2,'cuts_2'=8,'circ_0'=4,'circ_1'=2] {'circ_0'}, dimensions={0} | all-to-all | bytes 524288 | tf_op jit(solution)/shard_map/all_to_all | solution.py:181
  89.0 1.9 collective-permute-start.1
  91.0 1.5 collective-permute-done.1.got_ref
  92.6 13.8 %all_to_all.61.f_ref = f32[4,128,128]{2,1,0:T(8,128)S(1)} all-to-all(f32[4,128,128]{2,1,0:T(8,128)S(1)} %gather.5), channel_id=1, replica_groups=mesh['cuts_0'=4,'cuts_1'=2,'cuts_2'=8,'circ_0'=4,'circ_1'=2] {'circ_0'}, dimensions={0} | all-to-all | bytes 524288 | tf_op jit(solution)/shard_map/all_to_all | solution.py:181
  106.4 0.4 last.1
  106.7 14.8 %all_to_all.62.last_ref = f32[64,2,128]{2,1,0:T(2,128)S(1)} all-to-all(f32[64,2,128]{2,1,0:T(2,128)S(1)} %last.1), channel_id=1, replica_groups=mesh['cuts_0'=4,'cuts_1'=2,'cuts_2'=8,'circ_0'=4,'circ_1'=2] {'cuts_0','..., dimensions={0} | all-to-all | bytes 131072 | tf_op jit(solution)/shard_map/all_to_all | solution.py:173
  121.6 1.0 chain.4.old_ref
  122.5 14.5 %all_to_all.63.pieces_ref = f32[64,2,128]{2,1,0:T(2,128)S(1)} all-to-all(f32[64,2,128]{2,1,0:T(2,128)S(1)} %chain.4.old_ref), channel_id=1, replica_groups=mesh['cuts_0'=4,'cuts_1'=2,'cuts_2'=8,'circ_0'=4,'circ_1'=2] {'cuts_0','..., dimensions={0} | all-to-all | bytes 131072 | tf_op jit(solution)/shard_map/all_to_all | solution.py:173
  137.0 0.9 start.3
  137.9 3.5 %all-to-all-start.7 = ((f32[8,16,128]{2,1,0:T(8,128)}), f32[8,16,128]{2,1,0:T(8,128)S(1)}, u32[]{:S(2)}, u32[]{:S(2)}) async-start(f32[8,16,128]{2,1,0:T(8,128)} %get-tuple-element.46), calls=%async_computation.7 | async-start | bytes 131072 | tf_op jit(solution)/shard_map/all_to_all | solution.py:177
  141.5 1.6 copy-done.5
  143.0 2.6 %free.3 = (f32[128,1024]{1,0:T(8,128)S(1)}, f32[128,512]{1,0:T(8,128)S(1)}) custom-call(f32[16,1024]{1,0:T(8,128)S(1)} %get-tuple-element.47.start_ref, bf16[8,16,1024]{2,1,0:T(8,128)(2,1)S(1)} %bitcast.22, f32[1,1024]{1,0:T(1,128)S(1)} %bitcast.25, bf16[1024,1024]{1,0:T(8,128)(2,1)S(1)} %copy-done.5, bf16[1024,512]{1,0:T(8,128)(2,1)S(1)} %get-tuple-element.34.ct_ref), custom_call_target="tpu_custom_call" | custom-call | flops 402653184 | bytes 4263936 | tf_op jit(solution)/shard_map/free/pallas_call | solution.py:31
  145.7 3.8 %all-to-all-done.7.f_ref = f32[8,16,128]{2,1,0:T(8,128)S(1)} async-done(((f32[8,16,128]{2,1,0:T(8,128)}), f32[8,16,128]{2,1,0:T(8,128)S(1)}, u32[]{:S(2)}, u32[]{:S(2)}) %all-to-all-start.7) | async-done | bytes 65568 | tf_op jit(solution)/shard_map/all_to_all | solution.py:177
  149.8 1.9 collective-permute-start.2
  151.8 1.5 collective-permute-done.2.got_ref
  153.4 14.2 %all_to_all.64.f_ref = f32[4,128,128]{2,1,0:T(8,128)S(1)} all-to-all(f32[4,128,128]{2,1,0:T(8,128)S(1)} %gather.6), channel_id=1, replica_groups=mesh['cuts_0'=4,'cuts_1'=2,'cuts_2'=8,'circ_0'=4,'circ_1'=2] {'circ_0'}, dimensions={0} | all-to-all | bytes 524288 | tf_op jit(solution)/shard_map/all_to_all | solution.py:181
  168.0 1.9 collective-permute-start.3
  169.9 1.5 collective-permute-done.3.got_ref
  171.5 13.8 %all_to_all.65.f_ref = f32[4,128,128]{2,1,0:T(8,128)S(1)} all-to-all(f32[4,128,128]{2,1,0:T(8,128)S(1)} %gather.7), channel_id=1, replica_groups=mesh['cuts_0'=4,'cuts_1'=2,'cuts_2'=8,'circ_0'=4,'circ_1'=2] {'circ_0'}, dimensions={0} | all-to-all | bytes 524288 | tf_op jit(solution)/shard_map/all_to_all | solution.py:181
  185.3 1.2 wave.1
  186.4 14.7 %all_to_all.66.last_ref = f32[64,2,128]{2,1,0:T(2,128)S(1)} all-to-all(f32[64,2,128]{2,1,0:T(2,128)S(1)} %get-tuple-element.54), channel_id=1, replica_groups=mesh['cuts_0'=4,'cuts_1'=2,'cuts_2'=8,'circ_0'=4,'circ_1'=2] {'cuts_0','..., dimensions={0} | all-to-all | bytes 131072 | tf_op jit(solution)/shard_map/all_to_all | solution.py:173
  201.3 14.5 %all_to_all.67 = f32[64,2,128]{2,1,0:T(2,128)S(1)} all-to-all(f32[64,2,128]{2,1,0:T(2,128)S(1)} %chain.5), channel_id=1, replica_groups=mesh['cuts_0'=4,'cuts_1'=2,'cuts_2'=8,'circ_0'=4,'circ_1'=2] {'cuts_0','..., dimensions={0} | all-to-all | bytes 131072 | tf_op jit(solution)/shard_map/all_to_all | solution.py:173
  215.8 0.6 reshape.105
  (47 shorter events, 1.9 us)
Async XLA Ops:
  2.3 23.3 %all-to-all-start = ((f32[64,4,128]{2,1,0:T(4,128)}), f32[64,4,128]{2,1,0:T(4,128)S(1)}, u32[]{:S(2)}, u32[]{:S(2)}) async-start(f32[64,4,128]{2,1,0:T(4,128)} %load.1), calls=%async_computation | async-start | bytes 262144 | tf_op jit(solution)/shard_map/all_to_all | solution.py:173
  15.6 10.0 %copy-start.14 = (f32[2,128]{1,0:T(2,128)}, f32[2,128]{1,0:T(2,128)S(1)}, u32[]{:S(2)}) copy-start(f32[2,128]{1,0:T(2,128)S(1)} %dynamic-slice_bitcast_fusion.initial_ref) | copy-start | bytes 3076
  15.6 0.7 copy-start.11
  16.3 1.6 copy-start.16
  17.9 1.2 copy-start.17
  19.1 18.5 %copy-start.18 = (s32[1,4]{1,0:T(1,128)S(1)}, s32[1,4]{1,0:T(1,128)}, u32[]{:S(2)}) copy-start(s32[1,4]{1,0:T(1,128)} %param.10) | copy-start | bytes 52
  19.1 38.9 %copy-start.6 = (bf16[1,8,1,16,1024]{4,3,2,1,0:T(8,128)(2,1)S(1)}, bf16[1,8,1,16,1024]{4,3,2,1,0:T(8,128)(2,1)}, u32[]{:S(2)}) copy-start(bf16[1,8,1,16,1024]{4,3,2,1,0:T(8,128)(2,1)} %param.7) | copy-start | bytes 786436
  19.1 38.9 %copy-start.12 = (f32[1,1,1024]{2,1,0:T(1,128)S(1)}, f32[1,1,1024]{2,1,0:T(1,128)}, u32[]{:S(2)}) copy-start(f32[1,1,1024]{2,1,0:T(1,128)} %param.9) | copy-start | bytes 12292
  22.9 1.4 copy-start
  24.3 1.3 copy-start.3
  26.4 21.1 %all-to-all-start.1 = ((f32[64,2,128]{2,1,0:T(2,128)}), f32[64,2,128]{2,1,0:T(2,128)S(1)}, u32[]{:S(2)}, u32[]{:S(2)}) async-start(f32[64,2,128]{2,1,0:T(2,128)} %chain.3.old_ref), calls=%async_computation.1 | async-start | bytes 131072 | tf_op jit(solution)/shard_map/all_to_all | solution.py:173
  47.5 0.9 copy-start.9
  48.4 17.6 %all-to-all-start.2 = ((f32[8,16,128]{2,1,0:T(8,128)}), f32[8,16,128]{2,1,0:T(8,128)S(1)}, u32[]{:S(2)}, u32[]{:S(2)}) async-start(f32[8,16,128]{2,1,0:T(8,128)} %get-tuple-element.35), calls=%async_computation.2 | async-start | bytes 131072 | tf_op jit(solution)/shard_map/all_to_all | solution.py:177
  58.0 1.6 copy-start.4
  66.0 0.6 copy-start.7
  66.7 0.8 copy-start.8
  68.6 3.8 %collective-permute-start = (f32[4,128,128]{2,1,0:T(8,128)}, f32[4,128,128]{2,1,0:T(8,128)}, u32[]{:S(2)}, u32[]{:S(2)}) collective-permute-start(f32[4,128,128]{2,1,0:T(8,128)} %get-tuple-element.41), channel_id=1, source_target_pairs={{0,1},{1,0},{2,3},{3,2},{4,5},{5,4},{6,7},{7,6},{8,9},{9,8},{10,11... | collective-permute-start | bytes 786440 | tf_op jit(solution)/shard_map/ppermute | solution.py:185
  73.1 33.2 %copy-start.1 = (bf16[1024,1024]{1,0:T(8,128)(2,1)S(1)}, bf16[1024,1024]{1,0:T(8,128)(2,1)}, u32[]{:S(2)}) copy-start(bf16[1024,1024]{1,0:T(8,128)(2,1)} %copy-done) | copy-start | bytes 6291460
  89.0 3.4 %collective-permute-start.1 = (f32[4,128,128]{2,1,0:T(8,128)S(1)}, f32[4,128,128]{2,1,0:T(8,128)S(1)}, u32[]{:S(2)}, u32[]{:S(2)}) collective-permute-start(f32[4,128,128]{2,1,0:T(8,128)S(1)} %get-tuple-element.43), channel_id=1, source_target_pairs={{0,1},{1,0},{2,3},{3,2},{4,5},{5,4},{6,7},{7,6},{8,9},{9,8},{10,11... | collective-permute-start | bytes 786440 | tf_op jit(solution)/shard_map/ppermute | solution.py:185
  92.5 29.1 %copy-start.15 = (f32[2,128]{1,0:T(2,128)S(1)}, f32[2,128]{1,0:T(2,128)}, u32[]{:S(2)}) copy-start(f32[2,128]{1,0:T(2,128)} %copy-done.14) | copy-start | bytes 3076
  92.5 44.4 %copy-start.10 = (f32[32,128]{1,0:T(8,128)S(1)}, f32[32,128]{1,0:T(8,128)}, u32[]{:S(2)}) copy-start(f32[32,128]{1,0:T(8,128)} %copy-done.9) | copy-start | bytes 49156
  106.4 35.1 %copy-start.13 = (f32[1,1,1024]{2,1,0:T(1,128)S(1)}, f32[1,1,1024]{2,1,0:T(1,128)}, u32[]{:S(2)}) copy-start(f32[1,1,1024]{2,1,0:T(1,128)} %param.9) | copy-start | bytes 12292
  137.9 11.6 %all-to-all-start.7 = ((f32[8,16,128]{2,1,0:T(8,128)}), f32[8,16,128]{2,1,0:T(8,128)S(1)}, u32[]{:S(2)}, u32[]{:S(2)}) async-start(f32[8,16,128]{2,1,0:T(8,128)} %get-tuple-element.46), calls=%async_computation.7 | async-start | bytes 131072 | tf_op jit(solution)/shard_map/all_to_all | solution.py:177
  141.4 1.6 copy-start.5
  149.8 3.4 %collective-permute-start.2 = (f32[4,128,128]{2,1,0:T(8,128)S(1)}, f32[4,128,128]{2,1,0:T(8,128)S(1)}, u32[]{:S(2)}, u32[]{:S(2)}) collective-permute-start(f32[4,128,128]{2,1,0:T(8,128)S(1)} %get-tuple-element.50), channel_id=1, source_target_pairs={{0,1},{1,0},{2,3},{3,2},{4,5},{5,4},{6,7},{7,6},{8,9},{9,8},{10,11... | collective-permute-start | bytes 786440 | tf_op jit(solution)/shard_map/ppermute | solution.py:185
  153.3 32.0 %copy-start.2 = (bf16[1024,1024]{1,0:T(8,128)(2,1)S(1)}, bf16[1024,1024]{1,0:T(8,128)(2,1)}, u32[]{:S(2)}) copy-start(bf16[1024,1024]{1,0:T(8,128)(2,1)} %copy-done) | copy-start | bytes 6291460
  168.0 3.4 %collective-permute-start.3 = (f32[4,128,128]{2,1,0:T(8,128)S(1)}, f32[4,128,128]{2,1,0:T(8,128)S(1)}, u32[]{:S(2)}, u32[]{:S(2)}) collective-permute-start(f32[4,128,128]{2,1,0:T(8,128)S(1)} %get-tuple-element.52), channel_id=1, source_target_pairs={{0,1},{1,0},{2,3},{3,2},{4,5},{5,4},{6,7},{7,6},{8,9},{9,8},{10,11... | collective-permute-start | bytes 786440 | tf_op jit(solution)/shard_map/ppermute | solution.py:185

commit v3 on v2

--- a/solution.py
+++ b/solution.py
@@ -13,6 +13,7 @@
 KC = 4
 SUBS = 8
 CHIPS = 4
+PARTS = 4
 LANES = 128
 CUTS = ("cuts_0", "cuts_1", "cuts_2")
 CIRC = ("circ_0", "circ_1")
@@ -26,13 +27,13 @@
     return jax.ShapeDtypeStruct(dims, dtype)
 
 
-def call(body, outs, args, name, flops=0, scratch=(), place=VMEM, grant=16):
+def call(body, outs, args, name, flops=0, scratch=(), place=VMEM, grant=16, out_places=None):
     size = sum(a.size * a.dtype.itemsize for a in (*args, *outs))
     return pl.pallas_call(
         body,
         out_shape=outs,
         in_specs=[place] * len(args),
-        out_specs=[VMEM] * len(outs),
+        out_specs=out_places or [VMEM] * len(outs),
         scratch_shapes=list(scratch),
         compiler_params=pltpu.CompilerParams(vmem_limit_bytes=grant << 20),
         cost_estimate=pl.CostEstimate(flops=flops, bytes_accessed=size, transcendentals=0),
@@ -48,6 +49,12 @@
     for b in range(64):
         block, pair = divmod(b, 8)
         out_ref[b, 0:2, :] = state[2 * pair : 2 * pair + 2, block * LANES : (block + 1) * LANES]
+
+
+def unpack(pieces_ref, state_ref):
+    for b in range(64):
+        block, pair = divmod(b, 8)
+        state_ref[2 * pair : 2 * pair + 2, block * LANES : (block + 1) * LANES] = pieces_ref[b]
 
 
 def load_body(sources_ref, decay_ref, out_ref, held_ref, rate_ref, sems):
@@ -71,16 +78,39 @@
         out_ref[b, 2:4, :] = jnp.concatenate([row, row], axis=0)
 
 
-def setup_body(b_ref, c_ref, m_ref, bt_ref, ct_ref, h_ref, ch_ref):
-    bt_ref[...] = b_ref[...].T
-    ct_ref[...] = c_ref[...].T
+def setup_body(
+    b_hbm, c_hbm, m_hbm, bt_hbm, ct_ref, h_hbm, ch_ref, b_ref, c_ref, m_ref, bt_ref, h_ref, sems
+):
+    part = b_ref.shape[0] // PARTS
+    rows = [slice(k * part, (k + 1) * part) for k in range(PARTS)]
+    parts = [
+        pltpu.make_async_copy(b_hbm.at[r], b_ref.at[r], sems.at[k]) for k, r in enumerate(rows)
+    ]
+    weight = pltpu.make_async_copy(c_hbm, c_ref, sems.at[PARTS])
+    factor = pltpu.make_async_copy(m_hbm, m_ref, sems.at[PARTS + 1])
+    factor.start()
+    for copy in parts:
+        copy.start()
+    weight.start()
+    for r, copy in zip(rows, parts):
+        copy.wait()
+        bt_ref[:, r] = b_ref[r, :].T
+    turned = pltpu.make_async_copy(bt_ref, bt_hbm, sems.at[PARTS + 2])
+    turned.start()
+    factor.wait()
     response = bt_ref[0:PORTS, :]
     h_ref[0:PORTS, :] = response
     response = response.astype(F32)
     for k in range(1, STEPS):
         response = dot((m_ref[...] * response).astype(BF16), bt_ref[...])
         h_ref[k * PORTS : (k + 1) * PORTS, :] = response.astype(BF16)
+    kept = pltpu.make_async_copy(h_ref, h_hbm, sems.at[PARTS + 3])
+    kept.start()
+    weight.wait()
+    ct_ref[...] = c_ref[...].T
     ch_ref[...] = dot(h_ref[...], ct_ref[...]).astype(BF16)
+    turned.wait()
+    kept.wait()
 
 
 def first_chain_body(terms_ref, initial_ref, start_ref):
@@ -98,22 +128,20 @@
         start = decay * start + (last_ref[n] - decay * old_ref[n])
 
 
-def group(feeds_ref, first, blocks):
+def group(target_ref, first, owner, blocks):
     total = None
     for k in range(KC):
-        at = first * KC + k
-        term = feeds_ref[at : at + 1, :] * blocks[:, k * PORTS : (k + 1) * PORTS]
+        feeds = target_ref[first + k : first + k + 1, :] == owner
+        term = jnp.where(feeds, blocks[:, k * PORTS : (k + 1) * PORTS], F32(0.0))
         total = term if total is None else total + term
     return total
 
 
-def start_body(feeds_ref, pieces_ref, ct_ref, start_ref, out_ref):
-    for b in range(64):
-        block, pair = divmod(b, 8)
-        start_ref[2 * pair : 2 * pair + 2, block * LANES : (block + 1) * LANES] = pieces_ref[b]
+def start_body(target_ref, pieces_ref, ct_ref, start_ref, out_ref):
+    unpack(pieces_ref, start_ref)
     blocks = dot(start_ref[...].astype(BF16), ct_ref[...])
     for g in range(SUBS):
-        out_ref[g] = group(feeds_ref, g, blocks)
+        out_ref[g] = group(target_ref, 0, g, blocks)
 
 
 def free_body(start_ref, sources_ref, m_ref, bt_ref, ct_ref, z_ref, cz_ref, low_ref):
@@ -134,24 +162,24 @@
         x_ref[k * SCEN :, columns] = inflow[: (STEPS - k) * SCEN]
 
 
-def couple_first_body(feeds_ref, f_ref, cz_ref, ch_ref, blocks_ref, out_ref, x_ref):
+def couple_first_body(target_ref, f_ref, cz_ref, ch_ref, blocks_ref, out_ref, x_ref):
     inflow = jnp.sum(f_ref[...], axis=0).astype(BF16)
     delays(jnp.concatenate([inflow] * STEPS, axis=0), x_ref)
     blocks_ref[...] = cz_ref[...] + dot(x_ref[...], ch_ref[...])
     for g in range(CHIPS):
-        out_ref[g] = group(feeds_ref, g, blocks_ref[...])
-
-
-def couple_body(feeds_ref, f_ref, cz_ref, ch_ref, blocks_ref, out_ref, x_ref):
+        out_ref[g] = group(target_ref, 2 * KC, 2 * g, blocks_ref[...])
+
+
+def couple_body(target_ref, f_ref, cz_ref, ch_ref, blocks_ref, out_ref, x_ref):
     delays(jnp.sum(f_ref[...], axis=0).astype(BF16), x_ref)
     blocks_ref[...] = cz_ref[...] + dot(x_ref[...], ch_ref[...])
     for g in range(CHIPS):
-        out_ref[g] = group(feeds_ref, g, blocks_ref[...])
-
-
-def gather_body(feeds_ref, blocks_ref, got_ref, out_ref):
+        out_ref[g] = group(target_ref, 2 * KC, 2 * g, blocks_ref[...])
+
+
+def gather_body(target_ref, blocks_ref, got_ref, out_ref):
     for g in range(CHIPS):
-        out_ref[g] = got_ref[g] + group(feeds_ref, g, blocks_ref[...])
+        out_ref[g] = got_ref[g] + group(target_ref, KC, 2 * g, blocks_ref[...])
 
 
 def last_step_body(f_ref, z_ref, h_ref, out_ref, x_ref):
@@ -169,6 +197,10 @@
     pack(wave[(STEPS - 1) * SCEN :, :], out_ref)
 
 
+def unpack_body(pieces_ref, state_ref):
+    unpack(pieces_ref, state_ref)
+
+
 def over_cuts(pieces):
     return lax.all_to_all(pieces, CUTS, 0, 0, tiled=True)
 
@@ -183,11 +215,6 @@
 
 def other_core(blocks):
     return lax.ppermute(blocks, CIRC[1], [(0, 1), (1, 0)])
-
-
-def feeds_of(target, owners):
-    feeds = (target[None, :] == owners[:, None]).astype(F32)
-    return jnp.broadcast_to(feeds.reshape(-1, 1), (feeds.size, LANES))
 
 
 def shards(
@@ -208,10 +235,8 @@
     decay = coarse_decay.reshape(1, nodes)
     target = coupling_target.reshape(KC)
     core = lax.axis_index(CIRC[1]).astype(jnp.int32)
-    chips = 2 * jnp.arange(CHIPS, dtype=jnp.int32)
-    feeds_all = feeds_of(target, jnp.arange(SUBS, dtype=jnp.int32))
-    feeds_own = feeds_of(target, chips + core)
-    feeds_other = feeds_of(target, chips + 1 - core)
+    targets = jnp.concatenate([target, target - core, target - (1 - core)])
+    targets = jnp.broadcast_to(targets[:, None], (3 * KC, LANES))
     pairs = initial_state.reshape(SCEN, 8, LANES).transpose(1, 0, 2).reshape(64, 2, LANES)
     initial = lax.dynamic_index_in_dim(pairs, lax.axis_index(CUTS), 0, keepdims=False)
 
@@ -240,16 +265,29 @@
         (inverse, weight, factor),
         "setup",
         flops=2 * nodes * nodes * (7 * PORTS + KC * PORTS),
-    )
-    terms, bt, ct, h, ch = lax.optimization_barrier((terms, bt, ct, h, ch))
+        scratch=[
+            pltpu.VMEM((nodes, nodes), BF16),
+            pltpu.VMEM((KC * PORTS, nodes), BF16),
+            pltpu.VMEM((1, nodes), F32),
+            pltpu.VMEM((nodes, nodes), BF16),
+            pltpu.VMEM((STEPS * PORTS, nodes), BF16),
+            pltpu.SemaphoreType.DMA((PARTS + 4,)),
+        ],
+        place=HBM,
+        grant=56,
+        out_places=[HBM, VMEM, HBM, VMEM],
+    )
+    terms, targets, initial, bt, ct, h, ch = lax.optimization_barrier(
+        (terms, targets, initial, bt, ct, h, ch)
+    )
     (starts,) = call(first_chain_body, [shape((64, 2, LANES))], (terms, initial), "chain")
+    pieces = over_cuts(starts)
     wave = None
     for iteration in range(ITERS):
-        pieces = over_cuts(starts)
         start, sent = call(
             start_body,
             [shape((SCEN, nodes)), shape((SUBS, SCEN, PORTS))],
-            (feeds_all, pieces, ct),
+            (targets, pieces, ct),
             "start",
             flops=2 * SCEN * nodes * KC * PORTS,
         )
@@ -267,7 +305,7 @@
             blocks, sent = call(
                 body,
                 [shape((rows, KC * PORTS)), shape((CHIPS, rows, PORTS))],
-                (feeds_other, inflow, cz, ch),
+                (targets, inflow, cz, ch),
                 "couple",
                 flops=2 * rows * nodes * KC * PORTS,
                 scratch=delayed,
@@ -275,7 +313,7 @@
             (sent,) = call(
                 gather_body,
                 [shape((CHIPS, rows, PORTS))],
-                (feeds_own, blocks, other_core(sent)),
+                (targets, blocks, other_core(sent)),
                 "gather",
             )
             inflow = over_chips(sent)
@@ -303,9 +341,9 @@
             (over_cuts(last), terms, starts, initial),
             "chain",
         )
-    pieces = over_cuts(starts)
-    start = pieces.reshape(8, SCEN, LANES).transpose(1, 0, 2).reshape(1, 1, SCEN, nodes)
-    return start, wave.reshape(1, STEPS, 1, SCEN, nodes)
+        pieces = over_cuts(starts)
+    (start,) = call(unpack_body, [shape((SCEN, nodes))], (pieces,), "unpack")
+    return start.reshape(1, 1, SCEN, nodes), wave.reshape(1, STEPS, 1, SCEN, nodes)
 
 
 def solution(mesh):

time: 218 us -> 213 us (0.977)
  blocking collectives: 115 us -> 136 us
  starting transfers between devices: 44.2 us -> 32.8 us
  waiting for transfers between devices: 23.1 us -> 13.9 us
  local copies, waits for them, and re-layouts: 14.1 us -> 6.58 us
    all_to_all x4 -> x5, blocking collectives: 58.5 us -> 78.4 us  [over_cuts(): return lax.all_to_all(pieces, CUTS, 0, 0, tiled=True)]
    all_to_all x2 -> x1, starting transfers between devices: 23.6 us -> 12.4 us  [over_cuts(): return lax.all_to_all(pieces, CUTS, 0, 0, tiled=True)]
    all_to_all x2 -> x1, waiting for transfers between devices: 9.69 us -> 1.09 us  [over_cuts(): return lax.all_to_all(pieces, CUTS, 0, 0, tiled=True)]
    unnamed x39 -> x21, local copies, waits for them, and re-layouts: 11.7 us -> 6.5 us
    pallas_call x19 -> x20, Pallas kernels: 19.4 us -> 20.1 us  [call(): pl.pallas_call(body, out_shape=outs, in_specs=[place] * len(args), out_sp...]
  transfers between devices with their start and end apart: 8 -> 7, of which waited for: 7 -> 7; matrix products, arithmetic and copies ran while one was open for 1% -> 1% of each run, Pallas kernels for 4% -> 6%
where the time goes in v3:
time: 213 us; the launch traced here: 212 us
  blocking collectives  136 us (64%)
  starting transfers between devices  32.8 us (15%)
  Pallas kernels  20.1 us (9%)
  waiting for transfers between devices  13.9 us (7%)
  local copies, waits for them, and re-layouts  6.58 us (3%)
    all_to_all x5, blocking collectives, over_cuts(): return lax.all_to_all(pieces, CUTS, 0, 0, tiled=True)  78.4 us
    all_to_all x4, blocking collectives, over_chips(): return lax.all_to_all(blocks, CIRC[0], 0, 0, tiled=True)  57.5 us
    pallas_call x20, Pallas kernels, call(): pl.pallas_call(body, out_shape=outs, in_specs=[place] * len(args), out_sp...  20.1 us
    all_to_all x2, starting transfers between devices, over_circ(): return lax.all_to_all(blocks, CIRC, 0, 0, tiled=True)  12.8 us
    all_to_all x1, starting transfers between devices, over_cuts(): return lax.all_to_all(pieces, CUTS, 0, 0, tiled=True)  12.4 us
    ppermute x4, starting transfers between devices, other_core(): return lax.ppermute(blocks, CIRC[1], [(0, 1), (1, 0)])  7.68 us
    all_to_all x2, waiting for transfers between devices, over_circ(): return lax.all_to_all(blocks, CIRC, 0, 0, tiled=True)  6.79 us
    unnamed x21, local copies, waits for them, and re-layouts  6.5 us
  transfers between devices with their start and end apart: 7, of which 7 were waited for; matrix products, arithmetic and copies ran while one was open for 1% of the time, Pallas kernels for 6%

profile of v3, /device:TPU:8, one launch (start us, length us, event | category | flops | bytes accessed | tf_op | source)
XLA Modules:
  0.0 211.5 jit_solution(6543158789337244595)
XLA Ops:
  0.6 1.6 load.1
  2.3 12.4 %all-to-all-start = ((f32[64,4,128]{2,1,0:T(4,128)}), f32[64,4,128]{2,1,0:T(4,128)S(1)}, u32[]{:S(2)}, u32[]{:S(2)}) async-start(f32[64,4,128]{2,1,0:T(4,128)} %load.1), calls=%async_computation | async-start | bytes 262144 | tf_op jit(solution)/shard_map/all_to_all | solution.py:205
  14.7 0.9 copy.11
  15.6 0.7 broadcast_subtract_fusion.1
  16.2 0.7 pad_add_fusion
  17.0 7.0 %setup.1 = (bf16[1024,1024]{1,0:T(8,128)(2,1)}, bf16[1024,512]{1,0:T(8,128)(2,1)}, bf16[1024,1024]{1,0:T(8,128)(2,1)}, bf16[1024,512]{1,0:T(8,128)(2,1)}) custom-call(bf16[1024,1024]{1,0:T(8,128)(2,1)} %bitcast.32, bf16[512,1024]{1,0:T(8,128)(2,1)} %bitcast.33, f32[1,1024]{1,0:T(1,128)} %bitcast.23), custom_call_target="tpu_custom_call" | custom-call | flops 2952790016 | bytes 9441280 | tf_op jit(solution)/shard_map/setup/pallas_call | solution.py:32
  24.0 1.1 all-to-all-done.terms_ref
  25.1 0.1 chain.3.old_ref
  25.3 19.8 %all_to_all.60.pieces_ref = f32[64,2,128]{2,1,0:T(2,128)S(1)} all-to-all(f32[64,2,128]{2,1,0:T(2,128)S(1)} %chain.3.old_ref), channel_id=1, replica_groups=mesh['cuts_0'=4,'cuts_1'=2,'cuts_2'=8,'circ_0'=4,'circ_1'=2] {'cuts_0','..., dimensions={0} | all-to-all | bytes 131072 | tf_op jit(solution)/shard_map/all_to_all | solution.py:205
  45.0 1.2 copy-done.1
  46.3 0.9 start.2
  47.2 9.4 %all-to-all-start.2 = ((f32[8,16,128]{2,1,0:T(8,128)}), f32[8,16,128]{2,1,0:T(8,128)S(1)}, u32[]{:S(2)}, u32[]{:S(2)}) async-start(f32[8,16,128]{2,1,0:T(8,128)} %get-tuple-element.39), calls=%async_computation.2 | async-start | bytes 131072 | tf_op jit(solution)/shard_map/all_to_all | solution.py:209
  56.6 1.2 copy-done.2
  57.8 1.6 copy-done.6
  59.4 2.6 %free.2 = (f32[128,1024]{1,0:T(8,128)S(1)}, f32[128,512]{1,0:T(8,128)S(1)}) custom-call(f32[16,1024]{1,0:T(8,128)S(1)} %get-tuple-element.40.start_ref, bf16[8,16,1024]{2,1,0:T(8,128)(2,1)S(1)} %bitcast.21, f32[1,1024]{1,0:T(1,128)S(1)} %bitcast.24, bf16[1024,1024]{1,0:T(8,128)(2,1)S(1)} %copy-done.6, bf16[1024,512]{1,0:T(8,128)(2,1)S(1)} %copy-done.2), custom_call_target="tpu_custom_call" | custom-call | flops 402653184 | bytes 4263936 | tf_op jit(solution)/shard_map/free/pallas_call | solution.py:32
  62.0 2.8 %all-to-all-done.2.f_ref = f32[8,16,128]{2,1,0:T(8,128)S(1)} async-done(((f32[8,16,128]{2,1,0:T(8,128)}), f32[8,16,128]{2,1,0:T(8,128)S(1)}, u32[]{:S(2)}, u32[]{:S(2)}) %all-to-all-start.2) | async-done | bytes 65568 | tf_op jit(solution)/shard_map/all_to_all | solution.py:209
  64.8 0.3 couple.4
  65.2 1.9 collective-permute-start
  67.1 1.5 collective-permute-done.got_ref
  68.6 0.1 gather.4
  68.7 15.5 %all_to_all.61.f_ref = f32[4,128,128]{2,1,0:T(8,128)S(1)} all-to-all(f32[4,128,128]{2,1,0:T(8,128)S(1)} %gather.4), channel_id=1, replica_groups=mesh['cuts_0'=4,'cuts_1'=2,'cuts_2'=8,'circ_0'=4,'circ_1'=2] {'circ_0'}, dimensions={0} | all-to-all | bytes 524288 | tf_op jit(solution)/shard_map/all_to_all | solution.py:213
  84.2 0.4 couple.5
  84.6 1.9 collective-permute-start.1
  86.5 1.5 collective-permute-done.1.got_ref
  88.1 13.9 %all_to_all.62.f_ref = f32[4,128,128]{2,1,0:T(8,128)S(1)} all-to-all(f32[4,128,128]{2,1,0:T(8,128)S(1)} %gather.5), channel_id=1, replica_groups=mesh['cuts_0'=4,'cuts_1'=2,'cuts_2'=8,'circ_0'=4,'circ_1'=2] {'circ_0'}, dimensions={0} | all-to-all | bytes 524288 | tf_op jit(solution)/shard_map/all_to_all | solution.py:213
  102.1 0.4 last.1
  102.4 14.8 %all_to_all.63.last_ref = f32[64,2,128]{2,1,0:T(2,128)S(1)} all-to-all(f32[64,2,128]{2,1,0:T(2,128)S(1)} %last.1), channel_id=1, replica_groups=mesh['cuts_0'=4,'cuts_1'=2,'cuts_2'=8,'circ_0'=4,'circ_1'=2] {'cuts_0','..., dimensions={0} | all-to-all | bytes 131072 | tf_op jit(solution)/shard_map/all_to_all | solution.py:205
  117.3 0.1 chain.4.old_ref
  117.4 14.6 %all_to_all.64.pieces_ref = f32[64,2,128]{2,1,0:T(2,128)S(1)} all-to-all(f32[64,2,128]{2,1,0:T(2,128)S(1)} %chain.4.old_ref), channel_id=1, replica_groups=mesh['cuts_0'=4,'cuts_1'=2,'cuts_2'=8,'circ_0'=4,'circ_1'=2] {'cuts_0','..., dimensions={0} | all-to-all | bytes 131072 | tf_op jit(solution)/shard_map/all_to_all | solution.py:205
  132.0 0.9 start.3
  133.0 3.4 %all-to-all-start.7 = ((f32[8,16,128]{2,1,0:T(8,128)}), f32[8,16,128]{2,1,0:T(8,128)S(1)}, u32[]{:S(2)}, u32[]{:S(2)}) async-start(f32[8,16,128]{2,1,0:T(8,128)} %get-tuple-element.50), calls=%async_computation.7 | async-start | bytes 131072 | tf_op jit(solution)/shard_map/all_to_all | solution.py:209
  136.3 1.6 copy-done.7
  137.9 2.6 %free.3 = (f32[128,1024]{1,0:T(8,128)S(1)}, f32[128,512]{1,0:T(8,128)S(1)}) custom-call(f32[16,1024]{1,0:T(8,128)S(1)} %get-tuple-element.51.start_ref, bf16[8,16,1024]{2,1,0:T(8,128)(2,1)S(1)} %bitcast.22, f32[1,1024]{1,0:T(1,128)S(1)} %bitcast.25, bf16[1024,1024]{1,0:T(8,128)(2,1)S(1)} %copy-done.7, bf16[1024,512]{1,0:T(8,128)(2,1)S(1)} %copy-done.3), custom_call_target="tpu_custom_call" | custom-call | flops 402653184 | bytes 4263936 | tf_op jit(solution)/shard_map/free/pallas_call | solution.py:32
  140.5 4.0 %all-to-all-done.7.f_ref = f32[8,16,128]{2,1,0:T(8,128)S(1)} async-done(((f32[8,16,128]{2,1,0:T(8,128)}), f32[8,16,128]{2,1,0:T(8,128)S(1)}, u32[]{:S(2)}, u32[]{:S(2)}) %all-to-all-start.7) | async-done | bytes 65568 | tf_op jit(solution)/shard_map/all_to_all | solution.py:209
  144.5 0.3 couple.6
  144.9 1.9 collective-permute-start.2
  146.8 1.5 collective-permute-done.2.got_ref
  148.3 0.1 gather.6
  148.4 14.3 %all_to_all.65.f_ref = f32[4,128,128]{2,1,0:T(8,128)S(1)} all-to-all(f32[4,128,128]{2,1,0:T(8,128)S(1)} %gather.6), channel_id=1, replica_groups=mesh['cuts_0'=4,'cuts_1'=2,'cuts_2'=8,'circ_0'=4,'circ_1'=2] {'circ_0'}, dimensions={0} | all-to-all | bytes 524288 | tf_op jit(solution)/shard_map/all_to_all | solution.py:213
  162.6 0.4 couple.7
  163.0 1.9 collective-permute-start.3
  164.9 1.5 collective-permute-done.3.got_ref
  166.5 13.8 %all_to_all.66.f_ref = f32[4,128,128]{2,1,0:T(8,128)S(1)} all-to-all(f32[4,128,128]{2,1,0:T(8,128)S(1)} %gather.7), channel_id=1, replica_groups=mesh['cuts_0'=4,'cuts_1'=2,'cuts_2'=8,'circ_0'=4,'circ_1'=2] {'circ_0'}, dimensions={0} | all-to-all | bytes 524288 | tf_op jit(solution)/shard_map/all_to_all | solution.py:213
  180.3 1.2 wave.1
  181.5 14.8 %all_to_all.67.last_ref = f32[64,2,128]{2,1,0:T(2,128)S(1)} all-to-all(f32[64,2,128]{2,1,0:T(2,128)S(1)} %get-tuple-element.58), channel_id=1, replica_groups=mesh['cuts_0'=4,'cuts_1'=2,'cuts_2'=8,'circ_0'=4,'circ_1'=2] {'cuts_0','..., dimensions={0} | all-to-all | bytes 131072 | tf_op jit(solution)/shard_map/all_to_all | solution.py:205
  196.3 0.1 chain.5
  196.4 14.5 %all_to_all.68.pieces_ref = f32[64,2,128]{2,1,0:T(2,128)S(1)} all-to-all(f32[64,2,128]{2,1,0:T(2,128)S(1)} %chain.5), channel_id=1, replica_groups=mesh['cuts_0'=4,'cuts_1'=2,'cuts_2'=8,'circ_0'=4,'circ_1'=2] {'cuts_0','..., dimensions={0} | all-to-all | bytes 131072 | tf_op jit(solution)/shard_map/all_to_all | solution.py:205
  210.9 0.7 unpack.1
  (21 shorter events, 0.3 us)
Async XLA Ops:
  2.3 22.8 %all-to-all-start = ((f32[64,4,128]{2,1,0:T(4,128)}), f32[64,4,128]{2,1,0:T(4,128)S(1)}, u32[]{:S(2)}, u32[]{:S(2)}) async-start(f32[64,4,128]{2,1,0:T(4,128)} %load.1), calls=%async_computation | async-start | bytes 262144 | tf_op jit(solution)/shard_map/all_to_all | solution.py:205
  17.0 39.6 %copy-start.8 = (bf16[1,8,1,16,1024]{4,3,2,1,0:T(8,128)(2,1)S(1)}, bf16[1,8,1,16,1024]{4,3,2,1,0:T(8,128)(2,1)}, u32[]{:S(2)}) copy-start(bf16[1,8,1,16,1024]{4,3,2,1,0:T(8,128)(2,1)} %param.7) | copy-start | bytes 786436
  17.0 39.6 %copy-start.9 = (f32[1,1,1024]{2,1,0:T(1,128)S(1)}, f32[1,1,1024]{2,1,0:T(1,128)}, u32[]{:S(2)}) copy-start(f32[1,1,1024]{2,1,0:T(1,128)} %param.9) | copy-start | bytes 12292
  45.0 1.2 copy-start.1
  46.3 18.6 %copy-start = (bf16[1024,512]{1,0:T(8,128)(2,1)S(1)}, bf16[1024,512]{1,0:T(8,128)(2,1)}, u32[]{:S(2)}) copy-start(bf16[1024,512]{1,0:T(8,128)(2,1)} %get-tuple-element.43.ch_ref) | copy-start | bytes 3145732
  47.2 17.7 %all-to-all-start.2 = ((f32[8,16,128]{2,1,0:T(8,128)}), f32[8,16,128]{2,1,0:T(8,128)S(1)}, u32[]{:S(2)}, u32[]{:S(2)}) async-start(f32[8,16,128]{2,1,0:T(8,128)} %get-tuple-element.39), calls=%async_computation.2 | async-start | bytes 131072 | tf_op jit(solution)/shard_map/all_to_all | solution.py:209
  56.6 1.2 copy-start.2
  57.8 1.6 copy-start.6
  65.2 3.4 %collective-permute-start = (f32[4,128,128]{2,1,0:T(8,128)S(1)}, f32[4,128,128]{2,1,0:T(8,128)S(1)}, u32[]{:S(2)}, u32[]{:S(2)}) collective-permute-start(f32[4,128,128]{2,1,0:T(8,128)S(1)} %get-tuple-element.45), channel_id=1, source_target_pairs={{0,1},{1,0},{2,3},{3,2},{4,5},{5,4},{6,7},{7,6},{8,9},{9,8},{10,11... | collective-permute-start | bytes 786440 | tf_op jit(solution)/shard_map/ppermute | solution.py:217
  68.6 33.4 %copy-start.4 = (bf16[1024,1024]{1,0:T(8,128)(2,1)S(1)}, bf16[1024,1024]{1,0:T(8,128)(2,1)}, u32[]{:S(2)}) copy-start(bf16[1024,1024]{1,0:T(8,128)(2,1)} %get-tuple-element.49.h_ref) | copy-start | bytes 6291460
  84.6 3.4 %collective-permute-start.1 = (f32[4,128,128]{2,1,0:T(8,128)S(1)}, f32[4,128,128]{2,1,0:T(8,128)S(1)}, u32[]{:S(2)}, u32[]{:S(2)}) collective-permute-start(f32[4,128,128]{2,1,0:T(8,128)S(1)} %get-tuple-element.47), channel_id=1, source_target_pairs={{0,1},{1,0},{2,3},{3,2},{4,5},{5,4},{6,7},{7,6},{8,9},{9,8},{10,11... | collective-permute-start | bytes 786440 | tf_op jit(solution)/shard_map/ppermute | solution.py:217
  88.1 43.9 %copy-start.3 = (bf16[1024,512]{1,0:T(8,128)(2,1)S(1)}, bf16[1024,512]{1,0:T(8,128)(2,1)}, u32[]{:S(2)}) copy-start(bf16[1024,512]{1,0:T(8,128)(2,1)} %get-tuple-element.38.ct_ref) | copy-start | bytes 3145732
  133.0 11.5 %all-to-all-start.7 = ((f32[8,16,128]{2,1,0:T(8,128)}), f32[8,16,128]{2,1,0:T(8,128)S(1)}, u32[]{:S(2)}, u32[]{:S(2)}) async-start(f32[8,16,128]{2,1,0:T(8,128)} %get-tuple-element.50), calls=%async_computation.7 | async-start | bytes 131072 | tf_op jit(solution)/shard_map/all_to_all | solution.py:209
  136.3 1.6 copy-start.7
  144.9 3.4 %collective-permute-start.2 = (f32[4,128,128]{2,1,0:T(8,128)S(1)}, f32[4,128,128]{2,1,0:T(8,128)S(1)}, u32[]{:S(2)}, u32[]{:S(2)}) collective-permute-start(f32[4,128,128]{2,1,0:T(8,128)S(1)} %get-tuple-element.54), channel_id=1, source_target_pairs={{0,1},{1,0},{2,3},{3,2},{4,5},{5,4},{6,7},{7,6},{8,9},{9,8},{10,11... | collective-permute-start | bytes 786440 | tf_op jit(solution)/shard_map/ppermute | solution.py:217
  148.3 32.0 %copy-start.5 = (bf16[1024,1024]{1,0:T(8,128)(2,1)S(1)}, bf16[1024,1024]{1,0:T(8,128)(2,1)}, u32[]{:S(2)}) copy-start(bf16[1024,1024]{1,0:T(8,128)(2,1)} %get-tuple-element.49.h_ref) | copy-start | bytes 6291460
  163.0 3.4 %collective-permute-start.3 = (f32[4,128,128]{2,1,0:T(8,128)S(1)}, f32[4,128,128]{2,1,0:T(8,128)S(1)}, u32[]{:S(2)}, u32[]{:S(2)}) collective-permute-start(f32[4,128,128]{2,1,0:T(8,128)S(1)} %get-tuple-element.56), channel_id=1, source_target_pairs={{0,1},{1,0},{2,3},{3,2},{4,5},{5,4},{6,7},{7,6},{8,9},{9,8},{10,11... | collective-permute-start | bytes 786440 | tf_op jit(solution)/shard_map/ppermute | solution.py:217

commit v4 on v3

--- a/solution.py
+++ b/solution.py
@@ -14,6 +14,7 @@
 SUBS = 8
 CHIPS = 4
 PARTS = 4
+GRANT = 50
 LANES = 128
 CUTS = ("cuts_0", "cuts_1", "cuts_2")
 CIRC = ("circ_0", "circ_1")
@@ -27,12 +28,12 @@
     return jax.ShapeDtypeStruct(dims, dtype)
 
 
-def call(body, outs, args, name, flops=0, scratch=(), place=VMEM, grant=16, out_places=None):
+def call(body, outs, args, name, flops=0, scratch=(), places=None, grant=16, out_places=None):
     size = sum(a.size * a.dtype.itemsize for a in (*args, *outs))
     return pl.pallas_call(
         body,
         out_shape=outs,
-        in_specs=[place] * len(args),
+        in_specs=places or [VMEM] * len(args),
         out_specs=out_places or [VMEM] * len(outs),
         scratch_shapes=list(scratch),
         compiler_params=pltpu.CompilerParams(vmem_limit_bytes=grant << 20),
@@ -79,38 +80,54 @@
 
 
 def setup_body(
-    b_hbm, c_hbm, m_hbm, bt_hbm, ct_ref, h_hbm, ch_ref, b_ref, c_ref, m_ref, bt_ref, h_ref, sems
+    b_hbm,
+    c_hbm,
+    target_hbm,
+    initial_hbm,
+    bt_hbm,
+    ct_ref,
+    targets_ref,
+    initial_ref,
+    b_ref,
+    c_ref,
+    bt_ref,
+    target_ref,
+    tile_ref,
+    sems,
 ):
     part = b_ref.shape[0] // PARTS
     rows = [slice(k * part, (k + 1) * part) for k in range(PARTS)]
+    block, pair = jnp.divmod(lax.axis_index(CUTS), 8)
+    tile = initial_hbm.at[
+        pl.ds(pl.multiple_of(pair // 4 * 8, 8), 8), pl.ds(pl.multiple_of(block * LANES, LANES), LANES)
+    ]
+    copies = [
+        pltpu.make_async_copy(target_hbm, target_ref, sems.at[0]),
+        pltpu.make_async_copy(tile, tile_ref, sems.at[1]),
+        pltpu.make_async_copy(c_hbm, c_ref, sems.at[2]),
+    ]
     parts = [
-        pltpu.make_async_copy(b_hbm.at[r], b_ref.at[r], sems.at[k]) for k, r in enumerate(rows)
+        pltpu.make_async_copy(b_hbm.at[r], b_ref.at[r], sems.at[4 + k])
+        for k, r in enumerate(rows)
     ]
-    weight = pltpu.make_async_copy(c_hbm, c_ref, sems.at[PARTS])
-    factor = pltpu.make_async_copy(m_hbm, m_ref, sems.at[PARTS + 1])
-    factor.start()
-    for copy in parts:
+    for copy in copies + parts:
         copy.start()
-    weight.start()
+    for copy in copies:
+        copy.wait()
+    core = lax.axis_index(CIRC[1])
+    for k in range(KC):
+        target = jnp.broadcast_to(target_ref[:, k : k + 1], (1, LANES))
+        targets_ref[k : k + 1, :] = target
+        targets_ref[KC + k : KC + k + 1, :] = target - core
+        targets_ref[2 * KC + k : 2 * KC + k + 1, :] = target - (1 - core)
+    initial_ref[...] = tile_ref[pl.ds(pair % 4 * 2, 2), :]
+    ct_ref[...] = c_ref[...].T
     for r, copy in zip(rows, parts):
         copy.wait()
         bt_ref[:, r] = b_ref[r, :].T
-    turned = pltpu.make_async_copy(bt_ref, bt_hbm, sems.at[PARTS + 2])
+    turned = pltpu.make_async_copy(bt_ref, bt_hbm, sems.at[3])
     turned.start()
-    factor.wait()
-    response = bt_ref[0:PORTS, :]
-    h_ref[0:PORTS, :] = response
-    response = response.astype(F32)
-    for k in range(1, STEPS):
-        response = dot((m_ref[...] * response).astype(BF16), bt_ref[...])
-        h_ref[k * PORTS : (k + 1) * PORTS, :] = response.astype(BF16)
-    kept = pltpu.make_async_copy(h_ref, h_hbm, sems.at[PARTS + 3])
-    kept.start()
-    weight.wait()
-    ct_ref[...] = c_ref[...].T
-    ch_ref[...] = dot(h_ref[...], ct_ref[...]).astype(BF16)
     turned.wait()
-    kept.wait()
 
 
 def first_chain_body(terms_ref, initial_ref, start_ref):
@@ -152,6 +169,56 @@
         z_ref[t * SCEN : (t + 1) * SCEN, :] = previous
         low_ref[t * SCEN : (t + 1) * SCEN, :] = previous.astype(BF16)
     cz_ref[...] = dot(low_ref[...], ct_ref[...])
+
+
+def first_free_body(
+    start_ref,
+    sources_hbm,
+    m_hbm,
+    bt_hbm,
+    ct_ref,
+    z_ref,
+    cz_ref,
+    h_hbm,
+    ch_ref,
+    sources_ref,
+    m_ref,
+    bt_ref,
+    h_ref,
+    low_ref,
+    both_ref,
+    sems,
+):
+    copies = [
+        pltpu.make_async_copy(given, taken, sems.at[k])
+        for k, (given, taken) in enumerate(
+            ((m_hbm, m_ref), (sources_hbm, sources_ref), (bt_hbm, bt_ref))
+        )
+    ]
+    for copy in copies:
+        copy.start()
+    for copy in copies:
+        copy.wait()
+    previous = start_ref[...]
+    h_ref[0:PORTS, :] = bt_ref[0:PORTS, :]
+    response = bt_ref[0:PORTS, :].astype(F32)
+    for t in range(STEPS):
+        drive = m_ref[...] * previous + sources_ref[t].astype(F32)
+        if t == 0:
+            previous = dot(drive.astype(BF16), bt_ref[...])
+        else:
+            both_ref[0:SCEN, :] = drive.astype(BF16)
+            both_ref[SCEN:, :] = (m_ref[...] * response).astype(BF16)
+            both = dot(both_ref[...], bt_ref[...])
+            previous, response = both[:SCEN], both[SCEN:]
+            h_ref[t * PORTS : (t + 1) * PORTS, :] = response.astype(BF16)
+        z_ref[t * SCEN : (t + 1) * SCEN, :] = previous
+        low_ref[t * SCEN : (t + 1) * SCEN, :] = previous.astype(BF16)
+    kept = pltpu.make_async_copy(h_ref, h_hbm, sems.at[3])
+    kept.start()
+    cz_ref[...] = dot(low_ref[...], ct_ref[...])
+    ch_ref[...] = dot(h_ref[...], ct_ref[...]).astype(BF16)
+    kept.wait()
 
 
 def delays(inflow, x_ref):
@@ -233,13 +300,7 @@
     weight = coupling_weight.reshape(KC * PORTS, nodes)
     factor = memory_factor.reshape(1, nodes)
     decay = coarse_decay.reshape(1, nodes)
-    target = coupling_target.reshape(KC)
-    core = lax.axis_index(CIRC[1]).astype(jnp.int32)
-    targets = jnp.concatenate([target, target - core, target - (1 - core)])
-    targets = jnp.broadcast_to(targets[:, None], (3 * KC, LANES))
-    pairs = initial_state.reshape(SCEN, 8, LANES).transpose(1, 0, 2).reshape(64, 2, LANES)
-    initial = lax.dynamic_index_in_dim(pairs, lax.axis_index(CUTS), 0, keepdims=False)
-
+    first = initial_state.reshape(SCEN, nodes)
     (loads,) = call(
         load_body,
         [shape((64, 4, LANES))],
@@ -250,39 +311,37 @@
             pltpu.VMEM((1, nodes), F32),
             pltpu.SemaphoreType.DMA((STEPS + 1,)),
         ],
-        place=HBM,
+        places=[HBM] * 2,
         grant=60,
     )
     terms = over_cuts(loads)
-    bt, ct, h, ch = call(
+    bt, ct, targets, initial = call(
         setup_body,
         [
             shape((nodes, nodes), BF16),
             shape((nodes, KC * PORTS), BF16),
-            shape((STEPS * PORTS, nodes), BF16),
-            shape((STEPS * PORTS, KC * PORTS), BF16),
+            shape((3 * KC, LANES), jnp.int32),
+            shape((2, LANES)),
         ],
-        (inverse, weight, factor),
+        (inverse, weight, coupling_target, first),
         "setup",
-        flops=2 * nodes * nodes * (7 * PORTS + KC * PORTS),
+        flops=2 * nodes * nodes * SCEN,
         scratch=[
             pltpu.VMEM((nodes, nodes), BF16),
             pltpu.VMEM((KC * PORTS, nodes), BF16),
-            pltpu.VMEM((1, nodes), F32),
             pltpu.VMEM((nodes, nodes), BF16),
-            pltpu.VMEM((STEPS * PORTS, nodes), BF16),
-            pltpu.SemaphoreType.DMA((PARTS + 4,)),
+            pltpu.VMEM((1, KC), jnp.int32),
+            pltpu.VMEM((8, LANES), F32),
+            pltpu.SemaphoreType.DMA((4 + PARTS,)),
         ],
-        place=HBM,
-        grant=56,
-        out_places=[HBM, VMEM, HBM, VMEM],
+        places=[HBM] * 4,
+        grant=GRANT,
+        out_places=[HBM, VMEM, VMEM, VMEM],
     )
-    terms, targets, initial, bt, ct, h, ch = lax.optimization_barrier(
-        (terms, targets, initial, bt, ct, h, ch)
-    )
+    terms, targets, initial, bt, ct = lax.optimization_barrier((terms, targets, initial, bt, ct))
     (starts,) = call(first_chain_body, [shape((64, 2, LANES))], (terms, initial), "chain")
     pieces = over_cuts(starts)
-    wave = None
+    h = ch = wave = None
     for iteration in range(ITERS):
         start, sent = call(
             start_body,
@@ -292,14 +351,33 @@
             flops=2 * SCEN * nodes * KC * PORTS,
         )
         inflow = over_circ(sent)
-        z, cz = call(
-            free_body,
-            [shape((rows, nodes)), shape((rows, KC * PORTS))],
-            (start, src, factor, bt, ct),
-            "free",
-            flops=2 * rows * nodes * (nodes + KC * PORTS),
-            scratch=[pltpu.VMEM((rows, nodes), BF16)],
-        )
+        given = (start, src, factor, bt, ct)
+        free = [shape((rows, nodes)), shape((rows, KC * PORTS))]
+        low = pltpu.VMEM((rows, nodes), BF16)
+        flops = 2 * rows * nodes * (nodes + KC * PORTS)
+        if iteration == 0:
+            z, cz, h, ch = call(
+                first_free_body,
+                free
+                + [shape((STEPS * PORTS, nodes), BF16), shape((STEPS * PORTS, KC * PORTS), BF16)],
+                given,
+                "free",
+                flops=9 * flops,
+                scratch=[
+                    pltpu.VMEM((STEPS, SCEN, nodes), BF16),
+                    pltpu.VMEM((1, nodes), F32),
+                    pltpu.VMEM((nodes, nodes), BF16),
+                    pltpu.VMEM((STEPS * PORTS, nodes), BF16),
+                    low,
+                    pltpu.VMEM((SCEN + PORTS, nodes), BF16),
+                    pltpu.SemaphoreType.DMA((4,)),
+                ],
+                places=[VMEM, HBM, HBM, HBM, VMEM],
+                grant=GRANT,
+                out_places=[VMEM, VMEM, HBM, VMEM],
+            )
+        else:
+            z, cz = call(free_body, free, given, "free", flops=flops, scratch=[low])
         delayed = [pltpu.VMEM((rows, STEPS * PORTS), BF16)]
         for body in (couple_first_body, couple_body):
             blocks, sent = call(

time: 213 us -> 209 us (0.981)
  blocking collectives: 136 us -> 133 us
  local copies, waits for them, and re-layouts: 6.58 us -> 4.31 us
    all_to_all x5, blocking collectives: 78.4 us -> 75 us  [over_cuts(): return lax.all_to_all(pieces, CUTS, 0, 0, tiled=True)]
    all_to_all x1, waiting for transfers between devices: 1.09 us -> 4.32 us  [over_cuts(): return lax.all_to_all(pieces, CUTS, 0, 0, tiled=True)]
    unnamed x21 -> x16, local copies, waits for them, and re-layouts: 6.5 us -> 4.31 us
  transfers between devices with their start and end apart: 7 -> 7, of which waited for: 7 -> 7; matrix products, arithmetic and copies ran while one was open for 1% -> 0% of each run, Pallas kernels for 6% -> 6%
where the time goes in v4:
time: 209 us; the launch traced here: 208 us
  blocking collectives  133 us (64%)
  starting transfers between devices  33 us (16%)
  Pallas kernels  20.2 us (10%)
  waiting for transfers between devices  16 us (8%)
  local copies, waits for them, and re-layouts  4.31 us (2%)
    all_to_all x5, blocking collectives, over_cuts(): return lax.all_to_all(pieces, CUTS, 0, 0, tiled=True)  75 us
    all_to_all x4, blocking collectives, over_chips(): return lax.all_to_all(blocks, CIRC[0], 0, 0, tiled=True)  58.3 us
    pallas_call x20, Pallas kernels, call(): pl.pallas_call(body, out_shape=outs, in_specs=places or [VMEM] * len(args...  20.2 us
    all_to_all x2, starting transfers between devices, over_circ(): return lax.all_to_all(blocks, CIRC, 0, 0, tiled=True)  12.9 us
    all_to_all x1, starting transfers between devices, over_cuts(): return lax.all_to_all(pieces, CUTS, 0, 0, tiled=True)  12.4 us
    ppermute x4, starting transfers between devices, other_core(): return lax.ppermute(blocks, CIRC[1], [(0, 1), (1, 0)])  7.68 us
    ppermute x4, waiting for transfers between devices, other_core(): return lax.ppermute(blocks, CIRC[1], [(0, 1), (1, 0)])  6 us
    all_to_all x2, waiting for transfers between devices, over_circ(): return lax.all_to_all(blocks, CIRC, 0, 0, tiled=True)  5.7 us
  transfers between devices with their start and end apart: 7, of which 7 were waited for; matrix products, arithmetic and copies ran while one was open for 0% of the time, Pallas kernels for 6%

profile of v4, /device:TPU:8, one launch (start us, length us, event | category | flops | bytes accessed | tf_op | source)
XLA Modules:
  0.0 207.6 jit_solution(11594414534605533692)
XLA Ops:
  0.6 1.6 load.1
  2.3 12.4 %all-to-all-start = ((f32[64,4,128]{2,1,0:T(4,128)}), f32[64,4,128]{2,1,0:T(4,128)S(1)}, u32[]{:S(2)}, u32[]{:S(2)}) async-start(f32[64,4,128]{2,1,0:T(4,128)} %load.1), calls=%async_computation | async-start | bytes 262144 | tf_op jit(solution)/shard_map/all_to_all | solution.py:272
  14.7 0.0 copy-start.3
  14.7 1.2 copy-done.3
  15.9 0.8 copy-done.5
  16.7 0.7 copy-done.7
  17.4 3.4 %setup.1 = (bf16[1024,1024]{1,0:T(8,128)(2,1)}, bf16[1024,512]{1,0:T(8,128)(2,1)S(1)}, s32[12,128]{1,0:T(8,128)S(1)}, f32[2,128]{1,0:T(2,128)S(1)}) custom-call(bf16[1024,1024]{1,0:T(8,128)(2,1)} %bitcast.17, bf16[512,1024]{1,0:T(8,128)(2,1)S(1)} %bitcast.10, s32[1,4]{1,0:T(1,128)S(1)} %copy-done.7, f32[16,1024]{1,0:T(8,128)S(1)} %bitcast.14), custom_call_target="tpu_custom_call" | custom-call | flops 33554432 | bytes 6364176 | tf_op jit(solution)/shard_map/setup/pallas_call | solution.py:33
  20.8 4.3 %all-to-all-done.terms_ref = f32[64,4,128]{2,1,0:T(4,128)S(1)} async-done(((f32[64,4,128]{2,1,0:T(4,128)}), f32[64,4,128]{2,1,0:T(4,128)S(1)}, u32[]{:S(2)}, u32[]{:S(2)}) %all-to-all-start) | async-done | bytes 131104 | tf_op jit(solution)/shard_map/all_to_all | solution.py:272
  25.1 0.1 chain.3.old_ref
  25.2 16.5 %all_to_all.60.pieces_ref = f32[64,2,128]{2,1,0:T(2,128)S(1)} all-to-all(f32[64,2,128]{2,1,0:T(2,128)S(1)} %chain.3.old_ref), channel_id=1, replica_groups=mesh['cuts_0'=4,'cuts_1'=2,'cuts_2'=8,'circ_0'=4,'circ_1'=2] {'cuts_0','..., dimensions={0} | all-to-all | bytes 131072 | tf_op jit(solution)/shard_map/all_to_all | solution.py:272
  41.7 0.9 start.2
  42.7 9.4 %all-to-all-start.2 = ((f32[8,16,128]{2,1,0:T(8,128)}), f32[8,16,128]{2,1,0:T(8,128)S(1)}, u32[]{:S(2)}, u32[]{:S(2)}) async-start(f32[8,16,128]{2,1,0:T(8,128)} %get-tuple-element.39), calls=%async_computation.2 | async-start | bytes 131072 | tf_op jit(solution)/shard_map/all_to_all | solution.py:276
  52.1 6.4 %free.2 = (f32[128,1024]{1,0:T(8,128)S(1)}, f32[128,512]{1,0:T(8,128)S(1)}, bf16[1024,1024]{1,0:T(8,128)(2,1)}, bf16[1024,512]{1,0:T(8,128)(2,1)S(1)}) custom-call(f32[16,1024]{1,0:T(8,128)S(1)} %get-tuple-element.40.start_ref, bf16[8,16,1024]{2,1,0:T(8,128)(2,1)S(1)} %bitcast.12, f32[1,1024]{1,0:T(1,128)S(1)} %bitcast.15, ...), custom_call_target="tpu_custom_call" | custom-call | flops 3623878656 | bytes 7409664 | tf_op jit(solution)/shard_map/free/pallas_call | solution.py:33
  58.4 1.9 all-to-all-done.2.f_ref
  60.3 0.4 couple.4
  60.7 1.9 collective-permute-start
  62.6 1.5 collective-permute-done.got_ref
  64.1 0.1 gather.4
  64.2 16.5 %all_to_all.61.f_ref = f32[4,128,128]{2,1,0:T(8,128)S(1)} all-to-all(f32[4,128,128]{2,1,0:T(8,128)S(1)} %gather.4), channel_id=1, replica_groups=mesh['cuts_0'=4,'cuts_1'=2,'cuts_2'=8,'circ_0'=4,'circ_1'=2] {'circ_0'}, dimensions={0} | all-to-all | bytes 524288 | tf_op jit(solution)/shard_map/all_to_all | solution.py:280
  80.7 0.4 couple.5
  81.0 1.9 collective-permute-start.1
  82.9 1.5 collective-permute-done.1.got_ref
  84.4 0.1 gather.5
  84.5 13.8 %all_to_all.62.f_ref = f32[4,128,128]{2,1,0:T(8,128)S(1)} all-to-all(f32[4,128,128]{2,1,0:T(8,128)S(1)} %gather.5), channel_id=1, replica_groups=mesh['cuts_0'=4,'cuts_1'=2,'cuts_2'=8,'circ_0'=4,'circ_1'=2] {'circ_0'}, dimensions={0} | all-to-all | bytes 524288 | tf_op jit(solution)/shard_map/all_to_all | solution.py:280
  98.3 0.4 last.1
  98.7 14.8 %all_to_all.63.last_ref = f32[64,2,128]{2,1,0:T(2,128)S(1)} all-to-all(f32[64,2,128]{2,1,0:T(2,128)S(1)} %last.1), channel_id=1, replica_groups=mesh['cuts_0'=4,'cuts_1'=2,'cuts_2'=8,'circ_0'=4,'circ_1'=2] {'cuts_0','..., dimensions={0} | all-to-all | bytes 131072 | tf_op jit(solution)/shard_map/all_to_all | solution.py:272
  113.5 0.1 chain.4.old_ref
  113.7 14.5 %all_to_all.64.pieces_ref = f32[64,2,128]{2,1,0:T(2,128)S(1)} all-to-all(f32[64,2,128]{2,1,0:T(2,128)S(1)} %chain.4.old_ref), channel_id=1, replica_groups=mesh['cuts_0'=4,'cuts_1'=2,'cuts_2'=8,'circ_0'=4,'circ_1'=2] {'cuts_0','..., dimensions={0} | all-to-all | bytes 131072 | tf_op jit(solution)/shard_map/all_to_all | solution.py:272
  128.1 0.9 start.3
  129.0 3.5 %all-to-all-start.7 = ((f32[8,16,128]{2,1,0:T(8,128)}), f32[8,16,128]{2,1,0:T(8,128)S(1)}, u32[]{:S(2)}, u32[]{:S(2)}) async-start(f32[8,16,128]{2,1,0:T(8,128)} %get-tuple-element.50), calls=%async_computation.7 | async-start | bytes 131072 | tf_op jit(solution)/shard_map/all_to_all | solution.py:276
  132.6 1.6 copy-done.2
  134.2 2.6 %free.3 = (f32[128,1024]{1,0:T(8,128)S(1)}, f32[128,512]{1,0:T(8,128)S(1)}) custom-call(f32[16,1024]{1,0:T(8,128)S(1)} %get-tuple-element.51.start_ref, bf16[8,16,1024]{2,1,0:T(8,128)(2,1)S(1)} %bitcast.13, f32[1,1024]{1,0:T(1,128)S(1)} %bitcast.16, bf16[1024,1024]{1,0:T(8,128)(2,1)S(1)} %copy-done.2, bf16[1024,512]{1,0:T(8,128)(2,1)S(1)} %get-tuple-element.38.ct_ref), custom_call_target="tpu_custom_call" | custom-call | flops 402653184 | bytes 4263936 | tf_op jit(solution)/shard_map/free/pallas_call | solution.py:33
  136.8 3.8 %all-to-all-done.7.f_ref = f32[8,16,128]{2,1,0:T(8,128)S(1)} async-done(((f32[8,16,128]{2,1,0:T(8,128)}), f32[8,16,128]{2,1,0:T(8,128)S(1)}, u32[]{:S(2)}, u32[]{:S(2)}) %all-to-all-start.7) | async-done | bytes 65568 | tf_op jit(solution)/shard_map/all_to_all | solution.py:276
  140.6 0.4 couple.6
  141.0 1.9 collective-permute-start.2
  142.9 1.5 collective-permute-done.2.got_ref
  144.4 0.1 gather.6
  144.5 14.2 %all_to_all.65.f_ref = f32[4,128,128]{2,1,0:T(8,128)S(1)} all-to-all(f32[4,128,128]{2,1,0:T(8,128)S(1)} %gather.6), channel_id=1, replica_groups=mesh['cuts_0'=4,'cuts_1'=2,'cuts_2'=8,'circ_0'=4,'circ_1'=2] {'circ_0'}, dimensions={0} | all-to-all | bytes 524288 | tf_op jit(solution)/shard_map/all_to_all | solution.py:280
  158.7 0.4 couple.7
  159.1 1.9 collective-permute-start.3
  161.0 1.5 collective-permute-done.3.got_ref
  162.5 0.1 gather.7
  162.6 13.8 %all_to_all.66.f_ref = f32[4,128,128]{2,1,0:T(8,128)S(1)} all-to-all(f32[4,128,128]{2,1,0:T(8,128)S(1)} %gather.7), channel_id=1, replica_groups=mesh['cuts_0'=4,'cuts_1'=2,'cuts_2'=8,'circ_0'=4,'circ_1'=2] {'circ_0'}, dimensions={0} | all-to-all | bytes 524288 | tf_op jit(solution)/shard_map/all_to_all | solution.py:280
  176.4 1.2 wave.1
  177.6 14.8 %all_to_all.67.last_ref = f32[64,2,128]{2,1,0:T(2,128)S(1)} all-to-all(f32[64,2,128]{2,1,0:T(2,128)S(1)} %get-tuple-element.58), channel_id=1, replica_groups=mesh['cuts_0'=4,'cuts_1'=2,'cuts_2'=8,'circ_0'=4,'circ_1'=2] {'cuts_0','..., dimensions={0} | all-to-all | bytes 131072 | tf_op jit(solution)/shard_map/all_to_all | solution.py:272
  192.4 0.1 chain.5
  192.5 14.4 %all_to_all.68.pieces_ref = f32[64,2,128]{2,1,0:T(2,128)S(1)} all-to-all(f32[64,2,128]{2,1,0:T(2,128)S(1)} %chain.5), channel_id=1, replica_groups=mesh['cuts_0'=4,'cuts_1'=2,'cuts_2'=8,'circ_0'=4,'circ_1'=2] {'cuts_0','..., dimensions={0} | all-to-all | bytes 131072 | tf_op jit(solution)/shard_map/all_to_all | solution.py:272
  207.0 0.7 unpack.1
  (11 shorter events, 0.0 us)
Async XLA Ops:
  2.3 22.8 %all-to-all-start = ((f32[64,4,128]{2,1,0:T(4,128)}), f32[64,4,128]{2,1,0:T(4,128)S(1)}, u32[]{:S(2)}, u32[]{:S(2)}) async-start(f32[64,4,128]{2,1,0:T(4,128)} %load.1), calls=%async_computation | async-start | bytes 262144 | tf_op jit(solution)/shard_map/all_to_all | solution.py:272
  14.7 1.2 copy-start.3
  15.9 0.8 copy-start.5
  16.7 0.7 copy-start.7
  17.4 34.7 %copy-start.4 = (bf16[1,8,1,16,1024]{4,3,2,1,0:T(8,128)(2,1)S(1)}, bf16[1,8,1,16,1024]{4,3,2,1,0:T(8,128)(2,1)}, u32[]{:S(2)}) copy-start(bf16[1,8,1,16,1024]{4,3,2,1,0:T(8,128)(2,1)} %param.7) | copy-start | bytes 786436
  17.4 34.7 %copy-start.6 = (f32[1,1,1024]{2,1,0:T(1,128)S(1)}, f32[1,1,1024]{2,1,0:T(1,128)}, u32[]{:S(2)}) copy-start(f32[1,1,1024]{2,1,0:T(1,128)} %param.9) | copy-start | bytes 12292
  42.7 17.7 %all-to-all-start.2 = ((f32[8,16,128]{2,1,0:T(8,128)}), f32[8,16,128]{2,1,0:T(8,128)S(1)}, u32[]{:S(2)}, u32[]{:S(2)}) async-start(f32[8,16,128]{2,1,0:T(8,128)} %get-tuple-element.39), calls=%async_computation.2 | async-start | bytes 131072 | tf_op jit(solution)/shard_map/all_to_all | solution.py:276
  60.7 3.4 %collective-permute-start = (f32[4,128,128]{2,1,0:T(8,128)S(1)}, f32[4,128,128]{2,1,0:T(8,128)S(1)}, u32[]{:S(2)}, u32[]{:S(2)}) collective-permute-start(f32[4,128,128]{2,1,0:T(8,128)S(1)} %get-tuple-element.45), channel_id=1, source_target_pairs={{0,1},{1,0},{2,3},{3,2},{4,5},{5,4},{6,7},{7,6},{8,9},{9,8},{10,11... | collective-permute-start | bytes 786440 | tf_op jit(solution)/shard_map/ppermute | solution.py:284
  64.1 34.2 %copy-start = (bf16[1024,1024]{1,0:T(8,128)(2,1)S(1)}, bf16[1024,1024]{1,0:T(8,128)(2,1)}, u32[]{:S(2)}) copy-start(bf16[1024,1024]{1,0:T(8,128)(2,1)} %get-tuple-element.49.h_ref) | copy-start | bytes 6291460
  81.0 3.4 %collective-permute-start.1 = (f32[4,128,128]{2,1,0:T(8,128)S(1)}, f32[4,128,128]{2,1,0:T(8,128)S(1)}, u32[]{:S(2)}, u32[]{:S(2)}) collective-permute-start(f32[4,128,128]{2,1,0:T(8,128)S(1)} %get-tuple-element.47), channel_id=1, source_target_pairs={{0,1},{1,0},{2,3},{3,2},{4,5},{5,4},{6,7},{7,6},{8,9},{9,8},{10,11... | collective-permute-start | bytes 786440 | tf_op jit(solution)/shard_map/ppermute | solution.py:284
  129.0 11.6 %all-to-all-start.7 = ((f32[8,16,128]{2,1,0:T(8,128)}), f32[8,16,128]{2,1,0:T(8,128)S(1)}, u32[]{:S(2)}, u32[]{:S(2)}) async-start(f32[8,16,128]{2,1,0:T(8,128)} %get-tuple-element.50), calls=%async_computation.7 | async-start | bytes 131072 | tf_op jit(solution)/shard_map/all_to_all | solution.py:276
  132.6 1.6 copy-start.2
  141.0 3.4 %collective-permute-start.2 = (f32[4,128,128]{2,1,0:T(8,128)S(1)}, f32[4,128,128]{2,1,0:T(8,128)S(1)}, u32[]{:S(2)}, u32[]{:S(2)}) collective-permute-start(f32[4,128,128]{2,1,0:T(8,128)S(1)} %get-tuple-element.54), channel_id=1, source_target_pairs={{0,1},{1,0},{2,3},{3,2},{4,5},{5,4},{6,7},{7,6},{8,9},{9,8},{10,11... | collective-permute-start | bytes 786440 | tf_op jit(solution)/shard_map/ppermute | solution.py:284
  144.4 32.0 %copy-start.1 = (bf16[1024,1024]{1,0:T(8,128)(2,1)S(1)}, bf16[1024,1024]{1,0:T(8,128)(2,1)}, u32[]{:S(2)}) copy-start(bf16[1024,1024]{1,0:T(8,128)(2,1)} %get-tuple-element.49.h_ref) | copy-start | bytes 6291460
  159.1 3.4 %collective-permute-start.3 = (f32[4,128,128]{2,1,0:T(8,128)S(1)}, f32[4,128,128]{2,1,0:T(8,128)S(1)}, u32[]{:S(2)}, u32[]{:S(2)}) collective-permute-start(f32[4,128,128]{2,1,0:T(8,128)S(1)} %get-tuple-element.56), channel_id=1, source_target_pairs={{0,1},{1,0},{2,3},{3,2},{4,5},{5,4},{6,7},{7,6},{8,9},{9,8},{10,11... | collective-permute-start | bytes 786440 | tf_op jit(solution)/shard_map/ppermute | solution.py:284

commit v5 on v4

--- a/solution.py
+++ b/solution.py
@@ -14,7 +14,6 @@
 SUBS = 8
 CHIPS = 4
 PARTS = 4
-GRANT = 50
 LANES = 128
 CUTS = ("cuts_0", "cuts_1", "cuts_2")
 CIRC = ("circ_0", "circ_1")
@@ -58,62 +57,47 @@
         state_ref[2 * pair : 2 * pair + 2, block * LANES : (block + 1) * LANES] = pieces_ref[b]
 
 
-def load_body(sources_ref, decay_ref, out_ref, held_ref, rate_ref, sems):
-    rate = pltpu.make_async_copy(decay_ref, rate_ref, sems.at[STEPS])
+def load_body(
+    sources_ref,
+    decay_ref,
+    target_hbm,
+    initial_hbm,
+    out_ref,
+    targets_ref,
+    initial_ref,
+    held_ref,
+    rate_ref,
+    target_ref,
+    tile_ref,
+    sems,
+):
+    block, pair = jnp.divmod(lax.axis_index(CUTS), 8)
+    tile = initial_hbm.at[
+        pl.ds(pl.multiple_of(pair // 4 * 8, 8), 8), pl.ds(pl.multiple_of(block * LANES, LANES), LANES)
+    ]
     steps = [
         pltpu.make_async_copy(sources_ref.at[t], held_ref.at[t], sems.at[t]) for t in range(STEPS)
     ]
-    for step in steps:
-        step.start()
-    rate.start()
+    small = [
+        pltpu.make_async_copy(given, taken, sems.at[STEPS + k])
+        for k, (given, taken) in enumerate(
+            ((decay_ref, rate_ref), (target_hbm, target_ref), (tile, tile_ref))
+        )
+    ]
+    for copy in steps + small:
+        copy.start()
     total = None
     for t, step in enumerate(steps):
         step.wait()
         now = held_ref[t].astype(F32)
         total = now if total is None else total + now
     pack(total * (1.0 / STEPS), out_ref)
-    rate.wait()
+    for copy in small:
+        copy.wait()
     for b in range(64):
         block = b // 8
         row = rate_ref[:, block * LANES : (block + 1) * LANES]
         out_ref[b, 2:4, :] = jnp.concatenate([row, row], axis=0)
-
-
-def setup_body(
-    b_hbm,
-    c_hbm,
-    target_hbm,
-    initial_hbm,
-    bt_hbm,
-    ct_ref,
-    targets_ref,
-    initial_ref,
-    b_ref,
-    c_ref,
-    bt_ref,
-    target_ref,
-    tile_ref,
-    sems,
-):
-    part = b_ref.shape[0] // PARTS
-    rows = [slice(k * part, (k + 1) * part) for k in range(PARTS)]
-    block, pair = jnp.divmod(lax.axis_index(CUTS), 8)
-    tile = initial_hbm.at[
-        pl.ds(pl.multiple_of(pair // 4 * 8, 8), 8), pl.ds(pl.multiple_of(block * LANES, LANES), LANES)
-    ]
-    copies = [
-        pltpu.make_async_copy(target_hbm, target_ref, sems.at[0]),
-        pltpu.make_async_copy(tile, tile_ref, sems.at[1]),
-        pltpu.make_async_copy(c_hbm, c_ref, sems.at[2]),
-    ]
-    parts = [
-        pltpu.make_async_copy(b_hbm.at[r], b_ref.at[r], sems.at[4 + k])
-        for k, r in enumerate(rows)
-    ]
-    for copy in copies + parts:
-        copy.start()
-    for copy in copies:
-        copy.wait()
     core = lax.axis_index(CIRC[1])
     for k in range(KC):
         target = jnp.broadcast_to(target_ref[:, k : k + 1], (1, LANES))
@@ -121,12 +105,26 @@
         targets_ref[KC + k : KC + k + 1, :] = target - core
         targets_ref[2 * KC + k : 2 * KC + k + 1, :] = target - (1 - core)
     initial_ref[...] = tile_ref[pl.ds(pair % 4 * 2, 2), :]
-    ct_ref[...] = c_ref[...].T
+
+
+def setup_body(b_hbm, c_hbm, bt_hbm, ct_ref, b_ref, c_ref, bt_ref, sems):
+    part = b_ref.shape[0] // PARTS
+    rows = [slice(k * part, (k + 1) * part) for k in range(PARTS)]
+    weight = pltpu.make_async_copy(c_hbm, c_ref, sems.at[0])
+    parts = [
+        pltpu.make_async_copy(b_hbm.at[r], b_ref.at[r], sems.at[2 + k])
+        for k, r in enumerate(rows)
+    ]
+    for copy in parts:
+        copy.start()
+    weight.start()
     for r, copy in zip(rows, parts):
         copy.wait()
         bt_ref[:, r] = b_ref[r, :].T
-    turned = pltpu.make_async_copy(bt_ref, bt_hbm, sems.at[3])
+    turned = pltpu.make_async_copy(bt_ref, bt_hbm, sems.at[1])
     turned.start()
+    weight.wait()
+    ct_ref[...] = c_ref[...].T
     turned.wait()
 
 
@@ -301,44 +299,39 @@
     factor = memory_factor.reshape(1, nodes)
     decay = coarse_decay.reshape(1, nodes)
     first = initial_state.reshape(SCEN, nodes)
-    (loads,) = call(
+    loads, targets, initial = call(
         load_body,
-        [shape((64, 4, LANES))],
-        (src, decay),
+        [shape((64, 4, LANES)), shape((3 * KC, LANES), jnp.int32), shape((2, LANES))],
+        (src, decay, coupling_target, first),
         "load",
         scratch=[
             pltpu.VMEM((STEPS, SCEN, nodes), BF16),
             pltpu.VMEM((1, nodes), F32),
-            pltpu.SemaphoreType.DMA((STEPS + 1,)),
+            pltpu.VMEM((1, KC), jnp.int32),
+            pltpu.VMEM((8, LANES), F32),
+            pltpu.SemaphoreType.DMA((STEPS + 3,)),
         ],
-        places=[HBM] * 2,
+        places=[HBM] * 4,
         grant=60,
     )
     terms = over_cuts(loads)
-    bt, ct, targets, initial = call(
+    bt, ct = call(
         setup_body,
-        [
-            shape((nodes, nodes), BF16),
-            shape((nodes, KC * PORTS), BF16),
-            shape((3 * KC, LANES), jnp.int32),
-            shape((2, LANES)),
-        ],
-        (inverse, weight, coupling_target, first),
+        [shape((nodes, nodes), BF16), shape((nodes, KC * PORTS), BF16)],
+        (inverse, weight),
         "setup",
         flops=2 * nodes * nodes * SCEN,
         scratch=[
             pltpu.VMEM((nodes, nodes), BF16),
             pltpu.VMEM((KC * PORTS, nodes), BF16),
             pltpu.VMEM((nodes, nodes), BF16),
-            pltpu.VMEM((1, KC), jnp.int32),
-            pltpu.VMEM((8, LANES), F32),
-            pltpu.SemaphoreType.DMA((4 + PARTS,)),
+            pltpu.SemaphoreType.DMA((2 + PARTS,)),
         ],
-        places=[HBM] * 4,
-        grant=GRANT,
-        out_places=[HBM, VMEM, VMEM, VMEM],
+        places=[HBM] * 2,
+        grant=52,
+        out_places=[HBM, VMEM],
     )
-    terms, targets, initial, bt, ct = lax.optimization_barrier((terms, targets, initial, bt, ct))
+    terms, bt, ct = lax.optimization_barrier((terms, bt, ct))
     (starts,) = call(first_chain_body, [shape((64, 2, LANES))], (terms, initial), "chain")
     pieces = over_cuts(starts)
     h = ch = wave = None
@@ -373,7 +366,7 @@
                     pltpu.SemaphoreType.DMA((4,)),
                 ],
                 places=[VMEM, HBM, HBM, HBM, VMEM],
-                grant=GRANT,
+                grant=50,
                 out_places=[VMEM, VMEM, HBM, VMEM],
             )
         else:

time: 209 us -> 207 us (level)
  waiting for transfers between devices: 16 us -> 18.8 us
  local copies, waits for them, and re-layouts: 4.31 us -> 1.61 us
    all_to_all x1, waiting for transfers between devices: 4.32 us -> 7.1 us  [over_cuts(): return lax.all_to_all(pieces, CUTS, 0, 0, tiled=True)]
    unnamed x16 -> x14, local copies, waits for them, and re-layouts: 4.31 us -> 1.61 us
where the time goes in v5:
time: 207 us; the launch traced here: 206 us
  blocking collectives  131 us (63%)
  starting transfers between devices  33 us (16%)
  Pallas kernels  20.1 us (10%)
  waiting for transfers between devices  18.8 us (9%)
    all_to_all x5, blocking collectives, over_cuts(): return lax.all_to_all(pieces, CUTS, 0, 0, tiled=True)  73 us
    all_to_all x4, blocking collectives, over_chips(): return lax.all_to_all(blocks, CIRC[0], 0, 0, tiled=True)  58.3 us
    pallas_call x20, Pallas kernels, call(): pl.pallas_call(body, out_shape=outs, in_specs=places or [VMEM] * len(args...  20.1 us
    all_to_all x2, starting transfers between devices, over_circ(): return lax.all_to_all(blocks, CIRC, 0, 0, tiled=True)  12.9 us
    all_to_all x1, starting transfers between devices, over_cuts(): return lax.all_to_all(pieces, CUTS, 0, 0, tiled=True)  12.4 us
    ppermute x4, starting transfers between devices, other_core(): return lax.ppermute(blocks, CIRC[1], [(0, 1), (1, 0)])  7.68 us
    all_to_all x1, waiting for transfers between devices, over_cuts(): return lax.all_to_all(pieces, CUTS, 0, 0, tiled=True)  7.1 us
    ppermute x4, waiting for transfers between devices, other_core(): return lax.ppermute(blocks, CIRC[1], [(0, 1), (1, 0)])  6 us
  transfers between devices with their start and end apart: 7, of which 7 were waited for; matrix products, arithmetic and copies ran while one was open for 0% of the time, Pallas kernels for 6%

profile of v5, /device:TPU:8, one launch (start us, length us, event | category | flops | bytes accessed | tf_op | source)
XLA Modules:
  0.0 205.7 jit_solution(2898879324652589726)
XLA Ops:
  0.6 1.7 load.1
  2.3 0.0 copy-start.4
  2.3 12.4 %all-to-all-start = ((f32[64,4,128]{2,1,0:T(4,128)}), f32[64,4,128]{2,1,0:T(4,128)S(1)}, u32[]{:S(2)}, u32[]{:S(2)}) async-start(f32[64,4,128]{2,1,0:T(4,128)} %get-tuple-element.31), calls=%async_computation | async-start | bytes 262144 | tf_op jit(solution)/shard_map/all_to_all | solution.py:270
  14.7 0.0 copy-start.3
  14.7 0.0 copy-start.6
  14.7 3.3 %setup.1 = (bf16[1024,1024]{1,0:T(8,128)(2,1)}, bf16[1024,512]{1,0:T(8,128)(2,1)S(1)}) custom-call(bf16[1024,1024]{1,0:T(8,128)(2,1)} %bitcast.15, bf16[512,1024]{1,0:T(8,128)(2,1)} %bitcast.16), custom_call_target="tpu_custom_call" | custom-call | flops 33554432 | bytes 6291456 | tf_op jit(solution)/shard_map/setup/pallas_call | solution.py:32
  18.0 7.1 %all-to-all-done.terms_ref = f32[64,4,128]{2,1,0:T(4,128)S(1)} async-done(((f32[64,4,128]{2,1,0:T(4,128)}), f32[64,4,128]{2,1,0:T(4,128)S(1)}, u32[]{:S(2)}, u32[]{:S(2)}) %all-to-all-start) | async-done | bytes 131104 | tf_op jit(solution)/shard_map/all_to_all | solution.py:270
  25.1 0.1 chain.3.old_ref
  25.3 14.5 %all_to_all.60.pieces_ref = f32[64,2,128]{2,1,0:T(2,128)S(1)} all-to-all(f32[64,2,128]{2,1,0:T(2,128)S(1)} %chain.3.old_ref), channel_id=1, replica_groups=mesh['cuts_0'=4,'cuts_1'=2,'cuts_2'=8,'circ_0'=4,'circ_1'=2] {'cuts_0','..., dimensions={0} | all-to-all | bytes 131072 | tf_op jit(solution)/shard_map/all_to_all | solution.py:270
  39.8 0.9 start.2
  40.7 9.4 %all-to-all-start.2 = ((f32[8,16,128]{2,1,0:T(8,128)}), f32[8,16,128]{2,1,0:T(8,128)S(1)}, u32[]{:S(2)}, u32[]{:S(2)}) async-start(f32[8,16,128]{2,1,0:T(8,128)} %get-tuple-element.37), calls=%async_computation.2 | async-start | bytes 131072 | tf_op jit(solution)/shard_map/all_to_all | solution.py:274
  50.1 6.4 %free.2 = (f32[128,1024]{1,0:T(8,128)S(1)}, f32[128,512]{1,0:T(8,128)S(1)}, bf16[1024,1024]{1,0:T(8,128)(2,1)}, bf16[1024,512]{1,0:T(8,128)(2,1)S(1)}) custom-call(f32[16,1024]{1,0:T(8,128)S(1)} %get-tuple-element.38.start_ref, bf16[8,16,1024]{2,1,0:T(8,128)(2,1)S(1)} %bitcast.11, f32[1,1024]{1,0:T(1,128)S(1)} %bitcast.13, ...), custom_call_target="tpu_custom_call" | custom-call | flops 3623878656 | bytes 7409664 | tf_op jit(solution)/shard_map/free/pallas_call | solution.py:32
  56.5 1.9 all-to-all-done.2.f_ref
  58.3 0.4 couple.4
  58.7 1.9 collective-permute-start
  60.6 1.5 collective-permute-done.got_ref
  62.1 0.1 gather.4
  62.2 16.5 %all_to_all.61.f_ref = f32[4,128,128]{2,1,0:T(8,128)S(1)} all-to-all(f32[4,128,128]{2,1,0:T(8,128)S(1)} %gather.4), channel_id=1, replica_groups=mesh['cuts_0'=4,'cuts_1'=2,'cuts_2'=8,'circ_0'=4,'circ_1'=2] {'circ_0'}, dimensions={0} | all-to-all | bytes 524288 | tf_op jit(solution)/shard_map/all_to_all | solution.py:278
  78.7 0.4 couple.5
  79.0 1.9 collective-permute-start.1
  81.0 1.5 collective-permute-done.1.got_ref
  82.5 0.1 gather.5
  82.5 13.8 %all_to_all.62.f_ref = f32[4,128,128]{2,1,0:T(8,128)S(1)} all-to-all(f32[4,128,128]{2,1,0:T(8,128)S(1)} %gather.5), channel_id=1, replica_groups=mesh['cuts_0'=4,'cuts_1'=2,'cuts_2'=8,'circ_0'=4,'circ_1'=2] {'circ_0'}, dimensions={0} | all-to-all | bytes 524288 | tf_op jit(solution)/shard_map/all_to_all | solution.py:278
  96.4 0.4 last.1
  96.7 14.8 %all_to_all.63.last_ref = f32[64,2,128]{2,1,0:T(2,128)S(1)} all-to-all(f32[64,2,128]{2,1,0:T(2,128)S(1)} %last.1), channel_id=1, replica_groups=mesh['cuts_0'=4,'cuts_1'=2,'cuts_2'=8,'circ_0'=4,'circ_1'=2] {'cuts_0','..., dimensions={0} | all-to-all | bytes 131072 | tf_op jit(solution)/shard_map/all_to_all | solution.py:270
  111.5 0.1 chain.4.old_ref
  111.7 14.5 %all_to_all.64.pieces_ref = f32[64,2,128]{2,1,0:T(2,128)S(1)} all-to-all(f32[64,2,128]{2,1,0:T(2,128)S(1)} %chain.4.old_ref), channel_id=1, replica_groups=mesh['cuts_0'=4,'cuts_1'=2,'cuts_2'=8,'circ_0'=4,'circ_1'=2] {'cuts_0','..., dimensions={0} | all-to-all | bytes 131072 | tf_op jit(solution)/shard_map/all_to_all | solution.py:270
  126.1 0.9 start.3
  127.0 3.5 %all-to-all-start.7 = ((f32[8,16,128]{2,1,0:T(8,128)}), f32[8,16,128]{2,1,0:T(8,128)S(1)}, u32[]{:S(2)}, u32[]{:S(2)}) async-start(f32[8,16,128]{2,1,0:T(8,128)} %get-tuple-element.48), calls=%async_computation.7 | async-start | bytes 131072 | tf_op jit(solution)/shard_map/all_to_all | solution.py:274
  130.6 1.6 copy-done.2
  132.2 2.6 %free.3 = (f32[128,1024]{1,0:T(8,128)S(1)}, f32[128,512]{1,0:T(8,128)S(1)}) custom-call(f32[16,1024]{1,0:T(8,128)S(1)} %get-tuple-element.49.start_ref, bf16[8,16,1024]{2,1,0:T(8,128)(2,1)S(1)} %bitcast.12, f32[1,1024]{1,0:T(1,128)S(1)} %bitcast.14, bf16[1024,1024]{1,0:T(8,128)(2,1)S(1)} %copy-done.2, bf16[1024,512]{1,0:T(8,128)(2,1)S(1)} %get-tuple-element.36.ct_ref), custom_call_target="tpu_custom_call" | custom-call | flops 402653184 | bytes 4263936 | tf_op jit(solution)/shard_map/free/pallas_call | solution.py:32
  134.8 3.8 %all-to-all-done.7.f_ref = f32[8,16,128]{2,1,0:T(8,128)S(1)} async-done(((f32[8,16,128]{2,1,0:T(8,128)}), f32[8,16,128]{2,1,0:T(8,128)S(1)}, u32[]{:S(2)}, u32[]{:S(2)}) %all-to-all-start.7) | async-done | bytes 65568 | tf_op jit(solution)/shard_map/all_to_all | solution.py:274
  138.6 0.4 couple.6
  139.0 1.9 collective-permute-start.2
  140.9 1.5 collective-permute-done.2.got_ref
  142.4 0.1 gather.6
  142.5 14.2 %all_to_all.65.f_ref = f32[4,128,128]{2,1,0:T(8,128)S(1)} all-to-all(f32[4,128,128]{2,1,0:T(8,128)S(1)} %gather.6), channel_id=1, replica_groups=mesh['cuts_0'=4,'cuts_1'=2,'cuts_2'=8,'circ_0'=4,'circ_1'=2] {'circ_0'}, dimensions={0} | all-to-all | bytes 524288 | tf_op jit(solution)/shard_map/all_to_all | solution.py:278
  156.7 0.4 couple.7
  157.1 1.9 collective-permute-start.3
  159.0 1.5 collective-permute-done.3.got_ref
  160.5 0.1 gather.7
  160.6 13.8 %all_to_all.66.f_ref = f32[4,128,128]{2,1,0:T(8,128)S(1)} all-to-all(f32[4,128,128]{2,1,0:T(8,128)S(1)} %gather.7), channel_id=1, replica_groups=mesh['cuts_0'=4,'cuts_1'=2,'cuts_2'=8,'circ_0'=4,'circ_1'=2] {'circ_0'}, dimensions={0} | all-to-all | bytes 524288 | tf_op jit(solution)/shard_map/all_to_all | solution.py:278
  174.4 0.0 copy-done.1
  174.4 1.2 wave.1
  175.6 14.8 %all_to_all.67.last_ref = f32[64,2,128]{2,1,0:T(2,128)S(1)} all-to-all(f32[64,2,128]{2,1,0:T(2,128)S(1)} %get-tuple-element.56), channel_id=1, replica_groups=mesh['cuts_0'=4,'cuts_1'=2,'cuts_2'=8,'circ_0'=4,'circ_1'=2] {'cuts_0','..., dimensions={0} | all-to-all | bytes 131072 | tf_op jit(solution)/shard_map/all_to_all | solution.py:270
  190.4 0.1 chain.5
  190.5 14.5 %all_to_all.68.pieces_ref = f32[64,2,128]{2,1,0:T(2,128)S(1)} all-to-all(f32[64,2,128]{2,1,0:T(2,128)S(1)} %chain.5), channel_id=1, replica_groups=mesh['cuts_0'=4,'cuts_1'=2,'cuts_2'=8,'circ_0'=4,'circ_1'=2] {'cuts_0','..., dimensions={0} | all-to-all | bytes 131072 | tf_op jit(solution)/shard_map/all_to_all | solution.py:270
  205.0 0.7 unpack.1
  (9 shorter events, 0.0 us)
Async XLA Ops:
  2.3 22.8 %copy-start.5 = (f32[2,128]{1,0:T(2,128)S(1)}, f32[2,128]{1,0:T(2,128)}, u32[]{:S(2)}) copy-start(f32[2,128]{1,0:T(2,128)} %get-tuple-element.35.initial_ref) | copy-start | bytes 3076
  2.3 37.5 %copy-start.4 = (s32[12,128]{1,0:T(8,128)S(1)}, s32[12,128]{1,0:T(8,128)}, u32[]{:S(2)}) copy-start(s32[12,128]{1,0:T(8,128)} %get-tuple-element.30.target_ref) | copy-start | bytes 18436
  2.3 22.8 %all-to-all-start = ((f32[64,4,128]{2,1,0:T(4,128)}), f32[64,4,128]{2,1,0:T(4,128)S(1)}, u32[]{:S(2)}, u32[]{:S(2)}) async-start(f32[64,4,128]{2,1,0:T(4,128)} %get-tuple-element.31), calls=%async_computation | async-start | bytes 262144 | tf_op jit(solution)/shard_map/all_to_all | solution.py:270
  14.7 35.4 %copy-start.3 = (bf16[1,8,1,16,1024]{4,3,2,1,0:T(8,128)(2,1)S(1)}, bf16[1,8,1,16,1024]{4,3,2,1,0:T(8,128)(2,1)}, u32[]{:S(2)}) copy-start(bf16[1,8,1,16,1024]{4,3,2,1,0:T(8,128)(2,1)} %param.7) | copy-start | bytes 786436
  14.7 35.4 %copy-start.6 = (f32[1,1,1024]{2,1,0:T(1,128)S(1)}, f32[1,1,1024]{2,1,0:T(1,128)}, u32[]{:S(2)}) copy-start(f32[1,1,1024]{2,1,0:T(1,128)} %param.9) | copy-start | bytes 12292
  40.7 17.7 %all-to-all-start.2 = ((f32[8,16,128]{2,1,0:T(8,128)}), f32[8,16,128]{2,1,0:T(8,128)S(1)}, u32[]{:S(2)}, u32[]{:S(2)}) async-start(f32[8,16,128]{2,1,0:T(8,128)} %get-tuple-element.37), calls=%async_computation.2 | async-start | bytes 131072 | tf_op jit(solution)/shard_map/all_to_all | solution.py:274
  58.7 3.4 %collective-permute-start = (f32[4,128,128]{2,1,0:T(8,128)S(1)}, f32[4,128,128]{2,1,0:T(8,128)S(1)}, u32[]{:S(2)}, u32[]{:S(2)}) collective-permute-start(f32[4,128,128]{2,1,0:T(8,128)S(1)} %get-tuple-element.43), channel_id=1, source_target_pairs={{0,1},{1,0},{2,3},{3,2},{4,5},{5,4},{6,7},{7,6},{8,9},{9,8},{10,11... | collective-permute-start | bytes 786440 | tf_op jit(solution)/shard_map/ppermute | solution.py:282
  62.1 34.2 %copy-start = (bf16[1024,1024]{1,0:T(8,128)(2,1)S(1)}, bf16[1024,1024]{1,0:T(8,128)(2,1)}, u32[]{:S(2)}) copy-start(bf16[1024,1024]{1,0:T(8,128)(2,1)} %get-tuple-element.47.h_ref) | copy-start | bytes 6291460
  79.0 3.4 %collective-permute-start.1 = (f32[4,128,128]{2,1,0:T(8,128)S(1)}, f32[4,128,128]{2,1,0:T(8,128)S(1)}, u32[]{:S(2)}, u32[]{:S(2)}) collective-permute-start(f32[4,128,128]{2,1,0:T(8,128)S(1)} %get-tuple-element.45), channel_id=1, source_target_pairs={{0,1},{1,0},{2,3},{3,2},{4,5},{5,4},{6,7},{7,6},{8,9},{9,8},{10,11... | collective-permute-start | bytes 786440 | tf_op jit(solution)/shard_map/ppermute | solution.py:282
  127.0 11.6 %all-to-all-start.7 = ((f32[8,16,128]{2,1,0:T(8,128)}), f32[8,16,128]{2,1,0:T(8,128)S(1)}, u32[]{:S(2)}, u32[]{:S(2)}) async-start(f32[8,16,128]{2,1,0:T(8,128)} %get-tuple-element.48), calls=%async_computation.7 | async-start | bytes 131072 | tf_op jit(solution)/shard_map/all_to_all | solution.py:274
  130.6 1.6 copy-start.2
  139.0 3.4 %collective-permute-start.2 = (f32[4,128,128]{2,1,0:T(8,128)S(1)}, f32[4,128,128]{2,1,0:T(8,128)S(1)}, u32[]{:S(2)}, u32[]{:S(2)}) collective-permute-start(f32[4,128,128]{2,1,0:T(8,128)S(1)} %get-tuple-element.52), channel_id=1, source_target_pairs={{0,1},{1,0},{2,3},{3,2},{4,5},{5,4},{6,7},{7,6},{8,9},{9,8},{10,11... | collective-permute-start | bytes 786440 | tf_op jit(solution)/shard_map/ppermute | solution.py:282
  142.4 32.0 %copy-start.1 = (bf16[1024,1024]{1,0:T(8,128)(2,1)S(1)}, bf16[1024,1024]{1,0:T(8,128)(2,1)}, u32[]{:S(2)}) copy-start(bf16[1024,1024]{1,0:T(8,128)(2,1)} %get-tuple-element.47.h_ref) | copy-start | bytes 6291460
  157.1 3.4 %collective-permute-start.3 = (f32[4,128,128]{2,1,0:T(8,128)S(1)}, f32[4,128,128]{2,1,0:T(8,128)S(1)}, u32[]{:S(2)}, u32[]{:S(2)}) collective-permute-start(f32[4,128,128]{2,1,0:T(8,128)S(1)} %get-tuple-element.54), channel_id=1, source_target_pairs={{0,1},{1,0},{2,3},{3,2},{4,5},{5,4},{6,7},{7,6},{8,9},{9,8},{10,11... | collective-permute-start | bytes 786440 | tf_op jit(solution)/shard_map/ppermute | solution.py:282

commit v6 on v5

--- a/solution.py
+++ b/solution.py
@@ -45,10 +45,12 @@
     return jnp.dot(a, b, preferred_element_type=F32)
 
 
-def pack(state, out_ref):
-    for b in range(64):
+def pack(state, out_ref, first=0):
+    for b in range(state.shape[1] // LANES * 8):
         block, pair = divmod(b, 8)
-        out_ref[b, 0:2, :] = state[2 * pair : 2 * pair + 2, block * LANES : (block + 1) * LANES]
+        out_ref[first * 8 + b, 0:2, :] = state[
+            2 * pair : 2 * pair + 2, block * LANES : (block + 1) * LANES
+        ]
 
 
 def unpack(pieces_ref, state_ref):
@@ -187,23 +189,32 @@
     both_ref,
     sems,
 ):
+    part = bt_ref.shape[0] // PARTS
+    rows = [slice(k * part, (k + 1) * part) for k in range(PARTS)]
     copies = [
-        pltpu.make_async_copy(given, taken, sems.at[k])
-        for k, (given, taken) in enumerate(
-            ((m_hbm, m_ref), (sources_hbm, sources_ref), (bt_hbm, bt_ref))
-        )
-    ]
-    for copy in copies:
+        pltpu.make_async_copy(given, taken, sems.at[1 + k])
+        for k, (given, taken) in enumerate(((m_hbm, m_ref), (sources_hbm, sources_ref)))
+    ]
+    parts = [
+        pltpu.make_async_copy(bt_hbm.at[r], bt_ref.at[r], sems.at[3 + k])
+        for k, r in enumerate(rows)
+    ]
+    for copy in copies + parts:
         copy.start()
     for copy in copies:
         copy.wait()
     previous = start_ref[...]
-    h_ref[0:PORTS, :] = bt_ref[0:PORTS, :]
-    response = bt_ref[0:PORTS, :].astype(F32)
     for t in range(STEPS):
         drive = m_ref[...] * previous + sources_ref[t].astype(F32)
         if t == 0:
-            previous = dot(drive.astype(BF16), bt_ref[...])
+            drive = drive.astype(BF16)
+            previous = jnp.zeros_like(previous)
+            for r, copy in zip(rows, parts):
+                copy.wait()
+                previous = previous + dot(drive[:, r], bt_ref[r, :])
+            response = bt_ref[0:PORTS, :]
+            h_ref[0:PORTS, :] = response
+            response = response.astype(F32)
         else:
             both_ref[0:SCEN, :] = drive.astype(BF16)
             both_ref[SCEN:, :] = (m_ref[...] * response).astype(BF16)
@@ -212,7 +223,7 @@
             h_ref[t * PORTS : (t + 1) * PORTS, :] = response.astype(BF16)
         z_ref[t * SCEN : (t + 1) * SCEN, :] = previous
         low_ref[t * SCEN : (t + 1) * SCEN, :] = previous.astype(BF16)
-    kept = pltpu.make_async_copy(h_ref, h_hbm, sems.at[3])
+    kept = pltpu.make_async_copy(h_ref, h_hbm, sems.at[0])
     kept.start()
     cz_ref[...] = dot(low_ref[...], ct_ref[...])
     ch_ref[...] = dot(h_ref[...], ct_ref[...]).astype(BF16)
@@ -255,11 +266,21 @@
     pack(z_ref[(STEPS - 1) * SCEN :, :] + dot(x_ref[...], h_ref[...]), out_ref)
 
 
-def wave_body(f_ref, z_ref, h_ref, out_ref, wave_ref, x_ref):
+def wave_body(f_ref, z_ref, h_ref, out_ref, wave_hbm, wave_ref, x_ref, sems):
     delays(jnp.sum(f_ref[...], axis=0).astype(BF16), x_ref)
-    wave = z_ref[...] + dot(x_ref[...], h_ref[...])
-    wave_ref[...] = wave.astype(BF16)
-    pack(wave[(STEPS - 1) * SCEN :, :], out_ref)
+    part = wave_ref.shape[1] // PARTS
+    copies = []
+    for k in range(PARTS):
+        columns = slice(k * part, (k + 1) * part)
+        wave = z_ref[:, columns] + dot(x_ref[...], h_ref[:, columns])
+        wave_ref[:, columns] = wave.astype(BF16)
+        copies.append(
+            pltpu.make_async_copy(wave_ref.at[:, columns], wave_hbm.at[:, columns], sems.at[k])
+        )
+        copies[-1].start()
+        pack(wave[(STEPS - 1) * SCEN :, :], out_ref, k * part // LANES)
+    for copy in copies:
+        copy.wait()
 
 
 def unpack_body(pieces_ref, state_ref):
@@ -363,7 +384,7 @@
                     pltpu.VMEM((STEPS * PORTS, nodes), BF16),
                     low,
                     pltpu.VMEM((SCEN + PORTS, nodes), BF16),
-                    pltpu.SemaphoreType.DMA((4,)),
+                    pltpu.SemaphoreType.DMA((3 + PARTS,)),
                 ],
                 places=[VMEM, HBM, HBM, HBM, VMEM],
                 grant=50,
@@ -404,7 +425,12 @@
                 (inflow, z, h),
                 "wave",
                 flops=2 * rows * nodes * nodes,
-                scratch=delayed,
+                scratch=[
+                    pltpu.VMEM((rows, nodes), BF16),
+                    *delayed,
+                    pltpu.SemaphoreType.DMA((PARTS,)),
+                ],
+                out_places=[VMEM, HBM],
             )
         (starts,) = call(
             chain_body,

time: 207 us -> 206 us (level)
  no operation moved by 1% of the time
where the time goes in v6:
time: 206 us; the launch traced here: 205 us
  blocking collectives  130 us (63%)
  starting transfers between devices  33 us (16%)
  waiting for transfers between devices  19.8 us (10%)
  Pallas kernels  19.1 us (9%)
    all_to_all x5, blocking collectives, over_cuts(): return lax.all_to_all(pieces, CUTS, 0, 0, tiled=True)  72.9 us
    all_to_all x4, blocking collectives, over_chips(): return lax.all_to_all(blocks, CIRC[0], 0, 0, tiled=True)  57.3 us
    pallas_call x20, Pallas kernels, call(): pl.pallas_call(body, out_shape=outs, in_specs=places or [VMEM] * len(args...  19.1 us
    all_to_all x2, starting transfers between devices, over_circ(): return lax.all_to_all(blocks, CIRC, 0, 0, tiled=True)  12.9 us
    all_to_all x1, starting transfers between devices, over_cuts(): return lax.all_to_all(pieces, CUTS, 0, 0, tiled=True)  12.4 us
    ppermute x4, starting transfers between devices, other_core(): return lax.ppermute(blocks, CIRC[1], [(0, 1), (1, 0)])  7.68 us
    all_to_all x1, waiting for transfers between devices, over_cuts(): return lax.all_to_all(pieces, CUTS, 0, 0, tiled=True)  7.1 us
    all_to_all x2, waiting for transfers between devices, over_circ(): return lax.all_to_all(blocks, CIRC, 0, 0, tiled=True)  6.67 us
  transfers between devices with their start and end apart: 7, of which 7 were waited for; matrix products, arithmetic and copies ran while one was open for 0% of the time, Pallas kernels for 6%

profile of v6, /device:TPU:8, one launch (start us, length us, event | category | flops | bytes accessed | tf_op | source)
XLA Modules:
  0.0 204.6 jit_solution(7608045718873434172)
XLA Ops:
  0.6 1.7 load.1
  2.3 0.0 copy-start.4
  2.3 12.4 %all-to-all-start = ((f32[64,4,128]{2,1,0:T(4,128)}), f32[64,4,128]{2,1,0:T(4,128)S(1)}, u32[]{:S(2)}, u32[]{:S(2)}) async-start(f32[64,4,128]{2,1,0:T(4,128)} %get-tuple-element.31), calls=%async_computation | async-start | bytes 262144 | tf_op jit(solution)/shard_map/all_to_all | solution.py:291
  14.7 0.0 copy-start.3
  14.7 0.0 copy-start.6
  14.7 3.3 %setup.1 = (bf16[1024,1024]{1,0:T(8,128)(2,1)}, bf16[1024,512]{1,0:T(8,128)(2,1)S(1)}) custom-call(bf16[1024,1024]{1,0:T(8,128)(2,1)} %bitcast.15, bf16[512,1024]{1,0:T(8,128)(2,1)} %bitcast.16), custom_call_target="tpu_custom_call" | custom-call | flops 33554432 | bytes 6291456 | tf_op jit(solution)/shard_map/setup/pallas_call | solution.py:32
  18.0 7.1 %all-to-all-done.terms_ref = f32[64,4,128]{2,1,0:T(4,128)S(1)} async-done(((f32[64,4,128]{2,1,0:T(4,128)}), f32[64,4,128]{2,1,0:T(4,128)S(1)}, u32[]{:S(2)}, u32[]{:S(2)}) %all-to-all-start) | async-done | bytes 131104 | tf_op jit(solution)/shard_map/all_to_all | solution.py:291
  25.1 0.0 copy-done.5
  25.1 0.1 chain.3.old_ref
  25.3 14.5 %all_to_all.60.pieces_ref = f32[64,2,128]{2,1,0:T(2,128)S(1)} all-to-all(f32[64,2,128]{2,1,0:T(2,128)S(1)} %chain.3.old_ref), channel_id=1, replica_groups=mesh['cuts_0'=4,'cuts_1'=2,'cuts_2'=8,'circ_0'=4,'circ_1'=2] {'cuts_0','..., dimensions={0} | all-to-all | bytes 131072 | tf_op jit(solution)/shard_map/all_to_all | solution.py:291
  39.8 0.9 start.2
  40.7 9.4 %all-to-all-start.2 = ((f32[8,16,128]{2,1,0:T(8,128)}), f32[8,16,128]{2,1,0:T(8,128)S(1)}, u32[]{:S(2)}, u32[]{:S(2)}) async-start(f32[8,16,128]{2,1,0:T(8,128)} %get-tuple-element.37), calls=%async_computation.2 | async-start | bytes 131072 | tf_op jit(solution)/shard_map/all_to_all | solution.py:295
  50.1 5.4 %free.2 = (f32[128,1024]{1,0:T(8,128)S(1)}, f32[128,512]{1,0:T(8,128)S(1)}, bf16[1024,1024]{1,0:T(8,128)(2,1)}, bf16[1024,512]{1,0:T(8,128)(2,1)S(1)}) custom-call(f32[16,1024]{1,0:T(8,128)S(1)} %get-tuple-element.38.start_ref, bf16[8,16,1024]{2,1,0:T(8,128)(2,1)S(1)} %bitcast.11, f32[1,1024]{1,0:T(1,128)S(1)} %bitcast.13, ...), custom_call_target="tpu_custom_call" | custom-call | flops 3623878656 | bytes 7409664 | tf_op jit(solution)/shard_map/free/pallas_call | solution.py:32
  55.5 2.8 %all-to-all-done.2.f_ref = f32[8,16,128]{2,1,0:T(8,128)S(1)} async-done(((f32[8,16,128]{2,1,0:T(8,128)}), f32[8,16,128]{2,1,0:T(8,128)S(1)}, u32[]{:S(2)}, u32[]{:S(2)}) %all-to-all-start.2) | async-done | bytes 65568 | tf_op jit(solution)/shard_map/all_to_all | solution.py:295
  58.3 0.4 couple.4
  58.7 1.9 collective-permute-start
  60.6 1.5 collective-permute-done.got_ref
  62.1 0.1 gather.4
  62.2 15.5 %all_to_all.61.f_ref = f32[4,128,128]{2,1,0:T(8,128)S(1)} all-to-all(f32[4,128,128]{2,1,0:T(8,128)S(1)} %gather.4), channel_id=1, replica_groups=mesh['cuts_0'=4,'cuts_1'=2,'cuts_2'=8,'circ_0'=4,'circ_1'=2] {'circ_0'}, dimensions={0} | all-to-all | bytes 524288 | tf_op jit(solution)/shard_map/all_to_all | solution.py:299
  77.7 0.4 couple.5
  78.1 1.9 collective-permute-start.1
  80.0 1.5 collective-permute-done.1.got_ref
  81.5 0.1 gather.5
  81.6 13.8 %all_to_all.62.f_ref = f32[4,128,128]{2,1,0:T(8,128)S(1)} all-to-all(f32[4,128,128]{2,1,0:T(8,128)S(1)} %gather.5), channel_id=1, replica_groups=mesh['cuts_0'=4,'cuts_1'=2,'cuts_2'=8,'circ_0'=4,'circ_1'=2] {'circ_0'}, dimensions={0} | all-to-all | bytes 524288 | tf_op jit(solution)/shard_map/all_to_all | solution.py:299
  95.4 0.4 last.1
  95.8 14.8 %all_to_all.63.last_ref = f32[64,2,128]{2,1,0:T(2,128)S(1)} all-to-all(f32[64,2,128]{2,1,0:T(2,128)S(1)} %last.1), channel_id=1, replica_groups=mesh['cuts_0'=4,'cuts_1'=2,'cuts_2'=8,'circ_0'=4,'circ_1'=2] {'cuts_0','..., dimensions={0} | all-to-all | bytes 131072 | tf_op jit(solution)/shard_map/all_to_all | solution.py:291
  110.5 0.1 chain.4.old_ref
  110.7 14.5 %all_to_all.64.pieces_ref = f32[64,2,128]{2,1,0:T(2,128)S(1)} all-to-all(f32[64,2,128]{2,1,0:T(2,128)S(1)} %chain.4.old_ref), channel_id=1, replica_groups=mesh['cuts_0'=4,'cuts_1'=2,'cuts_2'=8,'circ_0'=4,'circ_1'=2] {'cuts_0','..., dimensions={0} | all-to-all | bytes 131072 | tf_op jit(solution)/shard_map/all_to_all | solution.py:291
  125.1 0.9 start.3
  126.0 3.5 %all-to-all-start.7 = ((f32[8,16,128]{2,1,0:T(8,128)}), f32[8,16,128]{2,1,0:T(8,128)S(1)}, u32[]{:S(2)}, u32[]{:S(2)}) async-start(f32[8,16,128]{2,1,0:T(8,128)} %get-tuple-element.48), calls=%async_computation.7 | async-start | bytes 131072 | tf_op jit(solution)/shard_map/all_to_all | solution.py:295
  129.6 1.6 copy-done.2
  131.2 2.6 %free.3 = (f32[128,1024]{1,0:T(8,128)S(1)}, f32[128,512]{1,0:T(8,128)S(1)}) custom-call(f32[16,1024]{1,0:T(8,128)S(1)} %get-tuple-element.49.start_ref, bf16[8,16,1024]{2,1,0:T(8,128)(2,1)S(1)} %bitcast.12, f32[1,1024]{1,0:T(1,128)S(1)} %bitcast.14, bf16[1024,1024]{1,0:T(8,128)(2,1)S(1)} %copy-done.2, bf16[1024,512]{1,0:T(8,128)(2,1)S(1)} %get-tuple-element.36.ct_ref), custom_call_target="tpu_custom_call" | custom-call | flops 402653184 | bytes 4263936 | tf_op jit(solution)/shard_map/free/pallas_call | solution.py:32
  133.8 3.8 %all-to-all-done.7.f_ref = f32[8,16,128]{2,1,0:T(8,128)S(1)} async-done(((f32[8,16,128]{2,1,0:T(8,128)}), f32[8,16,128]{2,1,0:T(8,128)S(1)}, u32[]{:S(2)}, u32[]{:S(2)}) %all-to-all-start.7) | async-done | bytes 65568 | tf_op jit(solution)/shard_map/all_to_all | solution.py:295
  137.6 0.4 couple.6
  138.0 1.9 collective-permute-start.2
  139.9 1.5 collective-permute-done.2.got_ref
  141.4 0.1 gather.6
  141.5 14.2 %all_to_all.65.f_ref = f32[4,128,128]{2,1,0:T(8,128)S(1)} all-to-all(f32[4,128,128]{2,1,0:T(8,128)S(1)} %gather.6), channel_id=1, replica_groups=mesh['cuts_0'=4,'cuts_1'=2,'cuts_2'=8,'circ_0'=4,'circ_1'=2] {'circ_0'}, dimensions={0} | all-to-all | bytes 524288 | tf_op jit(solution)/shard_map/all_to_all | solution.py:299
  155.7 0.4 couple.7
  156.1 1.9 collective-permute-start.3
  158.0 1.5 collective-permute-done.3.got_ref
  159.5 0.1 gather.7
  159.6 13.8 %all_to_all.66.f_ref = f32[4,128,128]{2,1,0:T(8,128)S(1)} all-to-all(f32[4,128,128]{2,1,0:T(8,128)S(1)} %gather.7), channel_id=1, replica_groups=mesh['cuts_0'=4,'cuts_1'=2,'cuts_2'=8,'circ_0'=4,'circ_1'=2] {'circ_0'}, dimensions={0} | all-to-all | bytes 524288 | tf_op jit(solution)/shard_map/all_to_all | solution.py:299
  173.4 1.2 wave.1
  174.6 14.8 %all_to_all.67.last_ref = f32[64,2,128]{2,1,0:T(2,128)S(1)} all-to-all(f32[64,2,128]{2,1,0:T(2,128)S(1)} %get-tuple-element.56), channel_id=1, replica_groups=mesh['cuts_0'=4,'cuts_1'=2,'cuts_2'=8,'circ_0'=4,'circ_1'=2] {'cuts_0','..., dimensions={0} | all-to-all | bytes 131072 | tf_op jit(solution)/shard_map/all_to_all | solution.py:291
  189.3 0.1 chain.5
  189.5 14.5 %all_to_all.68.pieces_ref = f32[64,2,128]{2,1,0:T(2,128)S(1)} all-to-all(f32[64,2,128]{2,1,0:T(2,128)S(1)} %chain.5), channel_id=1, replica_groups=mesh['cuts_0'=4,'cuts_1'=2,'cuts_2'=8,'circ_0'=4,'circ_1'=2] {'cuts_0','..., dimensions={0} | all-to-all | bytes 131072 | tf_op jit(solution)/shard_map/all_to_all | solution.py:291
  203.9 0.7 unpack.1
  (9 shorter events, 0.0 us)
Async XLA Ops:
  2.3 22.8 %copy-start.5 = (f32[2,128]{1,0:T(2,128)S(1)}, f32[2,128]{1,0:T(2,128)}, u32[]{:S(2)}) copy-start(f32[2,128]{1,0:T(2,128)} %get-tuple-element.35.initial_ref) | copy-start | bytes 3076
  2.3 37.5 %copy-start.4 = (s32[12,128]{1,0:T(8,128)S(1)}, s32[12,128]{1,0:T(8,128)}, u32[]{:S(2)}) copy-start(s32[12,128]{1,0:T(8,128)} %get-tuple-element.30.target_ref) | copy-start | bytes 18436
  2.3 22.8 %all-to-all-start = ((f32[64,4,128]{2,1,0:T(4,128)}), f32[64,4,128]{2,1,0:T(4,128)S(1)}, u32[]{:S(2)}, u32[]{:S(2)}) async-start(f32[64,4,128]{2,1,0:T(4,128)} %get-tuple-element.31), calls=%async_computation | async-start | bytes 262144 | tf_op jit(solution)/shard_map/all_to_all | solution.py:291
  14.7 35.4 %copy-start.3 = (bf16[1,8,1,16,1024]{4,3,2,1,0:T(8,128)(2,1)S(1)}, bf16[1,8,1,16,1024]{4,3,2,1,0:T(8,128)(2,1)}, u32[]{:S(2)}) copy-start(bf16[1,8,1,16,1024]{4,3,2,1,0:T(8,128)(2,1)} %param.7) | copy-start | bytes 786436
  14.7 35.4 %copy-start.6 = (f32[1,1,1024]{2,1,0:T(1,128)S(1)}, f32[1,1,1024]{2,1,0:T(1,128)}, u32[]{:S(2)}) copy-start(f32[1,1,1024]{2,1,0:T(1,128)} %param.9) | copy-start | bytes 12292
  40.7 17.7 %all-to-all-start.2 = ((f32[8,16,128]{2,1,0:T(8,128)}), f32[8,16,128]{2,1,0:T(8,128)S(1)}, u32[]{:S(2)}, u32[]{:S(2)}) async-start(f32[8,16,128]{2,1,0:T(8,128)} %get-tuple-element.37), calls=%async_computation.2 | async-start | bytes 131072 | tf_op jit(solution)/shard_map/all_to_all | solution.py:295
  58.7 3.4 %collective-permute-start = (f32[4,128,128]{2,1,0:T(8,128)S(1)}, f32[4,128,128]{2,1,0:T(8,128)S(1)}, u32[]{:S(2)}, u32[]{:S(2)}) collective-permute-start(f32[4,128,128]{2,1,0:T(8,128)S(1)} %get-tuple-element.43), channel_id=1, source_target_pairs={{0,1},{1,0},{2,3},{3,2},{4,5},{5,4},{6,7},{7,6},{8,9},{9,8},{10,11... | collective-permute-start | bytes 786440 | tf_op jit(solution)/shard_map/ppermute | solution.py:303
  62.1 33.3 %copy-start = (bf16[1024,1024]{1,0:T(8,128)(2,1)S(1)}, bf16[1024,1024]{1,0:T(8,128)(2,1)}, u32[]{:S(2)}) copy-start(bf16[1024,1024]{1,0:T(8,128)(2,1)} %get-tuple-element.47.h_ref) | copy-start | bytes 6291460
  78.1 3.4 %collective-permute-start.1 = (f32[4,128,128]{2,1,0:T(8,128)S(1)}, f32[4,128,128]{2,1,0:T(8,128)S(1)}, u32[]{:S(2)}, u32[]{:S(2)}) collective-permute-start(f32[4,128,128]{2,1,0:T(8,128)S(1)} %get-tuple-element.45), channel_id=1, source_target_pairs={{0,1},{1,0},{2,3},{3,2},{4,5},{5,4},{6,7},{7,6},{8,9},{9,8},{10,11... | collective-permute-start | bytes 786440 | tf_op jit(solution)/shard_map/ppermute | solution.py:303
  126.0 11.6 %all-to-all-start.7 = ((f32[8,16,128]{2,1,0:T(8,128)}), f32[8,16,128]{2,1,0:T(8,128)S(1)}, u32[]{:S(2)}, u32[]{:S(2)}) async-start(f32[8,16,128]{2,1,0:T(8,128)} %get-tuple-element.48), calls=%async_computation.7 | async-start | bytes 131072 | tf_op jit(solution)/shard_map/all_to_all | solution.py:295
  129.6 1.6 copy-start.2
  138.0 3.4 %collective-permute-start.2 = (f32[4,128,128]{2,1,0:T(8,128)S(1)}, f32[4,128,128]{2,1,0:T(8,128)S(1)}, u32[]{:S(2)}, u32[]{:S(2)}) collective-permute-start(f32[4,128,128]{2,1,0:T(8,128)S(1)} %get-tuple-element.52), channel_id=1, source_target_pairs={{0,1},{1,0},{2,3},{3,2},{4,5},{5,4},{6,7},{7,6},{8,9},{9,8},{10,11... | collective-permute-start | bytes 786440 | tf_op jit(solution)/shard_map/ppermute | solution.py:303
  141.4 32.0 %copy-start.1 = (bf16[1024,1024]{1,0:T(8,128)(2,1)S(1)}, bf16[1024,1024]{1,0:T(8,128)(2,1)}, u32[]{:S(2)}) copy-start(bf16[1024,1024]{1,0:T(8,128)(2,1)} %get-tuple-element.47.h_ref) | copy-start | bytes 6291460
  156.1 3.4 %collective-permute-start.3 = (f32[4,128,128]{2,1,0:T(8,128)S(1)}, f32[4,128,128]{2,1,0:T(8,128)S(1)}, u32[]{:S(2)}, u32[]{:S(2)}) collective-permute-start(f32[4,128,128]{2,1,0:T(8,128)S(1)} %get-tuple-element.54), channel_id=1, source_target_pairs={{0,1},{1,0},{2,3},{3,2},{4,5},{5,4},{6,7},{7,6},{8,9},{9,8},{10,11... | collective-permute-start | bytes 786440 | tf_op jit(solution)/shard_map/ppermute | solution.py:303

commit v7 on v6

--- a/solution.py
+++ b/solution.py
@@ -266,25 +266,18 @@
     pack(z_ref[(STEPS - 1) * SCEN :, :] + dot(x_ref[...], h_ref[...]), out_ref)
 
 
-def wave_body(f_ref, z_ref, h_ref, out_ref, wave_hbm, wave_ref, x_ref, sems):
+def wave_body(f_ref, z_ref, h_ref, out_ref, wave_ref, x_ref):
     delays(jnp.sum(f_ref[...], axis=0).astype(BF16), x_ref)
-    part = wave_ref.shape[1] // PARTS
-    copies = []
-    for k in range(PARTS):
-        columns = slice(k * part, (k + 1) * part)
-        wave = z_ref[:, columns] + dot(x_ref[...], h_ref[:, columns])
-        wave_ref[:, columns] = wave.astype(BF16)
-        copies.append(
-            pltpu.make_async_copy(wave_ref.at[:, columns], wave_hbm.at[:, columns], sems.at[k])
-        )
-        copies[-1].start()
-        pack(wave[(STEPS - 1) * SCEN :, :], out_ref, k * part // LANES)
-    for copy in copies:
-        copy.wait()
-
-
-def unpack_body(pieces_ref, state_ref):
+    wave = z_ref[...] + dot(x_ref[...], h_ref[...])
+    wave_ref[...] = wave.astype(BF16)
+    pack(wave[(STEPS - 1) * SCEN :, :], out_ref)
+
+
+def finish_body(pieces_ref, wave_ref, state_ref, out_hbm, sem):
+    copy = pltpu.make_async_copy(wave_ref, out_hbm, sem)
+    copy.start()
     unpack(pieces_ref, state_ref)
+    copy.wait()
 
 
 def over_cuts(pieces):
@@ -425,12 +418,7 @@
                 (inflow, z, h),
                 "wave",
                 flops=2 * rows * nodes * nodes,
-                scratch=[
-                    pltpu.VMEM((rows, nodes), BF16),
-                    *delayed,
-                    pltpu.SemaphoreType.DMA((PARTS,)),
-                ],
-                out_places=[VMEM, HBM],
+                scratch=delayed,
             )
         (starts,) = call(
             chain_body,
@@ -439,7 +427,14 @@
             "chain",
         )
         pieces = over_cuts(starts)
-    (start,) = call(unpack_body, [shape((SCEN, nodes))], (pieces,), "unpack")
+    start, wave = call(
+        finish_body,
+        [shape((SCEN, nodes)), shape((rows, nodes), BF16)],
+        (pieces, wave),
+        "finish",
+        scratch=[pltpu.SemaphoreType.DMA],
+        out_places=[VMEM, HBM],
+    )
     return start.reshape(1, 1, SCEN, nodes), wave.reshape(1, STEPS, 1, SCEN, nodes)
 
 

time: 206 us -> 206 us (level)
  no operation moved by 1% of the time
where the time goes in v7:
time: 206 us; the launch traced here: 205 us
  blocking collectives  130 us (63%)
  starting transfers between devices  33 us (16%)
  waiting for transfers between devices  19.7 us (10%)
  Pallas kernels  19.1 us (9%)
    all_to_all x5, blocking collectives, over_cuts(): return lax.all_to_all(pieces, CUTS, 0, 0, tiled=True)  72.9 us
    all_to_all x4, blocking collectives, over_chips(): return lax.all_to_all(blocks, CIRC[0], 0, 0, tiled=True)  57.3 us
    pallas_call x20, Pallas kernels, call(): pl.pallas_call(body, out_shape=outs, in_specs=places or [VMEM] * len(args...  19.1 us
    all_to_all x2, starting transfers between devices, over_circ(): return lax.all_to_all(blocks, CIRC, 0, 0, tiled=True)  12.9 us
    all_to_all x1, starting transfers between devices, over_cuts(): return lax.all_to_all(pieces, CUTS, 0, 0, tiled=True)  12.4 us
    ppermute x4, starting transfers between devices, other_core(): return lax.ppermute(blocks, CIRC[1], [(0, 1), (1, 0)])  7.68 us
    all_to_all x1, waiting for transfers between devices, over_cuts(): return lax.all_to_all(pieces, CUTS, 0, 0, tiled=True)  7.08 us
    all_to_all x2, waiting for transfers between devices, over_circ(): return lax.all_to_all(blocks, CIRC, 0, 0, tiled=True)  6.65 us
  transfers between devices with their start and end apart: 7, of which 7 were waited for; matrix products, arithmetic and copies ran while one was open for 0% of the time, Pallas kernels for 6%

profile of v7, /device:TPU:8, one launch (start us, length us, event | category | flops | bytes accessed | tf_op | source)
XLA Modules:
  0.0 204.8 jit_solution(7186841281600720741)
XLA Ops:
  0.6 1.7 load.1
  2.3 0.0 copy-start.4
  2.3 12.4 %all-to-all-start = ((f32[64,4,128]{2,1,0:T(4,128)}), f32[64,4,128]{2,1,0:T(4,128)S(1)}, u32[]{:S(2)}, u32[]{:S(2)}) async-start(f32[64,4,128]{2,1,0:T(4,128)} %get-tuple-element.33), calls=%async_computation | async-start | bytes 262144 | tf_op jit(solution)/shard_map/all_to_all | solution.py:284
  14.7 0.0 copy-start.3
  14.7 0.0 copy-start.6
  14.7 3.3 %setup.1 = (bf16[1024,1024]{1,0:T(8,128)(2,1)}, bf16[1024,512]{1,0:T(8,128)(2,1)S(1)}) custom-call(bf16[1024,1024]{1,0:T(8,128)(2,1)} %bitcast.15, bf16[512,1024]{1,0:T(8,128)(2,1)} %bitcast.16), custom_call_target="tpu_custom_call" | custom-call | flops 33554432 | bytes 6291456 | tf_op jit(solution)/shard_map/setup/pallas_call | solution.py:32
  18.0 7.1 %all-to-all-done.terms_ref = f32[64,4,128]{2,1,0:T(4,128)S(1)} async-done(((f32[64,4,128]{2,1,0:T(4,128)}), f32[64,4,128]{2,1,0:T(4,128)S(1)}, u32[]{:S(2)}, u32[]{:S(2)}) %all-to-all-start) | async-done | bytes 131104 | tf_op jit(solution)/shard_map/all_to_all | solution.py:284
  25.1 0.1 chain.3.old_ref
  25.3 14.5 %all_to_all.60.pieces_ref = f32[64,2,128]{2,1,0:T(2,128)S(1)} all-to-all(f32[64,2,128]{2,1,0:T(2,128)S(1)} %chain.3.old_ref), channel_id=1, replica_groups=mesh['cuts_0'=4,'cuts_1'=2,'cuts_2'=8,'circ_0'=4,'circ_1'=2] {'cuts_0','..., dimensions={0} | all-to-all | bytes 131072 | tf_op jit(solution)/shard_map/all_to_all | solution.py:284
  39.8 0.9 start.2
  40.7 9.4 %all-to-all-start.2 = ((f32[8,16,128]{2,1,0:T(8,128)}), f32[8,16,128]{2,1,0:T(8,128)S(1)}, u32[]{:S(2)}, u32[]{:S(2)}) async-start(f32[8,16,128]{2,1,0:T(8,128)} %get-tuple-element.39), calls=%async_computation.2 | async-start | bytes 131072 | tf_op jit(solution)/shard_map/all_to_all | solution.py:288
  50.1 5.4 %free.2 = (f32[128,1024]{1,0:T(8,128)S(1)}, f32[128,512]{1,0:T(8,128)S(1)}, bf16[1024,1024]{1,0:T(8,128)(2,1)}, bf16[1024,512]{1,0:T(8,128)(2,1)S(1)}) custom-call(f32[16,1024]{1,0:T(8,128)S(1)} %get-tuple-element.40.start_ref, bf16[8,16,1024]{2,1,0:T(8,128)(2,1)S(1)} %bitcast.11, f32[1,1024]{1,0:T(1,128)S(1)} %bitcast.13, ...), custom_call_target="tpu_custom_call" | custom-call | flops 3623878656 | bytes 7409664 | tf_op jit(solution)/shard_map/free/pallas_call | solution.py:32
  55.5 2.8 %all-to-all-done.2.f_ref = f32[8,16,128]{2,1,0:T(8,128)S(1)} async-done(((f32[8,16,128]{2,1,0:T(8,128)}), f32[8,16,128]{2,1,0:T(8,128)S(1)}, u32[]{:S(2)}, u32[]{:S(2)}) %all-to-all-start.2) | async-done | bytes 65568 | tf_op jit(solution)/shard_map/all_to_all | solution.py:288
  58.3 0.4 couple.4
  58.7 1.9 collective-permute-start
  60.6 1.5 collective-permute-done.got_ref
  62.1 0.1 gather.4
  62.2 15.5 %all_to_all.61.f_ref = f32[4,128,128]{2,1,0:T(8,128)S(1)} all-to-all(f32[4,128,128]{2,1,0:T(8,128)S(1)} %gather.4), channel_id=1, replica_groups=mesh['cuts_0'=4,'cuts_1'=2,'cuts_2'=8,'circ_0'=4,'circ_1'=2] {'circ_0'}, dimensions={0} | all-to-all | bytes 524288 | tf_op jit(solution)/shard_map/all_to_all | solution.py:292
  77.7 0.4 couple.5
  78.1 1.9 collective-permute-start.1
  80.0 1.5 collective-permute-done.1.got_ref
  81.5 0.1 gather.5
  81.6 13.8 %all_to_all.62.f_ref = f32[4,128,128]{2,1,0:T(8,128)S(1)} all-to-all(f32[4,128,128]{2,1,0:T(8,128)S(1)} %gather.5), channel_id=1, replica_groups=mesh['cuts_0'=4,'cuts_1'=2,'cuts_2'=8,'circ_0'=4,'circ_1'=2] {'circ_0'}, dimensions={0} | all-to-all | bytes 524288 | tf_op jit(solution)/shard_map/all_to_all | solution.py:292
  95.4 0.0 copy-done
  95.4 0.4 last.1
  95.8 14.8 %all_to_all.63.last_ref = f32[64,2,128]{2,1,0:T(2,128)S(1)} all-to-all(f32[64,2,128]{2,1,0:T(2,128)S(1)} %last.1), channel_id=1, replica_groups=mesh['cuts_0'=4,'cuts_1'=2,'cuts_2'=8,'circ_0'=4,'circ_1'=2] {'cuts_0','..., dimensions={0} | all-to-all | bytes 131072 | tf_op jit(solution)/shard_map/all_to_all | solution.py:284
  110.6 0.1 chain.4.old_ref
  110.7 14.5 %all_to_all.64.pieces_ref = f32[64,2,128]{2,1,0:T(2,128)S(1)} all-to-all(f32[64,2,128]{2,1,0:T(2,128)S(1)} %chain.4.old_ref), channel_id=1, replica_groups=mesh['cuts_0'=4,'cuts_1'=2,'cuts_2'=8,'circ_0'=4,'circ_1'=2] {'cuts_0','..., dimensions={0} | all-to-all | bytes 131072 | tf_op jit(solution)/shard_map/all_to_all | solution.py:284
  125.2 0.9 start.3
  126.1 3.5 %all-to-all-start.7 = ((f32[8,16,128]{2,1,0:T(8,128)}), f32[8,16,128]{2,1,0:T(8,128)S(1)}, u32[]{:S(2)}, u32[]{:S(2)}) async-start(f32[8,16,128]{2,1,0:T(8,128)} %get-tuple-element.50), calls=%async_computation.7 | async-start | bytes 131072 | tf_op jit(solution)/shard_map/all_to_all | solution.py:288
  129.6 1.6 copy-done.2
  131.2 2.6 %free.3 = (f32[128,1024]{1,0:T(8,128)S(1)}, f32[128,512]{1,0:T(8,128)S(1)}) custom-call(f32[16,1024]{1,0:T(8,128)S(1)} %get-tuple-element.51.start_ref, bf16[8,16,1024]{2,1,0:T(8,128)(2,1)S(1)} %bitcast.12, f32[1,1024]{1,0:T(1,128)S(1)} %bitcast.14, bf16[1024,1024]{1,0:T(8,128)(2,1)S(1)} %copy-done.2, bf16[1024,512]{1,0:T(8,128)(2,1)S(1)} %get-tuple-element.38.ct_ref), custom_call_target="tpu_custom_call" | custom-call | flops 402653184 | bytes 4263936 | tf_op jit(solution)/shard_map/free/pallas_call | solution.py:32
  133.8 3.8 %all-to-all-done.7.f_ref = f32[8,16,128]{2,1,0:T(8,128)S(1)} async-done(((f32[8,16,128]{2,1,0:T(8,128)}), f32[8,16,128]{2,1,0:T(8,128)S(1)}, u32[]{:S(2)}, u32[]{:S(2)}) %all-to-all-start.7) | async-done | bytes 65568 | tf_op jit(solution)/shard_map/all_to_all | solution.py:288
  137.6 0.4 couple.6
  138.0 1.9 collective-permute-start.2
  139.9 1.5 collective-permute-done.2.got_ref
  141.4 0.1 gather.6
  141.5 14.2 %all_to_all.65.f_ref = f32[4,128,128]{2,1,0:T(8,128)S(1)} all-to-all(f32[4,128,128]{2,1,0:T(8,128)S(1)} %gather.6), channel_id=1, replica_groups=mesh['cuts_0'=4,'cuts_1'=2,'cuts_2'=8,'circ_0'=4,'circ_1'=2] {'circ_0'}, dimensions={0} | all-to-all | bytes 524288 | tf_op jit(solution)/shard_map/all_to_all | solution.py:292
  155.8 0.4 couple.7
  156.1 1.9 collective-permute-start.3
  158.0 1.5 collective-permute-done.3.got_ref
  159.5 0.1 gather.7
  159.6 13.8 %all_to_all.66.f_ref = f32[4,128,128]{2,1,0:T(8,128)S(1)} all-to-all(f32[4,128,128]{2,1,0:T(8,128)S(1)} %gather.7), channel_id=1, replica_groups=mesh['cuts_0'=4,'cuts_1'=2,'cuts_2'=8,'circ_0'=4,'circ_1'=2] {'circ_0'}, dimensions={0} | all-to-all | bytes 524288 | tf_op jit(solution)/shard_map/all_to_all | solution.py:292
  173.5 0.5 wave.1
  173.9 14.7 %all_to_all.67.last_ref = f32[64,2,128]{2,1,0:T(2,128)S(1)} all-to-all(f32[64,2,128]{2,1,0:T(2,128)S(1)} %get-tuple-element.58), channel_id=1, replica_groups=mesh['cuts_0'=4,'cuts_1'=2,'cuts_2'=8,'circ_0'=4,'circ_1'=2] {'cuts_0','..., dimensions={0} | all-to-all | bytes 131072 | tf_op jit(solution)/shard_map/all_to_all | solution.py:284
  188.7 0.1 chain.5
  188.8 14.5 %all_to_all.68.pieces_ref = f32[64,2,128]{2,1,0:T(2,128)S(1)} all-to-all(f32[64,2,128]{2,1,0:T(2,128)S(1)} %chain.5), channel_id=1, replica_groups=mesh['cuts_0'=4,'cuts_1'=2,'cuts_2'=8,'circ_0'=4,'circ_1'=2] {'cuts_0','..., dimensions={0} | all-to-all | bytes 131072 | tf_op jit(solution)/shard_map/all_to_all | solution.py:284
  203.3 1.3 finish.1
  (9 shorter events, 0.0 us)
Async XLA Ops:
  2.3 22.8 %copy-start.5 = (f32[2,128]{1,0:T(2,128)S(1)}, f32[2,128]{1,0:T(2,128)}, u32[]{:S(2)}) copy-start(f32[2,128]{1,0:T(2,128)} %get-tuple-element.37.initial_ref) | copy-start | bytes 3076
  2.3 37.5 %copy-start.4 = (s32[12,128]{1,0:T(8,128)S(1)}, s32[12,128]{1,0:T(8,128)}, u32[]{:S(2)}) copy-start(s32[12,128]{1,0:T(8,128)} %get-tuple-element.32.target_ref) | copy-start | bytes 18436
  2.3 22.8 %all-to-all-start = ((f32[64,4,128]{2,1,0:T(4,128)}), f32[64,4,128]{2,1,0:T(4,128)S(1)}, u32[]{:S(2)}, u32[]{:S(2)}) async-start(f32[64,4,128]{2,1,0:T(4,128)} %get-tuple-element.33), calls=%async_computation | async-start | bytes 262144 | tf_op jit(solution)/shard_map/all_to_all | solution.py:284
  14.7 35.4 %copy-start.3 = (bf16[1,8,1,16,1024]{4,3,2,1,0:T(8,128)(2,1)S(1)}, bf16[1,8,1,16,1024]{4,3,2,1,0:T(8,128)(2,1)}, u32[]{:S(2)}) copy-start(bf16[1,8,1,16,1024]{4,3,2,1,0:T(8,128)(2,1)} %param.7) | copy-start | bytes 786436
  14.7 35.4 %copy-start.6 = (f32[1,1,1024]{2,1,0:T(1,128)S(1)}, f32[1,1,1024]{2,1,0:T(1,128)}, u32[]{:S(2)}) copy-start(f32[1,1,1024]{2,1,0:T(1,128)} %param.9) | copy-start | bytes 12292
  40.7 17.7 %all-to-all-start.2 = ((f32[8,16,128]{2,1,0:T(8,128)}), f32[8,16,128]{2,1,0:T(8,128)S(1)}, u32[]{:S(2)}, u32[]{:S(2)}) async-start(f32[8,16,128]{2,1,0:T(8,128)} %get-tuple-element.39), calls=%async_computation.2 | async-start | bytes 131072 | tf_op jit(solution)/shard_map/all_to_all | solution.py:288
  58.7 3.4 %collective-permute-start = (f32[4,128,128]{2,1,0:T(8,128)S(1)}, f32[4,128,128]{2,1,0:T(8,128)S(1)}, u32[]{:S(2)}, u32[]{:S(2)}) collective-permute-start(f32[4,128,128]{2,1,0:T(8,128)S(1)} %get-tuple-element.45), channel_id=1, source_target_pairs={{0,1},{1,0},{2,3},{3,2},{4,5},{5,4},{6,7},{7,6},{8,9},{9,8},{10,11... | collective-permute-start | bytes 786440 | tf_op jit(solution)/shard_map/ppermute | solution.py:296
  62.1 33.3 %copy-start = (bf16[1024,1024]{1,0:T(8,128)(2,1)S(1)}, bf16[1024,1024]{1,0:T(8,128)(2,1)}, u32[]{:S(2)}) copy-start(bf16[1024,1024]{1,0:T(8,128)(2,1)} %get-tuple-element.49.h_ref) | copy-start | bytes 6291460
  78.1 3.4 %collective-permute-start.1 = (f32[4,128,128]{2,1,0:T(8,128)S(1)}, f32[4,128,128]{2,1,0:T(8,128)S(1)}, u32[]{:S(2)}, u32[]{:S(2)}) collective-permute-start(f32[4,128,128]{2,1,0:T(8,128)S(1)} %get-tuple-element.47), channel_id=1, source_target_pairs={{0,1},{1,0},{2,3},{3,2},{4,5},{5,4},{6,7},{7,6},{8,9},{9,8},{10,11... | collective-permute-start | bytes 786440 | tf_op jit(solution)/shard_map/ppermute | solution.py:296
  126.1 11.6 %all-to-all-start.7 = ((f32[8,16,128]{2,1,0:T(8,128)}), f32[8,16,128]{2,1,0:T(8,128)S(1)}, u32[]{:S(2)}, u32[]{:S(2)}) async-start(f32[8,16,128]{2,1,0:T(8,128)} %get-tuple-element.50), calls=%async_computation.7 | async-start | bytes 131072 | tf_op jit(solution)/shard_map/all_to_all | solution.py:288
  129.6 1.6 copy-start.2
  138.0 3.4 %collective-permute-start.2 = (f32[4,128,128]{2,1,0:T(8,128)S(1)}, f32[4,128,128]{2,1,0:T(8,128)S(1)}, u32[]{:S(2)}, u32[]{:S(2)}) collective-permute-start(f32[4,128,128]{2,1,0:T(8,128)S(1)} %get-tuple-element.54), channel_id=1, source_target_pairs={{0,1},{1,0},{2,3},{3,2},{4,5},{5,4},{6,7},{7,6},{8,9},{9,8},{10,11... | collective-permute-start | bytes 786440 | tf_op jit(solution)/shard_map/ppermute | solution.py:296
  141.4 32.0 %copy-start.1 = (bf16[1024,1024]{1,0:T(8,128)(2,1)S(1)}, bf16[1024,1024]{1,0:T(8,128)(2,1)}, u32[]{:S(2)}) copy-start(bf16[1024,1024]{1,0:T(8,128)(2,1)} %get-tuple-element.49.h_ref) | copy-start | bytes 6291460
  156.1 3.4 %collective-permute-start.3 = (f32[4,128,128]{2,1,0:T(8,128)S(1)}, f32[4,128,128]{2,1,0:T(8,128)S(1)}, u32[]{:S(2)}, u32[]{:S(2)}) collective-permute-start(f32[4,128,128]{2,1,0:T(8,128)S(1)} %get-tuple-element.56), channel_id=1, source_target_pairs={{0,1},{1,0},{2,3},{3,2},{4,5},{5,4},{6,7},{7,6},{8,9},{9,8},{10,11... | collective-permute-start | bytes 786440 | tf_op jit(solution)/shard_map/ppermute | solution.py:296

commit v8 on v7

--- a/solution.py
+++ b/solution.py
@@ -64,13 +64,14 @@
     decay_ref,
     target_hbm,
     initial_hbm,
-    out_ref,
+    out_hbm,
     targets_ref,
     initial_ref,
     held_ref,
     rate_ref,
     target_ref,
     tile_ref,
+    out_ref,
     sems,
 ):
     block, pair = jnp.divmod(lax.axis_index(CUTS), 8)
@@ -86,19 +87,12 @@
             ((decay_ref, rate_ref), (target_hbm, target_ref), (tile, tile_ref))
         )
     ]
-    for copy in steps + small:
+    for copy in small + steps:
         copy.start()
-    total = None
-    for t, step in enumerate(steps):
-        step.wait()
-        now = held_ref[t].astype(F32)
-        total = now if total is None else total + now
-    pack(total * (1.0 / STEPS), out_ref)
     for copy in small:
         copy.wait()
     for b in range(64):
-        block = b // 8
-        row = rate_ref[:, block * LANES : (block + 1) * LANES]
+        row = rate_ref[:, b // 8 * LANES : (b // 8 + 1) * LANES]
         out_ref[b, 2:4, :] = jnp.concatenate([row, row], axis=0)
     core = lax.axis_index(CIRC[1])
     for k in range(KC):
@@ -107,6 +101,24 @@
         targets_ref[KC + k : KC + k + 1, :] = target - core
         targets_ref[2 * KC + k : 2 * KC + k + 1, :] = target - (1 - core)
     initial_ref[...] = tile_ref[pl.ds(pair % 4 * 2, 2), :]
+    for copy in steps:
+        copy.wait()
+    sent = []
+    for k in range(8):
+        columns = slice(k * LANES, (k + 1) * LANES)
+        total = held_ref[0, :, columns].astype(F32)
+        for t in range(1, STEPS):
+            total = total + held_ref[t, :, columns].astype(F32)
+        pack(total * (1.0 / STEPS), out_ref, k)
+        pieces = slice(8 * k, 8 * k + 8)
+        sent.append(
+            pltpu.make_async_copy(
+                out_ref.at[pieces], out_hbm.at[pieces], sems.at[STEPS + 3 + k]
+            )
+        )
+        sent[-1].start()
+    for copy in sent:
+        copy.wait()
 
 
 def setup_body(b_hbm, c_hbm, bt_hbm, ct_ref, b_ref, c_ref, bt_ref, sems):
@@ -323,10 +335,12 @@
             pltpu.VMEM((1, nodes), F32),
             pltpu.VMEM((1, KC), jnp.int32),
             pltpu.VMEM((8, LANES), F32),
-            pltpu.SemaphoreType.DMA((STEPS + 3,)),
+            pltpu.VMEM((64, 4, LANES), F32),
+            pltpu.SemaphoreType.DMA((STEPS + 11,)),
         ],
         places=[HBM] * 4,
         grant=60,
+        out_places=[HBM, VMEM, VMEM],
     )
     terms = over_cuts(loads)
     bt, ct = call(

time: 206 us -> 206 us (level)
  no operation moved by 1% of the time
where the time goes in v8:
time: 206 us
  blocking collectives  130 us (63%)
  starting transfers between devices  33 us (16%)
  Pallas kernels  19.8 us (10%)
  waiting for transfers between devices  19.7 us (10%)
    all_to_all x5, blocking collectives, over_cuts(): return lax.all_to_all(pieces, CUTS, 0, 0, tiled=True)  73 us
    all_to_all x4, blocking collectives, over_chips(): return lax.all_to_all(blocks, CIRC[0], 0, 0, tiled=True)  57.3 us
    pallas_call x20, Pallas kernels, call(): pl.pallas_call(body, out_shape=outs, in_specs=places or [VMEM] * len(args...  19.8 us
    all_to_all x2, starting transfers between devices, over_circ(): return lax.all_to_all(blocks, CIRC, 0, 0, tiled=True)  12.9 us
    all_to_all x1, starting transfers between devices, over_cuts(): return lax.all_to_all(pieces, CUTS, 0, 0, tiled=True)  12.4 us
    ppermute x4, starting transfers between devices, other_core(): return lax.ppermute(blocks, CIRC[1], [(0, 1), (1, 0)])  7.68 us
    all_to_all x1, waiting for transfers between devices, over_cuts(): return lax.all_to_all(pieces, CUTS, 0, 0, tiled=True)  7.08 us
    all_to_all x2, waiting for transfers between devices, over_circ(): return lax.all_to_all(blocks, CIRC, 0, 0, tiled=True)  6.65 us
  transfers between devices with their start and end apart: 7, of which 7 were waited for; matrix products, arithmetic and copies ran while one was open for 0% of the time, Pallas kernels for 6%

profile of v8, /device:TPU:8, one launch (start us, length us, event | category | flops | bytes accessed | tf_op | source)
XLA Modules:
  0.0 205.5 jit_solution(1082860209570428188)
XLA Ops:
  0.6 2.3 %load.1 = (f32[64,4,128]{2,1,0:T(4,128)}, s32[12,128]{1,0:T(8,128)}, f32[2,128]{1,0:T(2,128)}) custom-call(bf16[8,16,1024]{2,1,0:T(8,128)(2,1)} %bitcast.10, f32[1,1024]{1,0:T(1,128)} %bitcast.18, s32[1,4]{1,0:T(1,128)} %target_hbm.1, f32[16,1024]{1,0:T(8,128)} %bitcast.17), custom_call_target="tpu_custom_call" | custom-call | bytes 470032 | tf_op jit(solution)/shard_map/load/pallas_call | solution.py:32
  3.0 0.0 copy-start.4
  3.0 12.4 %all-to-all-start = ((f32[64,4,128]{2,1,0:T(4,128)}), f32[64,4,128]{2,1,0:T(4,128)S(1)}, u32[]{:S(2)}, u32[]{:S(2)}) async-start(f32[64,4,128]{2,1,0:T(4,128)} %get-tuple-element.33), calls=%async_computation | async-start | bytes 262144 | tf_op jit(solution)/shard_map/all_to_all | solution.py:296
  15.4 0.0 copy-start.3
  15.4 0.0 copy-start.6
  15.4 3.3 %setup.1 = (bf16[1024,1024]{1,0:T(8,128)(2,1)}, bf16[1024,512]{1,0:T(8,128)(2,1)S(1)}) custom-call(bf16[1024,1024]{1,0:T(8,128)(2,1)} %bitcast.15, bf16[512,1024]{1,0:T(8,128)(2,1)} %bitcast.16), custom_call_target="tpu_custom_call" | custom-call | flops 33554432 | bytes 6291456 | tf_op jit(solution)/shard_map/setup/pallas_call | solution.py:32
  18.7 7.1 %all-to-all-done.terms_ref = f32[64,4,128]{2,1,0:T(4,128)S(1)} async-done(((f32[64,4,128]{2,1,0:T(4,128)}), f32[64,4,128]{2,1,0:T(4,128)S(1)}, u32[]{:S(2)}, u32[]{:S(2)}) %all-to-all-start) | async-done | bytes 131104 | tf_op jit(solution)/shard_map/all_to_all | solution.py:296
  25.8 0.0 copy-done.5
  25.8 0.1 chain.3.old_ref
  25.9 14.5 %all_to_all.60.pieces_ref = f32[64,2,128]{2,1,0:T(2,128)S(1)} all-to-all(f32[64,2,128]{2,1,0:T(2,128)S(1)} %chain.3.old_ref), channel_id=1, replica_groups=mesh['cuts_0'=4,'cuts_1'=2,'cuts_2'=8,'circ_0'=4,'circ_1'=2] {'cuts_0','..., dimensions={0} | all-to-all | bytes 131072 | tf_op jit(solution)/shard_map/all_to_all | solution.py:296
  40.4 0.9 start.2
  41.4 9.4 %all-to-all-start.2 = ((f32[8,16,128]{2,1,0:T(8,128)}), f32[8,16,128]{2,1,0:T(8,128)S(1)}, u32[]{:S(2)}, u32[]{:S(2)}) async-start(f32[8,16,128]{2,1,0:T(8,128)} %get-tuple-element.39), calls=%async_computation.2 | async-start | bytes 131072 | tf_op jit(solution)/shard_map/all_to_all | solution.py:300
  50.8 5.4 %free.2 = (f32[128,1024]{1,0:T(8,128)S(1)}, f32[128,512]{1,0:T(8,128)S(1)}, bf16[1024,1024]{1,0:T(8,128)(2,1)}, bf16[1024,512]{1,0:T(8,128)(2,1)S(1)}) custom-call(f32[16,1024]{1,0:T(8,128)S(1)} %get-tuple-element.40.start_ref, bf16[8,16,1024]{2,1,0:T(8,128)(2,1)S(1)} %bitcast.11, f32[1,1024]{1,0:T(1,128)S(1)} %bitcast.13, ...), custom_call_target="tpu_custom_call" | custom-call | flops 3623878656 | bytes 7409664 | tf_op jit(solution)/shard_map/free/pallas_call | solution.py:32
  56.2 2.8 %all-to-all-done.2.f_ref = f32[8,16,128]{2,1,0:T(8,128)S(1)} async-done(((f32[8,16,128]{2,1,0:T(8,128)}), f32[8,16,128]{2,1,0:T(8,128)S(1)}, u32[]{:S(2)}, u32[]{:S(2)}) %all-to-all-start.2) | async-done | bytes 65568 | tf_op jit(solution)/shard_map/all_to_all | solution.py:300
  59.0 0.4 couple.4
  59.4 1.9 collective-permute-start
  61.3 1.5 collective-permute-done.got_ref
  62.8 0.1 gather.4
  62.9 15.5 %all_to_all.61.f_ref = f32[4,128,128]{2,1,0:T(8,128)S(1)} all-to-all(f32[4,128,128]{2,1,0:T(8,128)S(1)} %gather.4), channel_id=1, replica_groups=mesh['cuts_0'=4,'cuts_1'=2,'cuts_2'=8,'circ_0'=4,'circ_1'=2] {'circ_0'}, dimensions={0} | all-to-all | bytes 524288 | tf_op jit(solution)/shard_map/all_to_all | solution.py:304
  78.4 0.4 couple.5
  78.8 1.9 collective-permute-start.1
  80.7 1.5 collective-permute-done.1.got_ref
  82.2 0.1 gather.5
  82.3 13.8 %all_to_all.62.f_ref = f32[4,128,128]{2,1,0:T(8,128)S(1)} all-to-all(f32[4,128,128]{2,1,0:T(8,128)S(1)} %gather.5), channel_id=1, replica_groups=mesh['cuts_0'=4,'cuts_1'=2,'cuts_2'=8,'circ_0'=4,'circ_1'=2] {'circ_0'}, dimensions={0} | all-to-all | bytes 524288 | tf_op jit(solution)/shard_map/all_to_all | solution.py:304
  96.1 0.4 last.1
  96.5 14.8 %all_to_all.63.last_ref = f32[64,2,128]{2,1,0:T(2,128)S(1)} all-to-all(f32[64,2,128]{2,1,0:T(2,128)S(1)} %last.1), channel_id=1, replica_groups=mesh['cuts_0'=4,'cuts_1'=2,'cuts_2'=8,'circ_0'=4,'circ_1'=2] {'cuts_0','..., dimensions={0} | all-to-all | bytes 131072 | tf_op jit(solution)/shard_map/all_to_all | solution.py:296
  111.3 0.1 chain.4.old_ref
  111.4 14.5 %all_to_all.64.pieces_ref = f32[64,2,128]{2,1,0:T(2,128)S(1)} all-to-all(f32[64,2,128]{2,1,0:T(2,128)S(1)} %chain.4.old_ref), channel_id=1, replica_groups=mesh['cuts_0'=4,'cuts_1'=2,'cuts_2'=8,'circ_0'=4,'circ_1'=2] {'cuts_0','..., dimensions={0} | all-to-all | bytes 131072 | tf_op jit(solution)/shard_map/all_to_all | solution.py:296
  125.9 0.9 start.3
  126.8 3.5 %all-to-all-start.7 = ((f32[8,16,128]{2,1,0:T(8,128)}), f32[8,16,128]{2,1,0:T(8,128)S(1)}, u32[]{:S(2)}, u32[]{:S(2)}) async-start(f32[8,16,128]{2,1,0:T(8,128)} %get-tuple-element.50), calls=%async_computation.7 | async-start | bytes 131072 | tf_op jit(solution)/shard_map/all_to_all | solution.py:300
  130.3 1.6 copy-done.2
  131.9 2.6 %free.3 = (f32[128,1024]{1,0:T(8,128)S(1)}, f32[128,512]{1,0:T(8,128)S(1)}) custom-call(f32[16,1024]{1,0:T(8,128)S(1)} %get-tuple-element.51.start_ref, bf16[8,16,1024]{2,1,0:T(8,128)(2,1)S(1)} %bitcast.12, f32[1,1024]{1,0:T(1,128)S(1)} %bitcast.14, bf16[1024,1024]{1,0:T(8,128)(2,1)S(1)} %copy-done.2, bf16[1024,512]{1,0:T(8,128)(2,1)S(1)} %get-tuple-element.38.ct_ref), custom_call_target="tpu_custom_call" | custom-call | flops 402653184 | bytes 4263936 | tf_op jit(solution)/shard_map/free/pallas_call | solution.py:32
  134.5 3.8 %all-to-all-done.7.f_ref = f32[8,16,128]{2,1,0:T(8,128)S(1)} async-done(((f32[8,16,128]{2,1,0:T(8,128)}), f32[8,16,128]{2,1,0:T(8,128)S(1)}, u32[]{:S(2)}, u32[]{:S(2)}) %all-to-all-start.7) | async-done | bytes 65568 | tf_op jit(solution)/shard_map/all_to_all | solution.py:300
  138.4 0.4 couple.6
  138.7 1.9 collective-permute-start.2
  140.6 1.5 collective-permute-done.2.got_ref
  142.1 0.1 gather.6
  142.2 14.2 %all_to_all.65.f_ref = f32[4,128,128]{2,1,0:T(8,128)S(1)} all-to-all(f32[4,128,128]{2,1,0:T(8,128)S(1)} %gather.6), channel_id=1, replica_groups=mesh['cuts_0'=4,'cuts_1'=2,'cuts_2'=8,'circ_0'=4,'circ_1'=2] {'circ_0'}, dimensions={0} | all-to-all | bytes 524288 | tf_op jit(solution)/shard_map/all_to_all | solution.py:304
  156.5 0.4 couple.7
  156.8 1.9 collective-permute-start.3
  158.8 1.5 collective-permute-done.3.got_ref
  160.3 0.1 gather.7
  160.4 13.8 %all_to_all.66.f_ref = f32[4,128,128]{2,1,0:T(8,128)S(1)} all-to-all(f32[4,128,128]{2,1,0:T(8,128)S(1)} %gather.7), channel_id=1, replica_groups=mesh['cuts_0'=4,'cuts_1'=2,'cuts_2'=8,'circ_0'=4,'circ_1'=2] {'circ_0'}, dimensions={0} | all-to-all | bytes 524288 | tf_op jit(solution)/shard_map/all_to_all | solution.py:304
  174.2 0.5 wave.1
  174.6 14.8 %all_to_all.67.last_ref = f32[64,2,128]{2,1,0:T(2,128)S(1)} all-to-all(f32[64,2,128]{2,1,0:T(2,128)S(1)} %get-tuple-element.58), channel_id=1, replica_groups=mesh['cuts_0'=4,'cuts_1'=2,'cuts_2'=8,'circ_0'=4,'circ_1'=2] {'cuts_0','..., dimensions={0} | all-to-all | bytes 131072 | tf_op jit(solution)/shard_map/all_to_all | solution.py:296
  189.4 0.1 chain.5
  189.6 14.5 %all_to_all.68.pieces_ref = f32[64,2,128]{2,1,0:T(2,128)S(1)} all-to-all(f32[64,2,128]{2,1,0:T(2,128)S(1)} %chain.5), channel_id=1, replica_groups=mesh['cuts_0'=4,'cuts_1'=2,'cuts_2'=8,'circ_0'=4,'circ_1'=2] {'cuts_0','..., dimensions={0} | all-to-all | bytes 131072 | tf_op jit(solution)/shard_map/all_to_all | solution.py:296
  204.0 1.3 finish.1
  (9 shorter events, 0.0 us)
Async XLA Ops:
  3.0 22.8 %copy-start.5 = (f32[2,128]{1,0:T(2,128)S(1)}, f32[2,128]{1,0:T(2,128)}, u32[]{:S(2)}) copy-start(f32[2,128]{1,0:T(2,128)} %get-tuple-element.37.initial_ref) | copy-start | bytes 3076
  3.0 37.5 %copy-start.4 = (s32[12,128]{1,0:T(8,128)S(1)}, s32[12,128]{1,0:T(8,128)}, u32[]{:S(2)}) copy-start(s32[12,128]{1,0:T(8,128)} %get-tuple-element.32.target_ref) | copy-start | bytes 18436
  3.0 22.8 %all-to-all-start = ((f32[64,4,128]{2,1,0:T(4,128)}), f32[64,4,128]{2,1,0:T(4,128)S(1)}, u32[]{:S(2)}, u32[]{:S(2)}) async-start(f32[64,4,128]{2,1,0:T(4,128)} %get-tuple-element.33), calls=%async_computation | async-start | bytes 262144 | tf_op jit(solution)/shard_map/all_to_all | solution.py:296
  15.4 35.4 %copy-start.3 = (bf16[1,8,1,16,1024]{4,3,2,1,0:T(8,128)(2,1)S(1)}, bf16[1,8,1,16,1024]{4,3,2,1,0:T(8,128)(2,1)}, u32[]{:S(2)}) copy-start(bf16[1,8,1,16,1024]{4,3,2,1,0:T(8,128)(2,1)} %param.7) | copy-start | bytes 786436
  15.4 35.4 %copy-start.6 = (f32[1,1,1024]{2,1,0:T(1,128)S(1)}, f32[1,1,1024]{2,1,0:T(1,128)}, u32[]{:S(2)}) copy-start(f32[1,1,1024]{2,1,0:T(1,128)} %param.9) | copy-start | bytes 12292
  41.4 17.7 %all-to-all-start.2 = ((f32[8,16,128]{2,1,0:T(8,128)}), f32[8,16,128]{2,1,0:T(8,128)S(1)}, u32[]{:S(2)}, u32[]{:S(2)}) async-start(f32[8,16,128]{2,1,0:T(8,128)} %get-tuple-element.39), calls=%async_computation.2 | async-start | bytes 131072 | tf_op jit(solution)/shard_map/all_to_all | solution.py:300
  59.4 3.4 %collective-permute-start = (f32[4,128,128]{2,1,0:T(8,128)S(1)}, f32[4,128,128]{2,1,0:T(8,128)S(1)}, u32[]{:S(2)}, u32[]{:S(2)}) collective-permute-start(f32[4,128,128]{2,1,0:T(8,128)S(1)} %get-tuple-element.45), channel_id=1, source_target_pairs={{0,1},{1,0},{2,3},{3,2},{4,5},{5,4},{6,7},{7,6},{8,9},{9,8},{10,11... | collective-permute-start | bytes 786440 | tf_op jit(solution)/shard_map/ppermute | solution.py:308
  62.8 33.3 %copy-start = (bf16[1024,1024]{1,0:T(8,128)(2,1)S(1)}, bf16[1024,1024]{1,0:T(8,128)(2,1)}, u32[]{:S(2)}) copy-start(bf16[1024,1024]{1,0:T(8,128)(2,1)} %get-tuple-element.49.h_ref) | copy-start | bytes 6291460
  78.8 3.4 %collective-permute-start.1 = (f32[4,128,128]{2,1,0:T(8,128)S(1)}, f32[4,128,128]{2,1,0:T(8,128)S(1)}, u32[]{:S(2)}, u32[]{:S(2)}) collective-permute-start(f32[4,128,128]{2,1,0:T(8,128)S(1)} %get-tuple-element.47), channel_id=1, source_target_pairs={{0,1},{1,0},{2,3},{3,2},{4,5},{5,4},{6,7},{7,6},{8,9},{9,8},{10,11... | collective-permute-start | bytes 786440 | tf_op jit(solution)/shard_map/ppermute | solution.py:308
  126.8 11.6 %all-to-all-start.7 = ((f32[8,16,128]{2,1,0:T(8,128)}), f32[8,16,128]{2,1,0:T(8,128)S(1)}, u32[]{:S(2)}, u32[]{:S(2)}) async-start(f32[8,16,128]{2,1,0:T(8,128)} %get-tuple-element.50), calls=%async_computation.7 | async-start | bytes 131072 | tf_op jit(solution)/shard_map/all_to_all | solution.py:300
  130.3 1.6 copy-start.2
  138.7 3.4 %collective-permute-start.2 = (f32[4,128,128]{2,1,0:T(8,128)S(1)}, f32[4,128,128]{2,1,0:T(8,128)S(1)}, u32[]{:S(2)}, u32[]{:S(2)}) collective-permute-start(f32[4,128,128]{2,1,0:T(8,128)S(1)} %get-tuple-element.54), channel_id=1, source_target_pairs={{0,1},{1,0},{2,3},{3,2},{4,5},{5,4},{6,7},{7,6},{8,9},{9,8},{10,11... | collective-permute-start | bytes 786440 | tf_op jit(solution)/shard_map/ppermute | solution.py:308
  142.1 32.0 %copy-start.1 = (bf16[1024,1024]{1,0:T(8,128)(2,1)S(1)}, bf16[1024,1024]{1,0:T(8,128)(2,1)}, u32[]{:S(2)}) copy-start(bf16[1024,1024]{1,0:T(8,128)(2,1)} %get-tuple-element.49.h_ref) | copy-start | bytes 6291460
  156.8 3.4 %collective-permute-start.3 = (f32[4,128,128]{2,1,0:T(8,128)S(1)}, f32[4,128,128]{2,1,0:T(8,128)S(1)}, u32[]{:S(2)}, u32[]{:S(2)}) collective-permute-start(f32[4,128,128]{2,1,0:T(8,128)S(1)} %get-tuple-element.56), channel_id=1, source_target_pairs={{0,1},{1,0},{2,3},{3,2},{4,5},{5,4},{6,7},{7,6},{8,9},{9,8},{10,11... | collective-permute-start | bytes 786440 | tf_op jit(solution)/shard_map/ppermute | solution.py:308
